TPU v7x, 256 devices: a whole 4x4x8 slice. The times are simulated.
256 devices in a mesh: tm: 8 (over y, x_lo), space: 32 (over z, x_hi, core).
Axes of the slice: x: 4 (x_hi: 2, x_lo: 2; x = x_hi * 2 + x_lo), y: 4, z: 8, core: 2. Of those that a mesh axis runs over, the one named last changes fastest.
Arguments:
- video: bfloat16 [16, 256, 128, 128], P('tm', 'space'), may hold values from -6 to 6
- norm_gain: float32 [128], replicated, may hold values from 0.25 to 1.75
- conv_weight: bfloat16 [3, 3, 3, 128, 128], replicated, may hold values from -0.109375 to 0.109375
- conv_bias: float32 [128], replicated, may hold values from -1.5 to 1.5
- down_weight: bfloat16 [3, 3, 3, 128, 256], replicated, may hold values from -0.109375 to 0.109375
- down_bias: float32 [256], replicated, may hold values from -1.5 to 1.5
- attention_gain: float32 [256], replicated, may hold values from 0.25 to 1.75
- query_weight: bfloat16 [256, 256], replicated, may hold values from -4 to 4
- key_weight: bfloat16 [256, 256], replicated, may hold values from -0.375 to 0.375
- value_weight: bfloat16 [256, 256], replicated, may hold values from -0.375 to 0.375
- output_weight: bfloat16 [256, 256], replicated, may hold values from -0.375 to 0.375
Outputs:
- encoded: float32 [16, 128, 64, 256], P('tm', 'space')
All inputs are finite; a program needn't handle non-finite values.
Results may differ from a plain program's by a relative error of at most 0.02.
The roundings to bfloat16 on the way count: a program that leaves them out, or rounds other values in their place, can miss the bound.
Values may be sent and summed in bfloat16 or wider, within the bound.
No kernel may reach another device: no remote copies, remote signals or barrier semaphores. Data moves between devices by JAX's collectives and lax.ppermute only.
A program may use at most 128 MiB of HBM per device.

v0:
```python
import jax
import jax.numpy as jnp
from jax import lax
from jax.sharding import PartitionSpec as P

epsilon = 1e-05


def shifted(block, axis, distance):
    devices = range(lax.axis_size(axis))
    route = [(i - distance, i) for i in devices if i - distance in devices]
    return lax.ppermute(block, axis, route)


def extended_2(array, sides, width):
    for axis, dim in sides:
        size, length = (lax.axis_size(axis), array.shape[dim])
        up = [(i, (i + 1) % size) for i in range(size - 1)]
        down = [(j, i) for i, j in up]
        last = lax.slice_in_dim(array, length - width, length, axis=dim)
        first = lax.slice_in_dim(array, 0, width, axis=dim)
        before = lax.ppermute(last, axis, up)
        after = lax.ppermute(first, axis, down)
        array = jnp.concatenate([before, array, after], axis=dim)
    return array


def layer_norm(inputs, gain_vec):
    values_f = inputs.astype(jnp.float32)
    average = jnp.mean(values_f, axis=-1, keepdims=True)
    spread = jnp.mean((values_f - average) ** 2, axis=-1, keepdims=True)
    return (values_f - average) * lax.rsqrt(spread + epsilon) * gain_vec


def convolve(inputs, kernel, strides):
    result = lax.conv_general_dilated(
        inputs[None],
        kernel,
        strides,
        "VALID",
        dimension_numbers=("NDHWC", "DHWIO", "NDHWC"),
        preferred_element_type=jnp.float32,
    )
    return result[0]


def project(flattened, matrix):
    return jnp.einsum("fqc,cd->fqd", flattened, matrix, preferred_element_type=jnp.float32).astype(
        jnp.bfloat16
    )


def body(
    video,
    norm_gain,
    conv_weight,
    conv_bias,
    down_weight,
    down_bias,
    attention_gain,
    query_weight,
    key_weight,
    value_weight,
    output_weight,
):
    activated = jax.nn.silu(layer_norm(video, norm_gain)).astype(jnp.bfloat16)
    earlier = shifted(activated, "tm", 1)
    extended = jnp.concatenate([earlier, activated], axis=0)
    padded = extended_2(extended, (("space", 1),), 1)
    padded = jnp.pad(padded, ((0, 0), (0, 0), (1, 1), (0, 0)))
    summed = (
        video.astype(jnp.float32) + convolve(padded, conv_weight, (1, 1, 1)) + conv_bias
    ).astype(jnp.bfloat16)
    before = shifted(summed[-2:], "tm", 1)
    widened = jnp.concatenate([before, summed], axis=0)
    lower_rim = shifted(widened[:, :1], "space", -1)
    widened = jnp.concatenate([widened, lower_rim], axis=1)
    widened = jnp.pad(widened, ((0, 0), (0, 0), (0, 1), (0, 0)))
    reduced = convolve(widened, down_weight, (1, 2, 2)) + down_bias
    normed = layer_norm(reduced, attention_gain).astype(jnp.bfloat16)
    frame_count, row_count, col_count, channels = reduced.shape
    flattened = normed.reshape(frame_count, row_count * col_count, channels)
    queries = project(flattened, query_weight)
    score_scale = channels ** (-0.5)
    query_count = row_count * col_count
    key_grid = project(flattened, key_weight).reshape(reduced.shape)
    value_grid = project(flattened, value_weight).reshape(reduced.shape)
    key_block = lax.all_gather(key_grid, "space", axis=1, tiled=True).reshape(
        frame_count, -1, channels
    )
    value_block = lax.all_gather(value_grid, "space", axis=1, tiled=True).reshape(
        frame_count, -1, channels
    )
    running_max = jnp.full((frame_count, query_count), -jnp.inf, jnp.float32)
    running_sum = jnp.zeros((frame_count, query_count), jnp.float32)
    weighted = jnp.zeros((frame_count, query_count, channels), jnp.float32)
    scores = (
        jnp.einsum("fqc,fkc->fqk", queries, key_block, preferred_element_type=jnp.float32)
        * score_scale
    )
    new_max = jnp.maximum(running_max, jnp.max(scores, axis=-1))
    rescale = jnp.exp(running_max - new_max)
    probs = jnp.exp(scores - new_max[..., None]).astype(jnp.bfloat16)
    new_sum = running_sum * rescale + jnp.sum(probs.astype(jnp.float32), axis=-1)
    new_weighted = weighted * rescale[..., None] + jnp.einsum(
        "fqk,fkc->fqc", probs, value_block, preferred_element_type=jnp.float32
    )
    attended = (new_weighted / new_sum[..., None]).astype(jnp.bfloat16)
    mixed = jnp.einsum("fqc,cd->fqd", attended, output_weight, preferred_element_type=jnp.float32)
    encoded = reduced + mixed.reshape(reduced.shape)
    return encoded.astype(jnp.float32)


def solution(mesh):
    in_specs = (P("tm", "space", None, None), P(), P(), P(), P(), P(), P(), P(), P(), P(), P())
    out_specs = P("tm", "space", None, None)
    return jax.shard_map(body, mesh=mesh, in_specs=in_specs, out_specs=out_specs, check_vma=False)
```

profile of v0, /device:TPU:1, one launch (start us, length us, event | category | flops | bytes accessed | tf_op | source)
XLA Modules:
  0.0 306.9 jit_solution(8088070292944498132)
XLA Ops:
  6.5 1.6 convert_reduce_fusion.1
  8.1 1.7 fusion.38
  9.9 1.7 fusion.45
  11.6 4.0 %collective-permute-start = (bf16[2,8,128,128]{3,1,2,0:T(8,128)(2,1)S(1)}, bf16[2,8,128,128]{3,1,2,0:T(8,128)(2,1)S(1)}, u32[]{:S(2)}, u32[]{:S(2)}) collective-permute-start(bf16[2,8,128,128]{3,1,2,0:T(8,128)(2,1)S(1)} %fusion.45), channel_id=1, source_target_pairs={{0,32},{32,64},{64,96},{96,128},{128,160},{160,192},{192,224},{1,3... | collective-permute-start | bytes 1572872 | tf_op jit(solution)/shard_map/ppermute | solution.py:12
  15.6 10.5 %collective-permute-done = bf16[2,8,128,128]{3,1,2,0:T(8,128)(2,1)S(1)} collective-permute-done((bf16[2,8,128,128]{3,1,2,0:T(8,128)(2,1)S(1)}, bf16[2,8,128,128]{3,1,2,0:T(8,128)(2,1)S(1)}, u32[]{:S(2)}, u32[]{:S(2)}) %collective-permute-start) | collective-permute-done | bytes 524320 | tf_op jit(solution)/shard_map/ppermute | solution.py:12
  26.5 5.8 %collective-permute-start.1 = (bf16[4,1,128,128]{3,1,2,0:T(2,128)(2,1)S(1)}, bf16[4,1,128,128]{3,1,2,0:T(2,128)(2,1)S(1)}, u32[]{:S(2)}, u32[]{:S(2)}) collective-permute-start(bf16[4,1,128,128]{3,1,2,0:T(2,128)(2,1)S(1)} %get-tuple-element.5), channel_id=1, source_target_pairs={{0,1},{1,2},{2,3},{3,4},{4,5},{5,6},{6,7},{7,8},{8,9},{9,10},{10,1... | collective-permute-start | bytes 393224 | tf_op jit(solution)/shard_map/ppermute | solution.py:22
  32.3 1.9 collective-permute-start.2
  34.2 1.4 collective-permute-done.1
  35.6 5.9 %collective-permute-done.2 = bf16[4,1,128,128]{3,1,2,0:T(2,128)(2,1)S(1)} collective-permute-done((bf16[4,1,128,128]{3,1,2,0:T(2,128)(2,1)S(1)}, bf16[4,1,128,128]{3,1,2,0:T(2,128)(2,1)S(1)}, u32[]{:S(2)}, u32[]{:S(2)}) %collective-permute-start.2) | collective-permute-done | bytes 131104 | tf_op jit(solution)/shard_map/ppermute | solution.py:23
  41.5 2.1 fusion.6
  45.4 4.4 %fusion.27 = f32[2,8,8,17,128]{4,2,3,1,0:T(8,128)S(1)} fusion(bf16[3,3,3,128,128]{4,3,2,1,0:T(8,128)(2,1)S(1)} %copy-done.6, bf16[4,10,1,7,2,128]{5,3,4,1,0,2:T(8,128)(2,1)S(1)} %slice.16, bf16[4,10,1,8,17,128]{5,3,4,1,0,2:T(8,128)(2,1)S(1)} %copy.53, pred[8,17]{0,1:T(8,128)(4,1)S(1)} %copy-done.8), kind=kOutput, calls=%fused_computation.38 | convolution fusion | flops 1930133504 | bytes 3534984 | tf_op jit(solution)/shard_map/conv_general_dilated | solution.py:36
  50.4 3.5 %collective-permute-start.3 = (bf16[2,8,128,128]{3,1,2,0:T(8,128)(2,1)S(1)}, bf16[2,8,128,128]{3,1,2,0:T(8,128)(2,1)S(1)}, u32[]{:S(2)}, u32[]{:S(2)}) collective-permute-start(bf16[2,8,128,128]{3,1,2,0:T(8,128)(2,1)S(1)} %fusion.47), channel_id=1, source_target_pairs={{0,32},{32,64},{64,96},{96,128},{128,160},{160,192},{192,224},{1,3... | collective-permute-start | bytes 1572872 | tf_op jit(solution)/shard_map/ppermute | solution.py:12
  53.9 6.4 %collective-permute-done.3 = bf16[2,8,128,128]{3,1,2,0:T(8,128)(2,1)S(1)} collective-permute-done((bf16[2,8,128,128]{3,1,2,0:T(8,128)(2,1)S(1)}, bf16[2,8,128,128]{3,1,2,0:T(8,128)(2,1)S(1)}, u32[]{:S(2)}, u32[]{:S(2)}) %collective-permute-start.3) | collective-permute-done | bytes 524320 | tf_op jit(solution)/shard_map/ppermute | solution.py:12
  60.5 2.1 collective-permute-start.4
  62.6 7.4 %collective-permute-done.4 = bf16[4,1,128,128]{3,1,2,0:T(2,128)(2,1)S(1)} collective-permute-done((bf16[4,1,128,128]{3,1,2,0:T(2,128)(2,1)S(1)}, bf16[4,1,128,128]{3,1,2,0:T(2,128)(2,1)S(1)}, u32[]{:S(2)}, u32[]{:S(2)}) %collective-permute-start.4) | collective-permute-done | bytes 131104 | tf_op jit(solution)/shard_map/ppermute | solution.py:12
  72.0 1.3 fusion.32
  74.9 1.8 convolution_convert_fusion.1
  76.8 1.8 convolution_convert_fusion
  78.7 109.5 %all-gather.3.cloned.1.call-done = bf16[2,128,64,256]{3,2,1,0:T(8,128)(2,1)} async-done(((bf16[2,4,64,256]{3,2,1,0:T(8,128)(2,1)}), bf16[2,128,64,256]{3,2,1,0:T(8,128)(2,1)}) %all-gather.3.cloned.1.call-update) | async-done | bytes 8388624 | tf_op jit(solution)/shard_map/all_gather | solution.py:88
  188.2 12.6 %multiply_reduce_fusion = (f32[2,256]{1,0:T(2,128)S(1)}, f32[2,256,8192]{2,1,0:T(8,128)}) fusion(bf16[2,8192,256]{2,1,0:T(8,128)(2,1)} %bitcast.62, bf16[2,256,256]{2,1,0:T(8,128)(2,1)S(1)} %multiply_convert_fusion, bf16[256,256]{1,0:T(8,128)(2,1)S(1)} %copy-done.2), kind=kOutput, calls=%fused_computation.2 | convolution fusion | flops 2223111680 | bytes 25561088 | tf_op jit(solution)/shard_map/fqc,fkc->fqk/dot_general | solution.py:98
  200.7 8.7 %convert_reduce_fusion = f32[2,256]{1,0:T(2,128)S(1)} fusion(f32[2,256]{1,0:T(2,128)S(1)} %get-tuple-element.9, f32[2,256,8192]{2,1,0:T(8,128)} %get-tuple-element.10), kind=kLoop, calls=%fused_computation | loop fusion | flops 20971008 | bytes 16781312 | tf_op jit(solution)/shard_map/reduce_sum | solution.py:104
  209.4 79.6 %all-gather.5.cloned.1.call-done = bf16[2,128,64,256]{3,2,1,0:T(8,128)(2,1)} async-done(((bf16[2,4,64,256]{3,2,1,0:T(8,128)(2,1)}), bf16[2,128,64,256]{3,2,1,0:T(8,128)(2,1)}) %all-gather.5.cloned.1.call-update) | async-done | bytes 8388624 | tf_op jit(solution)/shard_map/all_gather | solution.py:91
  289.0 9.8 %fusion.49 = f32[2,256,256]{2,1,0:T(8,128)S(1)} fusion(bf16[2,8192,256]{2,1,0:T(8,128)(2,1)} %bitcast.70, f32[2,256,8192]{2,1,0:T(8,128)} %get-tuple-element.10, f32[2,256]{1,0:T(2,128)S(1)} %get-tuple-element.9, f32[2,256]{1,0:T(2,128)S(1)} %get-tuple-element.8, f32[2,256]{1,0:T(2,128)S(1)} %get-tuple-element.7, bf16[256,256]{1,0:T(8,128)(2,1)S(1)} %copy-done.7), kind=kOutput, calls=%fused_computation.61 | convolution fusion | flops 2227568640 | bytes 25827328 | tf_op jit(solution)/shard_map/fqc,cd->fqd/dot_general | solution.py:109
  299.2 0.9 copy.64
  (53 shorter events, 6.9 us)
Async XLA Ops:
  6.5 65.5 %copy-start = (bf16[3,3,3,128,256]{4,3,2,1,0:T(8,128)(2,1)S(1)}, bf16[3,3,3,128,256]{4,3,2,1,0:T(8,128)(2,1)}, u32[]{:S(2)}) copy-start(bf16[3,3,3,128,256]{4,3,2,1,0:T(8,128)(2,1)} %param.15) | copy-start | bytes 5308420
  6.5 181.6 %all-gather.3.cloned.1.call-start = ((), (), s32[]{:S(2)}) async-start(), calls=%async_computation | async-start | bytes 8650752 | tf_op jit(solution)/shard_map/all_gather | solution.py:88
  11.6 14.5 %collective-permute-start = (bf16[2,8,128,128]{3,1,2,0:T(8,128)(2,1)S(1)}, bf16[2,8,128,128]{3,1,2,0:T(8,128)(2,1)S(1)}, u32[]{:S(2)}, u32[]{:S(2)}) collective-permute-start(bf16[2,8,128,128]{3,1,2,0:T(8,128)(2,1)S(1)} %fusion.45), channel_id=1, source_target_pairs={{0,32},{32,64},{64,96},{96,128},{128,160},{160,192},{192,224},{1,3... | collective-permute-start | bytes 1572872 | tf_op jit(solution)/shard_map/ppermute | solution.py:12
  26.5 9.1 %collective-permute-start.1 = (bf16[4,1,128,128]{3,1,2,0:T(2,128)(2,1)S(1)}, bf16[4,1,128,128]{3,1,2,0:T(2,128)(2,1)S(1)}, u32[]{:S(2)}, u32[]{:S(2)}) collective-permute-start(bf16[4,1,128,128]{3,1,2,0:T(2,128)(2,1)S(1)} %get-tuple-element.5), channel_id=1, source_target_pairs={{0,1},{1,2},{2,3},{3,4},{4,5},{5,6},{6,7},{7,8},{8,9},{9,10},{10,1... | collective-permute-start | bytes 393224 | tf_op jit(solution)/shard_map/ppermute | solution.py:22
  32.3 9.2 %collective-permute-start.2 = (bf16[4,1,128,128]{3,1,2,0:T(2,128)(2,1)S(1)}, bf16[4,1,128,128]{3,1,2,0:T(2,128)(2,1)S(1)}, u32[]{:S(2)}, u32[]{:S(2)}) collective-permute-start(bf16[4,1,128,128]{3,1,2,0:T(2,128)(2,1)S(1)} %get-tuple-element.6), channel_id=1, source_target_pairs={{1,0},{2,1},{3,2},{4,3},{5,4},{6,5},{7,6},{8,7},{9,8},{10,9},{11,1... | collective-permute-start | bytes 393224 | tf_op jit(solution)/shard_map/ppermute | solution.py:23
  44.2 1.2 copy-start.6
  44.3 1.2 copy-start.8
  45.4 4.6 %copy-start.1 = (bf16[2,8,128,128]{3,2,1,0:T(8,128)(2,1)S(1)}, bf16[2,8,128,128]{3,2,1,0:T(8,128)(2,1)}, u32[]{:S(2)}) copy-start(bf16[2,8,128,128]{3,2,1,0:T(8,128)(2,1)} %param.11) | copy-start | bytes 1572868
  45.4 4.6 %copy-start.5 = (f32[128]{0:T(128)S(1)}, f32[128]{0:T(128)}, u32[]{:S(2)}) copy-start(f32[128]{0:T(128)} %param.14) | copy-start | bytes 1540
  50.4 9.9 %collective-permute-start.3 = (bf16[2,8,128,128]{3,1,2,0:T(8,128)(2,1)S(1)}, bf16[2,8,128,128]{3,1,2,0:T(8,128)(2,1)S(1)}, u32[]{:S(2)}, u32[]{:S(2)}) collective-permute-start(bf16[2,8,128,128]{3,1,2,0:T(8,128)(2,1)S(1)} %fusion.47), channel_id=1, source_target_pairs={{0,32},{32,64},{64,96},{96,128},{128,160},{160,192},{192,224},{1,3... | collective-permute-start | bytes 1572872 | tf_op jit(solution)/shard_map/ppermute | solution.py:12
  60.5 9.5 %collective-permute-start.4 = (bf16[4,1,128,128]{3,1,2,0:T(2,128)(2,1)S(1)}, bf16[4,1,128,128]{3,1,2,0:T(2,128)(2,1)S(1)}, u32[]{:S(2)}, u32[]{:S(2)}) collective-permute-start(bf16[4,1,128,128]{3,1,2,0:T(2,128)(2,1)S(1)} %pad_maximum_fusion), channel_id=1, source_target_pairs={{1,0},{2,1},{3,2},{4,3},{5,4},{6,5},{7,6},{8,7},{9,8},{10,9},{11,1... | collective-permute-start | bytes 393224 | tf_op jit(solution)/shard_map/ppermute | solution.py:12
  71.2 0.8 copy-start.9
  72.0 1.6 copy-start.3
  73.3 1.4 copy-start.4
  73.6 114.6 %copy-start.2 = (bf16[256,256]{1,0:T(8,128)(2,1)S(1)}, bf16[256,256]{1,0:T(8,128)(2,1)}, u32[]{:S(2)}) copy-start(bf16[256,256]{1,0:T(8,128)(2,1)} %param.18) | copy-start | bytes 393220
  76.8 212.2 %all-gather.5.cloned.1.call-start = ((), (), s32[]{:S(2)}) async-start(), calls=%async_computation.1 | async-start | bytes 8650752 | tf_op jit(solution)/shard_map/all_gather | solution.py:91
  200.7 88.3 %copy-start.7 = (bf16[256,256]{1,0:T(8,128)(2,1)S(1)}, bf16[256,256]{1,0:T(8,128)(2,1)}, u32[]{:S(2)}) copy-start(bf16[256,256]{1,0:T(8,128)(2,1)} %param.21) | copy-start | bytes 393220
Sparse Core Ops, SparseCore 0:
  76.9 111.2 all-gather.2
  191.0 97.9 all-gather.4
where the time goes:
time: 307 us
  waiting for transfers between devices  221 us (72%)
  matrix products  31.6 us (10%)
  other arithmetic  18.6 us (6%)
  starting transfers between devices  17.4 us (6%)
  between operations  13.8 us (4%)
  local copies, waits for them, and re-layouts  4.87 us (2%)
    all_gather x1, waiting for transfers between devices, body(): lax.all_gather(key_grid, 'space', axis=1, tiled=True)  109 us
    all_gather x1, waiting for transfers between devices, body(): lax.all_gather(value_grid, 'space', axis=1, tiled=True)  79.6 us
    ppermute x3, waiting for transfers between devices, shifted(): return lax.ppermute(block, axis, route)  24.3 us
    dot_general x1, matrix products, body(): jnp.einsum('fqc,fkc->fqk', queries, key_block, preferred_element_type=jnp...  12.6 us
    dot_general x1, matrix products, body(): jnp.einsum('fqc,cd->fqd', attended, output_weight, preferred_element_type...  9.76 us
    ppermute x3, starting transfers between devices, shifted(): return lax.ppermute(block, axis, route)  9.61 us
    reduce_sum x1, other arithmetic, body(): jnp.sum(probs.astype(jnp.float32), axis=-1)  8.67 us
  transfers between devices with their start and end apart: 7, of which 7 were waited for; matrix products, arithmetic and copies ran while one was open for 8% of the time, Pallas kernels for 0%

commit v1 on v0

v1 whole, which is shorter than its diff:
```python
import jax
import jax.numpy as jnp
from jax import lax
from jax.experimental import pallas as pl
from jax.experimental.pallas import tpu as pltpu
from jax.sharding import PartitionSpec as P

epsilon = 1e-05
f32 = jnp.float32
bf16 = jnp.bfloat16
VMEM = pl.BlockSpec(memory_space=pltpu.VMEM)
SMEM = pl.BlockSpec(memory_space=pltpu.SMEM)
COLS = 128
C1 = 128
C2 = 256
ROWS = 8
HALF = 64
QUERIES = 256


def call(kernel, outs, ins, scratch=(), scalars=0, aliases=None, flops=0, nbytes=0):
    return pl.pallas_call(
        kernel,
        out_shape=[jax.ShapeDtypeStruct(s, d) for s, d in outs],
        in_specs=[SMEM] * scalars + [VMEM] * (len(ins) - scalars),
        out_specs=[VMEM] * len(outs),
        scratch_shapes=list(scratch),
        input_output_aliases=aliases or {},
        compiler_params=pltpu.CompilerParams(vmem_limit_bytes=48 * 1024 * 1024),
        cost_estimate=pl.CostEstimate(flops=flops, bytes_accessed=nbytes, transcendentals=0),
    )(*ins)


def dot(a, b):
    return jnp.dot(a, b, preferred_element_type=f32)


def averaging():
    i = lax.broadcasted_iota(jnp.int32, (2 * C1, 2 * C1), 0) // C1
    j = lax.broadcasted_iota(jnp.int32, (2 * C1, 2 * C1), 1) // C1
    return jnp.where(i == j, 1.0 / C1, 0.0).astype(bf16)


def activate(pair, gain2, mean_of):
    centred = pair.astype(f32) - dot(pair, mean_of)
    squares = centred * centred
    high = squares.astype(bf16)
    low = (squares - high.astype(f32)).astype(bf16)
    spread = dot(high, mean_of) + dot(low, mean_of)
    y = centred * lax.rsqrt(spread + epsilon) * gain2
    return y / (1.0 + jnp.exp(-y))


def store_shifted(taps, row, act):
    col = lax.broadcasted_iota(jnp.int32, act.shape, 0)
    at = pl.ds(row * COLS, COLS)
    taps[0, at, :] = jnp.where(col == 0, 0.0, pltpu.roll(act, 1, 0)).astype(bf16)
    taps[1, at, :] = act.astype(bf16)
    taps[2, at, :] = jnp.where(col == COLS - 1, 0.0, pltpu.roll(act, COLS - 1, 0)).astype(bf16)


def fill_taps(taps, above, middle, below, gain_ref):
    gain2 = jnp.concatenate([gain_ref[...], gain_ref[...]], axis=1)
    mean_of = averaging()

    def put(row, ref, i):
        pair = jnp.concatenate([ref[0, i], ref[1, i]], axis=1)
        store_shifted(taps, row, activate(pair, gain2, mean_of))

    for row in range(ROWS + 3):
        if row < 1:
            put(row, above[0], above[1])
        elif row <= ROWS:
            put(row, middle, row - 1)
        else:
            put(row, below[0], below[1] + row - ROWS - 1)


def conv1_taps(taps, acc, weight_of, first):
    size = (ROWS + 1) * COLS
    for kr in range(3):
        for kc in range(3):
            part = dot(taps[kc, kr * COLS : kr * COLS + size, :], weight_of(kr, kc))
            if first and kr == 0 and kc == 0:
                acc[...] = part
            else:
                acc[...] += part


def stack(a, b, c, d):
    return jnp.concatenate([jnp.concatenate([a, b], axis=1), jnp.concatenate([c, d], axis=1)], axis=0)


def own_kernel(video, above, below, gain, weight, acc, taps):
    fill_taps(taps, (above, 0), video, (below, 0), gain)
    none = jnp.zeros((C1, C1), bf16)

    def weight_of(kr, kc):
        return stack(weight[2, kr, kc], weight[1, kr, kc], none, weight[2, kr, kc])

    conv1_taps(taps, acc, weight_of, True)


def halo_kernel(
    last, acc_in, halo, corner, video, below, gain, weight, bias, down, send, half_taps, acc, taps, wide
):
    fill_taps(taps, (corner, 0), halo, (corner, 1), gain)
    none = jnp.zeros((C1, C1), bf16)

    def weight_of(kr, kc):
        return stack(weight[0, kr, kc], none, weight[1, kr, kc], weight[0, kr, kc])

    acc[...] = acc_in[...]
    conv1_taps(taps, acc, weight_of, False)
    bias2 = jnp.concatenate([bias[...], bias[...]], axis=1)
    keep = jnp.where(last[0] == 1, 0.0, 1.0)
    for row in range(ROWS + 1):
        src, i = (video, row) if row < ROWS else (below, 0)
        pair = jnp.concatenate([src[0, i], src[1, i]], axis=1).astype(f32)
        at = pl.ds(row * COLS, COLS)
        summed = (pair + acc[at, :] + bias2).astype(bf16).astype(f32)
        if row == ROWS:
            summed = summed * keep
        wide[0, at, :] = summed[:, :C1]
        wide[1, at, :] = summed[:, C1:]
    j = lax.broadcasted_iota(jnp.int32, (HALF, C1), 0)
    for row in range(ROWS + 1):
        place = row // 2 if row % 2 == 0 else 5 + row // 2
        for frame in range(2):
            even = wide[frame, pl.ds(row * COLS, HALF, stride=2), :]
            odd = wide[frame, pl.ds(row * COLS + 1, HALF, stride=2), :]
            after = jnp.where(j == HALF - 1, 0.0, pltpu.roll(even, HALF - 1, 0))
            lanes = pl.ds(frame * C1, C1)
            at = pl.ds(place * HALF, HALF)
            half_taps[0, at, lanes] = even.astype(bf16)
            half_taps[1, at, lanes] = odd.astype(bf16)
            half_taps[2, at, lanes] = after.astype(bf16)
    first = jnp.zeros((QUERIES, C2), f32)
    second = jnp.zeros((QUERIES, C2), f32)
    for kr in range(3):
        start = (0, 5 * HALF, HALF)[kr]
        for kc in range(3):
            tile = half_taps[kc, start : start + QUERIES, :]
            first += dot(tile, jnp.concatenate([down[0, kr, kc], down[1, kr, kc]], axis=0))
            second += dot(tile[:, C1:], down[0, kr, kc])
    send[0] = first.astype(bf16)
    send[1] = second.astype(bf16)


def down_kernel(half_taps, down, bias, out):
    first = jnp.zeros((QUERIES, C2), f32) + bias[...]
    second = jnp.zeros((QUERIES, C2), f32) + bias[...]
    for kr in range(3):
        start = (0, 5 * HALF, HALF)[kr]
        for kc in range(3):
            tile = half_taps[kc, start : start + QUERIES, :]
            first += dot(tile[:, :C1], down[2, kr, kc])
            second += dot(tile, jnp.concatenate([down[1, kr, kc], down[2, kr, kc]], axis=0))
    out[0] = first
    out[1] = second


def norm_kernel(mine, part, received, gain, reduced, keep, send):
    frames = []
    for frame in range(2):
        value = part[frame] + received[frame].astype(f32)
        reduced[frame] = value
        centred = value - jnp.mean(value, axis=1, keepdims=True)
        spread = jnp.mean(centred * centred, axis=1, keepdims=True)
        frames.append(centred * lax.rsqrt(spread + epsilon) * gain[...])
    pick = mine[0] == 0
    keep[...] = jnp.where(pick, frames[0], frames[1]).astype(bf16)
    send[...] = jnp.where(pick, frames[1], frames[0]).astype(bf16)


TILE = 256
BLOCK = 2 * QUERIES
ALL = 2 * BLOCK


def attend_block(queries, total, top, mass, block, key_weight, value_weight, first):
    normed = block[...]
    keys = dot(normed, key_weight[...]).astype(bf16)
    values = dot(normed, value_weight[...]).astype(bf16)
    for tile in range(ALL // TILE):
        at = pl.ds(tile * TILE, TILE)
        scores = lax.dot_general(
            queries[at, :], keys, (((1,), (1,)), ((), ())), preferred_element_type=f32
        )
        highest = jnp.max(scores, axis=1, keepdims=True)
        if not first:
            old = top[at, :]
            new = jnp.maximum(old, highest)
            rescale = jnp.exp(old - new)
            highest = new[:, :1]
        else:
            new = jnp.broadcast_to(highest, (TILE, 128))
        weights = jnp.exp(scores - highest).astype(bf16)
        gathered = weights.astype(f32)
        sums = sum(gathered[:, i * 128 : (i + 1) * 128] for i in range(BLOCK // 128))
        product = dot(weights, values)
        if first:
            mass[at, :] = sums
            total[at, :] = product
        else:
            mass[at, :] = mass[at, :] * rescale + sums
            total[at, :] = total[at, :] * rescale[:, :1] + product
        top[at, :] = new


def first_attend_kernel(own, other, query_weight, key_weight, value_weight, queries, total, top, mass):
    scale = C2**-0.5
    for i, ref in enumerate((own, other)):
        at = pl.ds(i * BLOCK, BLOCK)
        queries[at, :] = (dot(ref[...], query_weight[...]).astype(bf16) * scale).astype(bf16)
    attend_block(queries, total, top, mass, own, key_weight, value_weight, True)


def attend_kernel(count, last, *refs):
    queries, total_in, top_in, mass_in = refs[:4]
    blocks = refs[4 : 4 + count]
    key_weight, value_weight = refs[4 + count : 6 + count]
    if last:
        mine, theirs, total, top, mass = refs[6 + count :]
    else:
        total, top, mass = refs[6 + count :]
    total[...] = total_in[...]
    top[...] = top_in[...]
    mass[...] = mass_in[...]
    for block in blocks:
        attend_block(queries, total, top, mass, block, key_weight, value_weight, False)
    if last:
        for out, at in ((mine, pl.ds(0, BLOCK)), (theirs, pl.ds(BLOCK, BLOCK))):
            out[:, :C2] = total[at, :]
            out[:, C2 : C2 + 128] = top[at, :]
            whole = jnp.sum(mass[at, :], axis=1, keepdims=True)
            out[:, C2 + 128 :] = jnp.broadcast_to(whole, (BLOCK, 128))


def merge_kernel(mine, theirs, keep, send):
    top_a, top_b = mine[:, C2 : C2 + 128], theirs[:, C2 : C2 + 128]
    top = jnp.maximum(top_a, top_b)
    scale_a, scale_b = jnp.exp(top_a - top), jnp.exp(top_b - top)
    inverse = 1.0 / (mine[:, C2 + 128 :] * scale_a + theirs[:, C2 + 128 :] * scale_b)
    scale_a, scale_b = scale_a * inverse, scale_b * inverse
    attended = (mine[:, :C2] * scale_a[:, :1] + theirs[:, :C2] * scale_b[:, :1]).astype(bf16)
    keep[...] = attended[:QUERIES]
    send[...] = attended[QUERIES:]


def last_kernel(mine, reduced, keep, received, weight, out):
    here = mine[0]
    there = 1 - here
    out[here] = reduced[here] + dot(keep[...], weight[...])
    out[there] = reduced[there] + dot(received[...], weight[...])


def body(
    video,
    norm_gain,
    conv_weight,
    conv_bias,
    down_weight,
    down_bias,
    attention_gain,
    query_weight,
    key_weight,
    value_weight,
    output_weight,
):
    space = lax.axis_size("space")
    times = lax.axis_size("tm")
    place = lax.axis_index("space")
    is_last = (place == space - 1).astype(jnp.int32).reshape(1)
    frame = ((place // 2) % 2).astype(jnp.int32).reshape(1)
    gain = norm_gain.reshape(1, C1)

    def next_frames(x):
        return lax.ppermute(x, "tm", [(i, i + 1) for i in range(times - 1)])

    def along_z(x, distance):
        return lax.ppermute(x, "space", [(i, (i + 4 * distance) % space) for i in range(space)])

    def swap(x, bit):
        return lax.ppermute(x, "space", [(i, i ^ bit) for i in range(space)])

    above = lax.ppermute(video[:, -1:], "space", [(i, i + 1) for i in range(space - 1)])
    below = lax.ppermute(video[:, :2], "space", [(i + 1, i) for i in range(space - 1)])
    halo = next_frames(video)
    corner = next_frames(jnp.concatenate([above, below], axis=1))

    size = (ROWS + 1) * COLS
    taps = pltpu.VMEM((3, (ROWS + 3) * COLS, 2 * C1), bf16)
    (acc,) = call(
        own_kernel,
        [((size, 2 * C1), f32)],
        [video, above, below, gain, conv_weight],
        [taps],
        flops=2 * 9 * size * 256 * 256,
        nbytes=3_000_000,
    )
    send, half_taps = call(
        halo_kernel,
        [((2, QUERIES, C2), bf16), ((3, 9 * HALF, 2 * C1), bf16)],
        [is_last, acc, halo, corner, video, below, gain, conv_weight, conv_bias.reshape(1, C1), down_weight],
        [pltpu.VMEM((size, 2 * C1), f32), taps, pltpu.VMEM((2, size, C1), f32)],
        scalars=1,
        flops=2 * 9 * size * 256 * 256 + 2 * 18 * 256 * 256 * 256,
        nbytes=6_000_000,
    )
    received = next_frames(send)
    (part,) = call(
        down_kernel,
        [((2, QUERIES, C2), f32)],
        [half_taps, down_weight, down_bias.reshape(1, C2)],
        flops=2 * 18 * 256 * 256 * 256,
        nbytes=3_000_000,
    )
    reduced, keep, give = call(
        norm_kernel,
        [((2, QUERIES, C2), f32), ((QUERIES, C2), bf16), ((QUERIES, C2), bf16)],
        [frame, part, received, attention_gain.reshape(1, C2)],
        scalars=1,
        nbytes=2_000_000,
    )
    own = jnp.concatenate([keep, swap(give, 2)], axis=0)
    plus, minus = along_z(own, 1), along_z(own, -1)
    other = swap(own, 1)
    state = [((ALL, C2), f32), ((ALL, 128), f32), ((ALL, 128), f32)]
    block_flops = 2 * BLOCK * 256 * (512 + 2 * ALL)
    queries, *carry = call(
        first_attend_kernel,
        [((ALL, C2), bf16)] + state,
        [own, other, query_weight, key_weight, value_weight],
        flops=block_flops,
        nbytes=4_000_000,
    )
    for step in range(1, 4):
        blocks = [plus, minus]
        plus = along_z(plus, 1)
        if step < 3:
            minus = along_z(minus, -1)
        carry = call(
            lambda *refs: attend_kernel(2, False, *refs),
            state,
            [queries, *carry, *blocks, key_weight, value_weight],
            aliases={1: 0, 2: 1, 3: 2},
            flops=2 * block_flops,
            nbytes=6_000_000,
        )
    ends = [((BLOCK, C2 + 256), f32)] * 2
    mine, theirs = call(
        lambda *refs: attend_kernel(1, True, *refs),
        ends,
        [queries, *carry, plus, key_weight, value_weight],
        [pltpu.VMEM(s, d) for s, d in state],
        flops=block_flops,
        nbytes=6_000_000,
    )
    theirs = swap(theirs, 1)
    keep, give = call(
        merge_kernel,
        [((QUERIES, C2), bf16)] * 2,
        [mine, theirs],
        nbytes=3_000_000,
    )
    back = swap(give, 2)
    (encoded,) = call(
        last_kernel,
        [((2, QUERIES, C2), f32)],
        [frame, reduced, keep, back, output_weight],
        scalars=1,
        nbytes=2_000_000,
    )
    return encoded.reshape(2, ROWS // 2, HALF, C2)


def solution(mesh):
    in_specs = (P("tm", "space", None, None), P(), P(), P(), P(), P(), P(), P(), P(), P(), P())
    out_specs = P("tm", "space", None, None)
    return jax.shard_map(body, mesh=mesh, in_specs=in_specs, out_specs=out_specs, check_vma=False)
```

time: 307 us -> 106 us (0.35)
  the two profiles are of different devices: /device:TPU:1 before, /device:TPU:8 now
where the time goes in v1:
time: 106 us
  waiting for transfers between devices  38.3 us (36%)
  starting transfers between devices  37.2 us (35%)
  Pallas kernels  23.4 us (22%)
  local copies, waits for them, and re-layouts  6.3 us (6%)
    pallas_call x11, Pallas kernels, call(): pl.pallas_call(kernel, out_shape=[jax.ShapeDtypeStruct(s, d) for s, d in...  23.4 us
    ppermute x7, waiting for transfers between devices, along_z(): lax.ppermute(x, 'space', [(i, (i + 4 * distance) % space) for i in range(...  17.2 us
    ppermute x7, starting transfers between devices, along_z(): lax.ppermute(x, 'space', [(i, (i + 4 * distance) % space) for i in range(...  13.8 us
    ppermute x4, waiting for transfers between devices, swap(): return lax.ppermute(x, 'space', [(i, i ^ bit) for i in range(space)])  13 us
    ppermute x4, starting transfers between devices, swap(): return lax.ppermute(x, 'space', [(i, i ^ bit) for i in range(space)])  9.67 us
    ppermute x3, starting transfers between devices, next_frames(): return lax.ppermute(x, 'tm', [(i, i + 1) for i in range(times - 1)])  9.46 us
    ppermute x3, waiting for transfers between devices, next_frames(): return lax.ppermute(x, 'tm', [(i, i + 1) for i in range(times - 1)])  7.26 us
    unnamed x29, local copies, waits for them, and re-layouts  4.51 us
  transfers between devices with their start and end apart: 16, of which 9 were waited for; matrix products, arithmetic and copies ran while one was open for 2% of the time, Pallas kernels for 13%

profile of v1, /device:TPU:8, one launch (start us, length us, event | category | flops | bytes accessed | tf_op | source)
XLA Modules:
  0.0 105.5 jit_solution(16635602586291229078)
XLA Ops:
  0.0 3.4 %collective-permute-start.2 = (bf16[2,8,128,128]{3,2,1,0:T(8,128)(2,1)}, bf16[2,8,128,128]{3,2,1,0:T(8,128)(2,1)S(1)}, u32[]{:S(2)}, u32[]{:S(2)}) collective-permute-start(bf16[2,8,128,128]{3,2,1,0:T(8,128)(2,1)} %video.3), channel_id=1, source_target_pairs={{0,32},{32,64},{64,96},{96,128},{128,160},{160,192},{192,224},{1,3... | collective-permute-start | bytes 1572872 | tf_op jit(solution)/shard_map/ppermute | solution.py:279
  4.3 1.3 %collective-permute-start.1 = (bf16[2,2,128,128]{3,2,1,0:T(8,128)(2,1)S(1)}, bf16[2,2,128,128]{3,2,1,0:T(8,128)(2,1)S(1)}, u32[]{:S(2)}, u32[]{:S(2)}) collective-permute-start(bf16[2,2,128,128]{3,2,1,0:T(8,128)(2,1)S(1)} %slice.7), channel_id=1, source_target_pairs={{1,0},{2,1},{3,2},{4,3},{5,4},{6,5},{7,6},{8,7},{9,8},{10,9},{11,1... | collective-permute-start | bytes 393224 | tf_op jit(solution)/shard_map/ppermute | solution.py:288
  6.5 3.0 %collective-permute-start = (bf16[2,1,128,128]{3,2,1,0:T(8,128)(2,1)S(1)}, bf16[2,1,128,128]{3,2,1,0:T(8,128)(2,1)S(1)}, u32[]{:S(2)}, u32[]{:S(2)}) collective-permute-start(bf16[2,1,128,128]{3,2,1,0:T(8,128)(2,1)S(1)} %slice.6), channel_id=1, source_target_pairs={{0,1},{1,2},{2,3},{3,4},{4,5},{5,6},{6,7},{7,8},{8,9},{9,10},{10,1... | collective-permute-start | bytes 196616 | tf_op jit(solution)/shard_map/ppermute | solution.py:287
  10.4 3.5 %collective-permute-start.3 = (bf16[2,3,128,128]{3,2,1,0:T(8,128)(2,1)S(1)}, bf16[2,3,128,128]{3,2,1,0:T(8,128)(2,1)S(1)}, u32[]{:S(2)}, u32[]{:S(2)}) collective-permute-start(bf16[2,3,128,128]{3,2,1,0:T(8,128)(2,1)S(1)} %pad_maximum_fusion), channel_id=1, source_target_pairs={{0,32},{32,64},{64,96},{96,128},{128,160},{160,192},{192,224},{1,3... | collective-permute-start | bytes 589832 | tf_op jit(solution)/shard_map/ppermute | solution.py:279
  16.8 2.9 %shard_map.109.acc_in = f32[1152,256]{1,0:T(8,128)S(1)} custom-call(bf16[2,8,128,128]{3,2,1,0:T(8,128)(2,1)S(1)} %copy-done.4, bf16[2,1,128,128]{3,2,1,0:T(8,128)(2,1)S(1)} %collective-permute-done.above, bf16[2,2,128,128]{3,2,1,0:T(8,128)(2,1)S(1)} %collective-permute-done.1.below, f32[1,128]{1,0:T(1,128)S(1)} %bitcast.9, ...), custom_call_target="tpu_custom_call" | custom-call | flops 1358954496 | bytes 3000000 | tf_op jit(solution)/shard_map/pallas_call | solution.py:22
  22.5 7.0 %shard_map.110 = (bf16[2,256,256]{2,1,0:T(8,128)(2,1)}, bf16[3,576,256]{2,1,0:T(8,128)(2,1)S(1)}) custom-call(s32[1]{0:T(128)} %bitcast.1.last, f32[1152,256]{1,0:T(8,128)S(1)} %shard_map.109.acc_in, bf16[2,8,128,128]{3,2,1,0:T(8,128)(2,1)S(1)} %collective-permute-done.2.halo, bf16[2,3,128,128]{3,2,1,0:T(8,128)(2,1)S(1)} %copy-done.10, ...), custom_call_target="tpu_custom_call" | custom-call | flops 1962934272 | bytes 6000000 | tf_op jit(solution)/shard_map/pallas_call | solution.py:22
  29.4 2.6 %collective-permute-start.4 = (bf16[2,256,256]{2,1,0:T(8,128)(2,1)}, bf16[2,256,256]{2,1,0:T(8,128)(2,1)S(1)}, u32[]{:S(2)}, u32[]{:S(2)}) collective-permute-start(bf16[2,256,256]{2,1,0:T(8,128)(2,1)} %get-tuple-element.28), channel_id=1, source_target_pairs={{0,32},{32,64},{64,96},{96,128},{128,160},{160,192},{192,224},{1,3... | collective-permute-start | bytes 786440 | tf_op jit(solution)/shard_map/ppermute | solution.py:279
  32.9 6.0 %collective-permute-done.4.received = bf16[2,256,256]{2,1,0:T(8,128)(2,1)S(1)} collective-permute-done((bf16[2,256,256]{2,1,0:T(8,128)(2,1)}, bf16[2,256,256]{2,1,0:T(8,128)(2,1)S(1)}, u32[]{:S(2)}, u32[]{:S(2)}) %collective-permute-start.4) | collective-permute-done | bytes 262176 | tf_op jit(solution)/shard_map/ppermute | solution.py:279
  39.2 9.5 %collective-permute-start.5 = (bf16[256,256]{1,0:T(8,128)(2,1)S(1)}, bf16[256,256]{1,0:T(8,128)(2,1)S(1)}, u32[]{:S(2)}, u32[]{:S(2)}) collective-permute-start(bf16[256,256]{1,0:T(8,128)(2,1)S(1)} %get-tuple-element.31), channel_id=1, source_target_pairs={{0,2},{1,3},{2,0},{3,1},{4,6},{5,7},{6,4},{7,5},{8,10},{9,11},{10,... | collective-permute-start | bytes 393224 | tf_op jit(solution)/shard_map/ppermute | solution.py:285
  48.7 3.3 %collective-permute-done.5 = bf16[256,256]{1,0:T(8,128)(2,1)S(1)} collective-permute-done((bf16[256,256]{1,0:T(8,128)(2,1)S(1)}, bf16[256,256]{1,0:T(8,128)(2,1)S(1)}, u32[]{:S(2)}, u32[]{:S(2)}) %collective-permute-start.5) | collective-permute-done | bytes 131104 | tf_op jit(solution)/shard_map/ppermute | solution.py:285
  52.0 2.6 %collective-permute-start.7 = (bf16[512,256]{1,0:T(8,128)(2,1)S(1)}, bf16[512,256]{1,0:T(8,128)(2,1)S(1)}, u32[]{:S(2)}, u32[]{:S(2)}) collective-permute-start(bf16[512,256]{1,0:T(8,128)(2,1)S(1)} %constant_dynamic-update-slice_fusion.own), channel_id=1, source_target_pairs={{0,4},{1,5},{2,6},{3,7},{4,8},{5,9},{6,10},{7,11},{8,12},{9,13},{1... | collective-permute-start | bytes 786440 | tf_op jit(solution)/shard_map/ppermute | solution.py:282
  54.7 4.6 %collective-permute-start.8 = (bf16[512,256]{1,0:T(8,128)(2,1)S(1)}, bf16[512,256]{1,0:T(8,128)(2,1)S(1)}, u32[]{:S(2)}, u32[]{:S(2)}) collective-permute-start(bf16[512,256]{1,0:T(8,128)(2,1)S(1)} %constant_dynamic-update-slice_fusion.own), channel_id=1, source_target_pairs={{0,28},{1,29},{2,30},{3,31},{4,0},{5,1},{6,2},{7,3},{8,4},{9,5},{1... | collective-permute-start | bytes 786440 | tf_op jit(solution)/shard_map/ppermute | solution.py:282
  59.3 7.0 %collective-permute-done.7.refs_4_ = bf16[512,256]{1,0:T(8,128)(2,1)S(1)} collective-permute-done((bf16[512,256]{1,0:T(8,128)(2,1)S(1)}, bf16[512,256]{1,0:T(8,128)(2,1)S(1)}, u32[]{:S(2)}, u32[]{:S(2)}) %collective-permute-start.7) | collective-permute-done | bytes 262176 | tf_op jit(solution)/shard_map/ppermute | solution.py:282
  66.3 3.2 %collective-permute-start.10 = (bf16[512,256]{1,0:T(8,128)(2,1)S(1)}, bf16[512,256]{1,0:T(8,128)(2,1)S(1)}, u32[]{:S(2)}, u32[]{:S(2)}) collective-permute-start(bf16[512,256]{1,0:T(8,128)(2,1)S(1)} %collective-permute-done.8.refs_5_), channel_id=1, source_target_pairs={{0,28},{1,29},{2,30},{3,31},{4,0},{5,1},{6,2},{7,3},{8,4},{9,5},{1... | collective-permute-start | bytes 786440 | tf_op jit(solution)/shard_map/ppermute | solution.py:282
  69.5 6.2 %collective-permute-done.9.refs_4_ = bf16[512,256]{1,0:T(8,128)(2,1)S(1)} collective-permute-done((bf16[512,256]{1,0:T(8,128)(2,1)S(1)}, bf16[512,256]{1,0:T(8,128)(2,1)S(1)}, u32[]{:S(2)}, u32[]{:S(2)}) %collective-permute-start.9) | collective-permute-done | bytes 262176 | tf_op jit(solution)/shard_map/ppermute | solution.py:282
  75.7 3.2 %collective-permute-start.12 = (bf16[512,256]{1,0:T(8,128)(2,1)S(1)}, bf16[512,256]{1,0:T(8,128)(2,1)S(1)}, u32[]{:S(2)}, u32[]{:S(2)}) collective-permute-start(bf16[512,256]{1,0:T(8,128)(2,1)S(1)} %collective-permute-done.10.refs_5_), channel_id=1, source_target_pairs={{0,28},{1,29},{2,30},{3,31},{4,0},{5,1},{6,2},{7,3},{8,4},{9,5},{1... | collective-permute-start | bytes 786440 | tf_op jit(solution)/shard_map/ppermute | solution.py:282
  79.0 1.3 %shard_map.113 = (bf16[1024,256]{1,0:T(8,128)(2,1)S(1)}, f32[1024,256]{1,0:T(8,128)S(1)}, f32[1024,128]{1,0:T(8,128)S(1)}, f32[1024,128]{1,0:T(8,128)S(1)}) custom-call(bf16[512,256]{1,0:T(8,128)(2,1)S(1)} %constant_dynamic-update-slice_fusion.own, bf16[512,256]{1,0:T(8,128)(2,1)S(1)} %collective-permute-done.6.other, bf16[256,256]{1,0:T(8,128)(2,1)S(1)} %copy-done.11, ...), custom_call_target="tpu_custom_call" | custom-call | flops 671088640 | bytes 4000000 | tf_op jit(solution)/shard_map/pallas_call | solution.py:22
  80.3 4.0 %collective-permute-done.11.refs_4_ = bf16[512,256]{1,0:T(8,128)(2,1)S(1)} collective-permute-done((bf16[512,256]{1,0:T(8,128)(2,1)S(1)}, bf16[512,256]{1,0:T(8,128)(2,1)S(1)}, u32[]{:S(2)}, u32[]{:S(2)}) %collective-permute-start.11) | collective-permute-done | bytes 262176 | tf_op jit(solution)/shard_map/ppermute | solution.py:282
  84.3 2.8 %shard_map.114 = (f32[1024,256]{1,0:T(8,128)S(1)}, f32[1024,128]{1,0:T(8,128)S(1)}, f32[1024,128]{1,0:T(8,128)S(1)}) custom-call(bf16[1024,256]{1,0:T(8,128)(2,1)S(1)} %get-tuple-element.32.refs_0_, f32[1024,256]{1,0:T(8,128)S(1)} %get-tuple-element.33.refs_1_, ...), custom_call_target="tpu_custom_call", output_to_operand_aliasing={{0}: (1, {}), {1}: (2, {}), {2}: (3, {})} | custom-call | flops 1342177280 | bytes 6000000 | tf_op jit(solution)/shard_map/pallas_call | solution.py:22
  87.1 2.8 %shard_map.115 = (f32[1024,256]{1,0:T(8,128)S(1)}, f32[1024,128]{1,0:T(8,128)S(1)}, f32[1024,128]{1,0:T(8,128)S(1)}) custom-call(bf16[1024,256]{1,0:T(8,128)(2,1)S(1)} %get-tuple-element.32.refs_0_, f32[1024,256]{1,0:T(8,128)S(1)} %get-tuple-element.36.refs_1_, ...), custom_call_target="tpu_custom_call", output_to_operand_aliasing={{0}: (1, {}), {1}: (2, {}), {2}: (3, {})} | custom-call | flops 1342177280 | bytes 6000000 | tf_op jit(solution)/shard_map/pallas_call | solution.py:22
  89.9 2.8 %shard_map.116 = (f32[1024,256]{1,0:T(8,128)S(1)}, f32[1024,128]{1,0:T(8,128)S(1)}, f32[1024,128]{1,0:T(8,128)S(1)}) custom-call(bf16[1024,256]{1,0:T(8,128)(2,1)S(1)} %get-tuple-element.32.refs_0_, f32[1024,256]{1,0:T(8,128)S(1)} %get-tuple-element.39.refs_1_, ...), custom_call_target="tpu_custom_call", output_to_operand_aliasing={{0}: (1, {}), {1}: (2, {}), {2}: (3, {})} | custom-call | flops 1342177280 | bytes 6000000 | tf_op jit(solution)/shard_map/pallas_call | solution.py:22
  92.7 1.6 %shard_map.117 = (f32[512,512]{1,0:T(8,128)S(1)}, f32[512,512]{1,0:T(8,128)S(1)}) custom-call(bf16[1024,256]{1,0:T(8,128)(2,1)S(1)} %get-tuple-element.32.refs_0_, f32[1024,256]{1,0:T(8,128)S(1)} %get-tuple-element.42.refs_1_, f32[1024,128]{1,0:T(8,128)S(1)} %get-tuple-element.43.refs_2_, f32[1024,128]{1,0:T(8,128)S(1)} %get-tuple-element.44.refs_3_, ...), custom_call_target="tpu_custom_call" | custom-call | flops 671088640 | bytes 6000000 | tf_op jit(solution)/shard_map/pallas_call | solution.py:22
  94.4 2.6 %collective-permute-done.14.theirs = f32[512,512]{1,0:T(8,128)S(1)} collective-permute-done((f32[512,512]{1,0:T(8,128)S(1)}, f32[512,512]{1,0:T(8,128)S(1)}, u32[]{:S(2)}, u32[]{:S(2)}) %collective-permute-start.14) | collective-permute-done | bytes 1048608 | tf_op jit(solution)/shard_map/ppermute | solution.py:285
  97.4 7.0 %collective-permute-done.15.received = bf16[256,256]{1,0:T(8,128)(2,1)S(1)} collective-permute-done((bf16[256,256]{1,0:T(8,128)(2,1)S(1)}, bf16[256,256]{1,0:T(8,128)(2,1)S(1)}, u32[]{:S(2)}, u32[]{:S(2)}) %collective-permute-start.15) | collective-permute-done | bytes 131104 | tf_op jit(solution)/shard_map/ppermute | solution.py:285
  (52 shorter events, 11.0 us)
Async XLA Ops:
  0.0 21.6 %collective-permute-start.2 = (bf16[2,8,128,128]{3,2,1,0:T(8,128)(2,1)}, bf16[2,8,128,128]{3,2,1,0:T(8,128)(2,1)S(1)}, u32[]{:S(2)}, u32[]{:S(2)}) collective-permute-start(bf16[2,8,128,128]{3,2,1,0:T(8,128)(2,1)} %video.3), channel_id=1, source_target_pairs={{0,32},{32,64},{64,96},{96,128},{128,160},{160,192},{192,224},{1,3... | collective-permute-start | bytes 1572872 | tf_op jit(solution)/shard_map/ppermute | solution.py:279
  4.3 6.1 %collective-permute-start.1 = (bf16[2,2,128,128]{3,2,1,0:T(8,128)(2,1)S(1)}, bf16[2,2,128,128]{3,2,1,0:T(8,128)(2,1)S(1)}, u32[]{:S(2)}, u32[]{:S(2)}) collective-permute-start(bf16[2,2,128,128]{3,2,1,0:T(8,128)(2,1)S(1)} %slice.7), channel_id=1, source_target_pairs={{1,0},{2,1},{3,2},{4,3},{5,4},{6,5},{7,6},{8,7},{9,8},{10,9},{11,1... | collective-permute-start | bytes 393224 | tf_op jit(solution)/shard_map/ppermute | solution.py:288
  6.5 3.9 %collective-permute-start = (bf16[2,1,128,128]{3,2,1,0:T(8,128)(2,1)S(1)}, bf16[2,1,128,128]{3,2,1,0:T(8,128)(2,1)S(1)}, u32[]{:S(2)}, u32[]{:S(2)}) collective-permute-start(bf16[2,1,128,128]{3,2,1,0:T(8,128)(2,1)S(1)} %slice.6), channel_id=1, source_target_pairs={{0,1},{1,2},{2,3},{3,4},{4,5},{5,6},{6,7},{7,8},{8,9},{9,10},{10,1... | collective-permute-start | bytes 196616 | tf_op jit(solution)/shard_map/ppermute | solution.py:287
  10.4 10.5 %collective-permute-start.3 = (bf16[2,3,128,128]{3,2,1,0:T(8,128)(2,1)S(1)}, bf16[2,3,128,128]{3,2,1,0:T(8,128)(2,1)S(1)}, u32[]{:S(2)}, u32[]{:S(2)}) collective-permute-start(bf16[2,3,128,128]{3,2,1,0:T(8,128)(2,1)S(1)} %pad_maximum_fusion), channel_id=1, source_target_pairs={{0,32},{32,64},{64,96},{96,128},{128,160},{160,192},{192,224},{1,3... | collective-permute-start | bytes 589832 | tf_op jit(solution)/shard_map/ppermute | solution.py:279
  16.8 4.8 %copy-start.13 = (f32[128]{0:T(128)S(1)}, f32[128]{0:T(128)}, u32[]{:S(2)}) copy-start(f32[128]{0:T(128)} %param.14) | copy-start | bytes 1540
  22.5 9.6 %copy-start = (bf16[3,3,3,128,256]{4,3,2,1,0:T(8,128)(2,1)S(1)}, bf16[3,3,3,128,256]{4,3,2,1,0:T(8,128)(2,1)}, u32[]{:S(2)}) copy-start(bf16[3,3,3,128,256]{4,3,2,1,0:T(8,128)(2,1)} %down.3) | copy-start | bytes 5308420
  22.5 9.6 %copy-start.5 = (f32[256]{0:T(256)S(1)}, f32[256]{0:T(256)}, u32[]{:S(2)}) copy-start(f32[256]{0:T(256)} %param.16) | copy-start | bytes 3076
  29.4 9.5 %copy-start.6 = (f32[256]{0:T(256)S(1)}, f32[256]{0:T(256)}, u32[]{:S(2)}) copy-start(f32[256]{0:T(256)} %param.17) | copy-start | bytes 3076
  29.4 9.5 %collective-permute-start.4 = (bf16[2,256,256]{2,1,0:T(8,128)(2,1)}, bf16[2,256,256]{2,1,0:T(8,128)(2,1)S(1)}, u32[]{:S(2)}, u32[]{:S(2)}) collective-permute-start(bf16[2,256,256]{2,1,0:T(8,128)(2,1)} %get-tuple-element.28), channel_id=1, source_target_pairs={{0,32},{32,64},{64,96},{96,128},{128,160},{160,192},{192,224},{1,3... | collective-permute-start | bytes 786440 | tf_op jit(solution)/shard_map/ppermute | solution.py:279
  32.1 46.8 %copy-start.1 = (bf16[256,256]{1,0:T(8,128)(2,1)S(1)}, bf16[256,256]{1,0:T(8,128)(2,1)}, u32[]{:S(2)}) copy-start(bf16[256,256]{1,0:T(8,128)(2,1)} %refs_5_.1) | copy-start | bytes 393220
  32.1 46.8 %copy-start.2 = (bf16[256,256]{1,0:T(8,128)(2,1)S(1)}, bf16[256,256]{1,0:T(8,128)(2,1)}, u32[]{:S(2)}) copy-start(bf16[256,256]{1,0:T(8,128)(2,1)} %refs_6_.7) | copy-start | bytes 393220
  32.1 46.8 %copy-start.11 = (bf16[256,256]{1,0:T(8,128)(2,1)S(1)}, bf16[256,256]{1,0:T(8,128)(2,1)}, u32[]{:S(2)}) copy-start(bf16[256,256]{1,0:T(8,128)(2,1)} %query_weight.1) | copy-start | bytes 393220
  39.2 12.8 %collective-permute-start.5 = (bf16[256,256]{1,0:T(8,128)(2,1)S(1)}, bf16[256,256]{1,0:T(8,128)(2,1)S(1)}, u32[]{:S(2)}, u32[]{:S(2)}) collective-permute-start(bf16[256,256]{1,0:T(8,128)(2,1)S(1)} %get-tuple-element.31), channel_id=1, source_target_pairs={{0,2},{1,3},{2,0},{3,1},{4,6},{5,7},{6,4},{7,5},{8,10},{9,11},{10,... | collective-permute-start | bytes 393224 | tf_op jit(solution)/shard_map/ppermute | solution.py:285
  52.0 14.2 %collective-permute-start.7 = (bf16[512,256]{1,0:T(8,128)(2,1)S(1)}, bf16[512,256]{1,0:T(8,128)(2,1)S(1)}, u32[]{:S(2)}, u32[]{:S(2)}) collective-permute-start(bf16[512,256]{1,0:T(8,128)(2,1)S(1)} %constant_dynamic-update-slice_fusion.own), channel_id=1, source_target_pairs={{0,4},{1,5},{2,6},{3,7},{4,8},{5,9},{6,10},{7,11},{8,12},{9,13},{1... | collective-permute-start | bytes 786440 | tf_op jit(solution)/shard_map/ppermute | solution.py:282
  54.7 11.6 %collective-permute-start.8 = (bf16[512,256]{1,0:T(8,128)(2,1)S(1)}, bf16[512,256]{1,0:T(8,128)(2,1)S(1)}, u32[]{:S(2)}, u32[]{:S(2)}) collective-permute-start(bf16[512,256]{1,0:T(8,128)(2,1)S(1)} %constant_dynamic-update-slice_fusion.own), channel_id=1, source_target_pairs={{0,28},{1,29},{2,30},{3,31},{4,0},{5,1},{6,2},{7,3},{8,4},{9,5},{1... | collective-permute-start | bytes 786440 | tf_op jit(solution)/shard_map/ppermute | solution.py:282
  66.3 9.4 %collective-permute-start.9 = (bf16[512,256]{1,0:T(8,128)(2,1)S(1)}, bf16[512,256]{1,0:T(8,128)(2,1)S(1)}, u32[]{:S(2)}, u32[]{:S(2)}) collective-permute-start(bf16[512,256]{1,0:T(8,128)(2,1)S(1)} %collective-permute-done.7.refs_4_), channel_id=1, source_target_pairs={{0,4},{1,5},{2,6},{3,7},{4,8},{5,9},{6,10},{7,11},{8,12},{9,13},{1... | collective-permute-start | bytes 786440 | tf_op jit(solution)/shard_map/ppermute | solution.py:282
  66.3 9.4 %collective-permute-start.10 = (bf16[512,256]{1,0:T(8,128)(2,1)S(1)}, bf16[512,256]{1,0:T(8,128)(2,1)S(1)}, u32[]{:S(2)}, u32[]{:S(2)}) collective-permute-start(bf16[512,256]{1,0:T(8,128)(2,1)S(1)} %collective-permute-done.8.refs_5_), channel_id=1, source_target_pairs={{0,28},{1,29},{2,30},{3,31},{4,0},{5,1},{6,2},{7,3},{8,4},{9,5},{1... | collective-permute-start | bytes 786440 | tf_op jit(solution)/shard_map/ppermute | solution.py:282
  69.5 9.4 %collective-permute-start.6 = (bf16[512,256]{1,0:T(8,128)(2,1)S(1)}, bf16[512,256]{1,0:T(8,128)(2,1)S(1)}, u32[]{:S(2)}, u32[]{:S(2)}) collective-permute-start(bf16[512,256]{1,0:T(8,128)(2,1)S(1)} %constant_dynamic-update-slice_fusion.own), channel_id=1, source_target_pairs={{0,1},{1,0},{2,3},{3,2},{4,5},{5,4},{6,7},{7,6},{8,9},{9,8},{10,11... | collective-permute-start | bytes 786440 | tf_op jit(solution)/shard_map/ppermute | solution.py:285
  75.7 8.6 %collective-permute-start.11 = (bf16[512,256]{1,0:T(8,128)(2,1)S(1)}, bf16[512,256]{1,0:T(8,128)(2,1)S(1)}, u32[]{:S(2)}, u32[]{:S(2)}) collective-permute-start(bf16[512,256]{1,0:T(8,128)(2,1)S(1)} %collective-permute-done.9.refs_4_), channel_id=1, source_target_pairs={{0,4},{1,5},{2,6},{3,7},{4,8},{5,9},{6,10},{7,11},{8,12},{9,13},{1... | collective-permute-start | bytes 786440 | tf_op jit(solution)/shard_map/ppermute | solution.py:282
  75.7 14.2 %collective-permute-start.12 = (bf16[512,256]{1,0:T(8,128)(2,1)S(1)}, bf16[512,256]{1,0:T(8,128)(2,1)S(1)}, u32[]{:S(2)}, u32[]{:S(2)}) collective-permute-start(bf16[512,256]{1,0:T(8,128)(2,1)S(1)} %collective-permute-done.10.refs_5_), channel_id=1, source_target_pairs={{0,28},{1,29},{2,30},{3,31},{4,0},{5,1},{6,2},{7,3},{8,4},{9,5},{1... | collective-permute-start | bytes 786440 | tf_op jit(solution)/shard_map/ppermute | solution.py:282
  84.3 8.4 %collective-permute-start.13 = (bf16[512,256]{1,0:T(8,128)(2,1)S(1)}, bf16[512,256]{1,0:T(8,128)(2,1)S(1)}, u32[]{:S(2)}, u32[]{:S(2)}) collective-permute-start(bf16[512,256]{1,0:T(8,128)(2,1)S(1)} %collective-permute-done.11.refs_4_), channel_id=1, source_target_pairs={{0,4},{1,5},{2,6},{3,7},{4,8},{5,9},{6,10},{7,11},{8,12},{9,13},{1... | collective-permute-start | bytes 786440 | tf_op jit(solution)/shard_map/ppermute | solution.py:282
  94.3 10.2 %copy-start.3 = (bf16[256,256]{1,0:T(8,128)(2,1)S(1)}, bf16[256,256]{1,0:T(8,128)(2,1)}, u32[]{:S(2)}) copy-start(bf16[256,256]{1,0:T(8,128)(2,1)} %weight.5) | copy-start | bytes 393220
  94.3 2.7 %collective-permute-start.14 = (f32[512,512]{1,0:T(8,128)S(1)}, f32[512,512]{1,0:T(8,128)S(1)}, u32[]{:S(2)}, u32[]{:S(2)}) collective-permute-start(f32[512,512]{1,0:T(8,128)S(1)} %get-tuple-element.46), channel_id=1, source_target_pairs={{0,1},{1,0},{2,3},{3,2},{4,5},{5,4},{6,7},{7,6},{8,9},{9,8},{10,11... | collective-permute-start | bytes 3145736 | tf_op jit(solution)/shard_map/ppermute | solution.py:285
  97.3 7.1 %collective-permute-start.15 = (bf16[256,256]{1,0:T(8,128)(2,1)S(1)}, bf16[256,256]{1,0:T(8,128)(2,1)S(1)}, u32[]{:S(2)}, u32[]{:S(2)}) collective-permute-start(bf16[256,256]{1,0:T(8,128)(2,1)S(1)} %get-tuple-element.48), channel_id=1, source_target_pairs={{0,2},{1,3},{2,0},{3,1},{4,6},{5,7},{6,4},{7,5},{8,10},{9,11},{10,... | collective-permute-start | bytes 393224 | tf_op jit(solution)/shard_map/ppermute | solution.py:285
  (6 other events, 9.3 us)

commit v2 on v1

v2 whole, which is shorter than its diff:
```python
import jax
import jax.numpy as jnp
from jax import lax
from jax.experimental import pallas as pl
from jax.experimental.pallas import tpu as pltpu
from jax.sharding import PartitionSpec as P

epsilon = 1e-05
f32 = jnp.float32
bf16 = jnp.bfloat16
VMEM = pl.BlockSpec(memory_space=pltpu.VMEM)
SMEM = pl.BlockSpec(memory_space=pltpu.SMEM)
HBM = pl.BlockSpec(memory_space=pltpu.HBM)
COLS = 128
C1 = 128
C2 = 256
ROWS = 8
HALF = 64
QUERIES = 256


def call(kernel, outs, ins, scratch=(), spaces=None, aliases=None, flops=0, nbytes=0):
    spaces = spaces or {}
    ins = [
        pltpu.with_memory_space_constraint(x, pltpu.HBM) if spaces.get(i) is HBM else x
        for i, x in enumerate(ins)
    ]
    return pl.pallas_call(
        kernel,
        out_shape=[jax.ShapeDtypeStruct(s, d) for s, d in outs],
        in_specs=[spaces.get(i, VMEM) for i in range(len(ins))],
        out_specs=[VMEM] * len(outs),
        scratch_shapes=list(scratch),
        input_output_aliases=aliases or {},
        compiler_params=pltpu.CompilerParams(vmem_limit_bytes=24 * 1024 * 1024),
        cost_estimate=pl.CostEstimate(flops=flops, bytes_accessed=nbytes, transcendentals=0),
    )(*ins)


def dot(a, b):
    return jnp.dot(a, b, preferred_element_type=f32)


def dot_t(a, b):
    return lax.dot_general(a, b, (((1,), (1,)), ((), ())), preferred_element_type=f32)


def averaging():
    i = lax.broadcasted_iota(jnp.int32, (2 * C1, 2 * C1), 0) // C1
    j = lax.broadcasted_iota(jnp.int32, (2 * C1, 2 * C1), 1) // C1
    return jnp.where(i == j, 1.0 / C1, 0.0).astype(bf16)


def activate(pair, gain2, mean_of):
    centred = pair.astype(f32) - dot(pair, mean_of)
    squares = centred * centred
    high = squares.astype(bf16)
    low = (squares - high.astype(f32)).astype(bf16)
    spread = dot(high, mean_of) + dot(low, mean_of)
    y = centred * lax.rsqrt(spread + epsilon) * gain2
    return y / (1.0 + jnp.exp(-y))


def store_shifted(taps, row, act):
    col = lax.broadcasted_iota(jnp.int32, act.shape, 0)
    at = pl.ds(row * COLS, COLS)
    taps[0, at, :] = jnp.where(col == 0, 0.0, pltpu.roll(act, 1, 0)).astype(bf16)
    taps[1, at, :] = act.astype(bf16)
    taps[2, at, :] = jnp.where(col == COLS - 1, 0.0, pltpu.roll(act, COLS - 1, 0)).astype(bf16)


def pair_of(ref, i):
    return jnp.concatenate([ref[0, i], ref[1, i]], axis=1)


def fill_taps(taps, rows, gain_ref):
    gain2 = jnp.concatenate([gain_ref[...], gain_ref[...]], axis=1)
    mean_of = averaging()
    for row, ref, i, factor in rows:
        act = activate(pair_of(ref, i), gain2, mean_of)
        store_shifted(taps, row, act if factor is None else act * factor)


SIZE = (ROWS + 1) * COLS


def conv1_taps(taps, weight, acc, base):
    for kr in range(3):
        tile = jnp.concatenate([taps[kc, kr * COLS : kr * COLS + SIZE, :] for kc in range(3)], axis=1)
        part = dot(tile, weight[kr].reshape(3 * C2, C2))
        acc[...] = (acc[...] if kr else base()) + part


def stack(a, b, c, d):
    return jnp.concatenate([jnp.concatenate([a, b], axis=1), jnp.concatenate([c, d], axis=1)], axis=0)


def edge_kernel(video, bottom, top, sem):
    copies = [
        pltpu.make_async_copy(video.at[:, ROWS - 1 : ROWS], bottom, sem.at[0]),
        pltpu.make_async_copy(video.at[:, 0:2], top, sem.at[1]),
    ]
    for copy in copies:
        copy.start()
    for copy in copies:
        copy.wait()


def blank_edges(taps):
    for row in (0, ROWS + 1, ROWS + 2):
        taps[:, row * COLS : (row + 1) * COLS, :] = jnp.zeros((3, COLS, C2), bf16)


def own_kernel(
    video_h, gain_h, bias_h, conv_h, down_h, query_h, key_h, value_h, output_h, down_bias_h, attention_gain_h,
    acc, now, before, down, query, key, value_t, output, gain, down_bias, attention_gain,
    taps, video, bias, conv, value, sem,
):
    pairs = (
        (gain_h, gain), (video_h, video), (bias_h, bias), (conv_h, conv), (value_h, value), (down_h, down),
        (query_h, query), (key_h, key), (output_h, output),
        (down_bias_h, down_bias), (attention_gain_h, attention_gain),
    )
    copies = [pltpu.make_async_copy(src, dst, sem.at[i]) for i, (src, dst) in enumerate(pairs)]
    for copy in copies:
        copy.start()
    blank_edges(taps)
    for copy in copies[:3]:
        copy.wait()
    fill_taps(taps, [(row + 1, video, row, None) for row in range(ROWS)], gain)
    copies[3].wait()
    none = jnp.zeros((C1, C1), bf16)
    for kr in range(3):
        for kc in range(3):
            w0, w1, w2 = (conv[kt, kr, kc] for kt in range(3))
            now[kr, kc] = stack(w2, w1, none, w2)
            before[kr, kc] = stack(w0, none, w1, w0)

    def base():
        bias2 = jnp.concatenate([bias[...], bias[...]], axis=1)
        rows = [pair_of(video, i).astype(f32) for i in range(ROWS)] + [jnp.zeros((COLS, C2), f32)]
        return jnp.concatenate(rows, axis=0) + bias2

    conv1_taps(taps, now, acc, base)
    copies[4].wait()
    value_t[...] = value[...].astype(f32).T.astype(bf16)
    for copy in copies[5:]:
        copy.wait()


def halo_kernel(flags, acc_in, halo, gain, weight, acc, taps):
    blank_edges(taps)
    fill_taps(taps, [(row + 1, halo, row, flags[0]) for row in range(ROWS)], gain)
    conv1_taps(taps, weight, acc, lambda: acc_in[...])


def sum_kernel(
    flags, acc_in, above, below, far_above, far_below, gain, now, before, down,
    send, half_taps, acc, taps, far_taps, wide,
):
    past = flags[0]
    edges = [(0, above, 0, flags[1]), (1, below, 0, flags[2]), (2, below, 1, flags[2])]
    fill_taps(taps, edges, gain)
    edges = [(0, far_above, 0, flags[1]), (1, far_below, 0, flags[2]), (2, far_below, 1, flags[2])]
    fill_taps(far_taps, [(row, ref, i, factor * past) for row, ref, i, factor in edges], gain)

    def add(kr, taps_row, count, row):
        tile = jnp.concatenate(
            [
                source[kc, taps_row * COLS : (taps_row + count) * COLS, :]
                for source in (taps, far_taps)
                for kc in range(3)
            ],
            axis=1,
        )
        weight = jnp.concatenate([now[kr].reshape(3 * C2, C2), before[kr].reshape(3 * C2, C2)], axis=0)
        at = pl.ds(row * COLS, count * COLS)
        acc[at, :] += dot(tile, weight)

    acc[...] = acc_in[...]
    acc[pl.ds(ROWS * COLS, COLS), :] += pair_of(below, 0).astype(f32)
    add(0, 0, 1, 0)
    add(1, 1, 1, ROWS)
    add(2, 1, 2, ROWS - 1)
    for row in range(ROWS + 1):
        at = pl.ds(row * COLS, COLS)
        summed = acc[at, :].astype(bf16).astype(f32)
        if row == ROWS:
            summed = summed * flags[2]
        wide[0, at, :] = summed[:, :C1]
        wide[1, at, :] = summed[:, C1:]
    j = lax.broadcasted_iota(jnp.int32, (HALF, C1), 0)
    for row in range(ROWS + 1):
        place = row // 2 if row % 2 == 0 else 5 + row // 2
        for frame in range(2):
            even = wide[frame, pl.ds(row * COLS, HALF, stride=2), :]
            odd = wide[frame, pl.ds(row * COLS + 1, HALF, stride=2), :]
            after = jnp.where(j == HALF - 1, 0.0, pltpu.roll(even, HALF - 1, 0))
            lanes = pl.ds(frame * C1, C1)
            at = pl.ds(place * HALF, HALF)
            half_taps[0, at, lanes] = even.astype(bf16)
            half_taps[1, at, lanes] = odd.astype(bf16)
            half_taps[2, at, lanes] = after.astype(bf16)
    first = jnp.zeros((QUERIES, C2), f32)
    second = jnp.zeros((QUERIES, C2), f32)
    for kr in range(3):
        start = (0, 5 * HALF, HALF)[kr]
        for kc in range(3):
            tile = half_taps[kc, start : start + QUERIES, :]
            first += dot(tile, jnp.concatenate([down[0, kr, kc], down[1, kr, kc]], axis=0))
            second += dot(tile[:, C1:], down[0, kr, kc])
    send[0] = first.astype(bf16)
    send[1] = second.astype(bf16)


def down_kernel(half_taps, down, bias, out):
    first = jnp.zeros((QUERIES, C2), f32) + bias[...]
    second = jnp.zeros((QUERIES, C2), f32) + bias[...]
    for kr in range(3):
        start = (0, 5 * HALF, HALF)[kr]
        for kc in range(3):
            tile = half_taps[kc, start : start + QUERIES, :]
            first += dot(tile[:, :C1], down[2, kr, kc])
            second += dot(tile, jnp.concatenate([down[1, kr, kc], down[2, kr, kc]], axis=0))
    out[0] = first
    out[1] = second


def norm_kernel(flags, part, received, gain, reduced, normed):
    for frame in range(2):
        value = part[frame] + received[frame].astype(f32) * flags[0]
        reduced[frame] = value
        centred = value - jnp.mean(value, axis=1, keepdims=True)
        spread = jnp.mean(centred * centred, axis=1, keepdims=True)
        normed[frame] = (centred * lax.rsqrt(spread + epsilon) * gain[...]).astype(bf16)


GROUPS = 4
STATE = C2 + 16


def attend(queries, before, outs, blocks, key_weight, value_weight_t, groups=range(4)):
    normed = jnp.concatenate([block[...] for block in blocks], axis=0)
    keys = dot(normed, key_weight[...]).astype(bf16)
    values = dot_t(value_weight_t[...], normed).astype(bf16)
    values = jnp.concatenate([values, jnp.ones((16, values.shape[1]), bf16)], axis=0)
    ahead = dot_t(keys, queries[groups[0]])
    for i, group in enumerate(groups):
        scores = ahead
        if i + 1 < len(groups):
            ahead = dot_t(keys, queries[groups[i + 1]])
        highest = jnp.max(scores, axis=0, keepdims=True)
        if before is not None:
            old = before[group, C2 + 8 : C2 + 9, :]
            highest = jnp.maximum(old, highest)
            rescale = jnp.exp(old - highest)
        weights = jnp.exp(scores - highest).astype(bf16)
        product = dot(values, weights)[: C2 + 8]
        if before is not None:
            product += before[group, : C2 + 8, :] * rescale
        out, place = outs(group)
        out[place, : C2 + 8, :] = product
        out[place, C2 + 8 :, :] = jnp.broadcast_to(highest, (8, C2))


def query_kernel(normed, weight, queries):
    for frame in range(2):
        queries[frame] = (dot(normed[frame], weight[...]).astype(bf16) * (C2**-0.5)).astype(bf16)


def first_attend_kernel(
    frame, own, sibling, across, both, block, plus, minus, key_weight, value_weight_t, queries, state
):
    for group, source in enumerate((own, sibling, across, both)):
        queries[group] = source[frame]
    blocks = [ref.at[frame] for ref in (block, plus, minus)]
    attend(queries, None, lambda g: (state, g), blocks, key_weight, value_weight_t)


def attend_kernel(frame, queries, before, plus, minus, key_weight, value_weight_t, state):
    blocks = [ref.at[frame] for ref in (plus, minus)]
    attend(queries, before, lambda g: (state, g), blocks, key_weight, value_weight_t)


def cut_kernel(plus, minus, first, second):
    first[...] = plus[0]
    second[...] = minus[1]


def last_attend_kernel(groups, *refs):
    queries, before, blocks = refs[0:2], refs[2:4], refs[4:6]
    key_weight, value_weight_t, mine, theirs = refs[6:]
    for frame in range(2):
        attend(
            queries[frame],
            before[frame],
            lambda g: (mine if g == groups[0] else theirs, frame),
            (blocks[frame],),
            key_weight,
            value_weight_t,
            groups,
        )


def split3(x):
    high = x.astype(bf16).astype(f32)
    middle = (x - high).astype(bf16).astype(f32)
    return [high, middle, x - high - middle]


def merged(mine, theirs, frame):
    top_a, top_b = mine[frame, C2 + 8 :, :], theirs[frame, C2 + 8 :, :]
    top = jnp.maximum(top_a, top_b)
    scale_a, scale_b = jnp.exp(top_a - top), jnp.exp(top_b - top)
    mass = mine[frame, C2 : C2 + 8, :] * scale_a + theirs[frame, C2 : C2 + 8, :] * scale_b
    return mass, top, scale_a, scale_b


def merge_keep_kernel(mine, theirs, state):
    for frame in range(2):
        mass, top, scale_a, scale_b = merged(mine, theirs, frame)
        state[frame, :C2, :] = mine[frame, :C2, :] * scale_a[:1] + theirs[frame, :C2, :] * scale_b[:1]
        state[frame, C2 : C2 + 8, :] = mass
        state[frame, C2 + 8 :, :] = top


def merge_send_kernel(mine, theirs, send):
    for frame in range(2):
        mass, top, scale_a, scale_b = merged(mine, theirs, frame)
        inverse = 1.0 / mass
        scale_a, scale_b = scale_a * inverse, scale_b * inverse
        total = mine[frame, :C2, :] * scale_a[:1] + theirs[frame, :C2, :] * scale_b[:1]
        send[frame, :C2, :] = total.astype(bf16)
        rows = split3(top[:1]) + split3(mass[:1]) + [jnp.zeros((10, C2), f32)]
        send[frame, C2:, :] = jnp.concatenate(rows, axis=0).astype(bf16)


def last_kernel(reduced, state, received, weight, out):
    for frame in range(2):
        rows = received[frame, C2:, :].astype(f32)
        top_a, mass_a = state[frame, C2 + 8 : C2 + 9, :], state[frame, C2 : C2 + 1, :]
        top_b = rows[0:1] + rows[1:2] + rows[2:3]
        mass_b = rows[3:4] + rows[4:5] + rows[5:6]
        top = jnp.maximum(top_a, top_b)
        scale_a = jnp.exp(top_a - top)
        scale_b = jnp.exp(top_b - top) * mass_b
        inverse = 1.0 / (mass_a * scale_a + scale_b)
        attended = state[frame, :C2, :] * (scale_a * inverse)
        attended += received[frame, :C2, :].astype(f32) * (scale_b * inverse)
        mixed = lax.dot_general(
            attended.astype(bf16), weight[...], (((0,), (0,)), ((), ())), preferred_element_type=f32
        )
        out[frame] = reduced[frame] + mixed


def body(
    video,
    norm_gain,
    conv_weight,
    conv_bias,
    down_weight,
    down_bias,
    attention_gain,
    query_weight,
    key_weight,
    value_weight,
    output_weight,
):
    space = lax.axis_size("space")
    times = lax.axis_size("tm")
    place = lax.axis_index("space")
    has = [lax.axis_index("tm") > 0, place > 0, place < space - 1]
    flags = jnp.stack(has).astype(f32)
    scalar = {0: SMEM}

    def next_frames(x):
        return lax.ppermute(x, "tm", [(i, (i + 1) % times) for i in range(times)])

    def along(x, distance):
        return lax.ppermute(x, "space", [(i, (i + distance) % space) for i in range(space)])

    def diagonal(x, distance):
        route = [
            (t * space + i, ((t + 1) % times) * space + (i + distance) % space)
            for t in range(times)
            for i in range(space)
        ]
        return lax.ppermute(x, ("tm", "space"), route)

    def swap(x, bit):
        return lax.ppermute(x, "space", [(i, i ^ bit) for i in range(space)])

    bottom, top = call(
        edge_kernel,
        [((2, 1, COLS, C1), bf16), ((2, 2, COLS, C1), bf16)],
        [video],
        [pltpu.SemaphoreType.DMA((2,))],
        {0: HBM},
        nbytes=400_000,
    )
    above = along(bottom, 1)
    below = along(top, -1)
    halo = next_frames(video)
    far_above, far_below = diagonal(bottom, 1), diagonal(top, -1)

    square = (C2, C2)
    taps = pltpu.VMEM((3, (ROWS + 3) * COLS, C2), bf16)
    whole = ((SIZE, C2), f32)
    prepared = (3, 3) + square
    (
        acc, now, before, down_weight, query_weight, key_weight, value_weight, output_weight,
        gain, down_bias, attention_gain,
    ) = call(
        own_kernel,
        [whole, (prepared, bf16), (prepared, bf16), (down_weight.shape, bf16)]
        + [(square, bf16)] * 4
        + [((1, C1), f32), ((1, C2), f32), ((1, C2), f32)],
        [video, norm_gain.reshape(1, C1), conv_bias.reshape(1, C1), conv_weight, down_weight]
        + [query_weight, key_weight, value_weight, output_weight]
        + [down_bias.reshape(1, C2), attention_gain.reshape(1, C2)],
        [
            taps,
            pltpu.VMEM(video.shape, bf16),
            pltpu.VMEM((1, C1), f32),
            pltpu.VMEM(conv_weight.shape, bf16),
            pltpu.VMEM(square, bf16),
            pltpu.SemaphoreType.DMA((11,)),
        ],
        {i: HBM for i in range(11)},
        flops=2 * 9 * SIZE * 256 * 256,
        nbytes=6_000_000,
    )
    (acc,) = call(
        halo_kernel,
        [whole],
        [flags, acc, halo, gain, before],
        [taps],
        scalar,
        flops=2 * 9 * SIZE * 256 * 256,
        nbytes=5_000_000,
    )
    send, half_taps = call(
        sum_kernel,
        [((2, QUERIES, C2), bf16), ((3, 9 * HALF, C2), bf16)],
        [flags, acc, above, below, far_above, far_below, gain, now, before, down_weight],
        [pltpu.VMEM(*whole)] + [pltpu.VMEM((3, 3 * COLS, C2), bf16)] * 2 + [pltpu.VMEM((2, SIZE, C1), f32)],
        scalar,
        flops=2 * 18 * 256 * 256 * 256,
        nbytes=5_000_000,
    )
    received = next_frames(send)
    (part,) = call(
        down_kernel,
        [((2, QUERIES, C2), f32)],
        [half_taps, down_weight, down_bias],
        flops=2 * 18 * 256 * 256 * 256,
        nbytes=3_000_000,
    )
    pixels = ((2, QUERIES, C2), bf16)
    reduced, normed = call(
        norm_kernel,
        [((2, QUERIES, C2), f32), pixels],
        [flags, part, received, attention_gain],
        spaces=scalar,
        nbytes=2_000_000,
    )
    plus, minus = [along(normed, 4)], [along(normed, -4)]
    (own,) = call(query_kernel, [pixels], [normed, query_weight], nbytes=600_000)
    for step in range(2):
        plus.append(along(plus[step], 4))
        minus.append(along(minus[step], -4))
    given, _ = lax.optimization_barrier((own, plus[0]))
    sibling, across = swap(given, 1), swap(given, 2)
    both = swap(across, 1)
    state = [((GROUPS, STATE, C2), f32)]
    flops = 2 * QUERIES * 256 * (512 + 2 * GROUPS * QUERIES)
    carry, queries = [0, 0], [0, 0]
    weights = [key_weight, value_weight]
    for frame in range(2):
        queries[frame], carry[frame] = call(
            lambda *refs: first_attend_kernel(frame, *refs),
            [((GROUPS, QUERIES, C2), bf16)] + state,
            [own, sibling, across, both, normed, plus[0], minus[0]] + weights,
            flops=3 * flops,
            nbytes=4_000_000,
        )
    (plus[2], minus[2]), carry = lax.optimization_barrier(((plus[2], minus[2]), carry))
    ends = call(cut_kernel, [((QUERIES, C2), bf16)] * 2, [plus[2], minus[2]], nbytes=500_000)
    ends = [along(ends[0], 4), along(ends[1], -4)]
    for step in range(1, 3):
        for frame in range(2):
            (carry[frame],) = call(
                lambda *refs: attend_kernel(frame, *refs),
                state,
                [queries[frame], carry[frame], plus[step], minus[step]] + weights,
                aliases={1: 0},
                flops=2 * flops,
                nbytes=4_000_000,
            )
    pair = ((2, STATE, C2), f32)

    def finish(groups):
        mine, theirs = call(
            lambda *refs: last_attend_kernel(groups, *refs),
            [pair, pair],
            [*queries, *carry, *ends] + weights,
            flops=flops,
            nbytes=4_000_000,
        )
        return mine, swap(theirs, 1)

    (give,) = call(
        merge_send_kernel, [((2, STATE, C2), bf16)], list(finish((2, 3))), nbytes=1_500_000
    )
    received = swap(give, 2)
    (kept,) = call(merge_keep_kernel, [pair], list(finish((0, 1))), nbytes=2_000_000)
    (encoded,) = call(
        last_kernel,
        [((2, QUERIES, C2), f32)],
        [reduced, kept, received, output_weight],
        nbytes=2_000_000,
    )
    return encoded.reshape(2, ROWS // 2, HALF, C2)


def solution(mesh):
    in_specs = (P("tm", "space", None, None), P(), P(), P(), P(), P(), P(), P(), P(), P(), P())
    out_specs = P("tm", "space", None, None)
    return jax.shard_map(body, mesh=mesh, in_specs=in_specs, out_specs=out_specs, check_vma=False)
```

time: 106 us -> 89.2 us (0.84)
  the two profiles are of different devices: /device:TPU:8 before, /device:TPU:1 now
where the time goes in v2:
time: 89.2 us
  starting transfers between devices  43.3 us (49%)
  Pallas kernels  26 us (29%)
  waiting for transfers between devices  19.6 us (22%)
    pallas_call x19, Pallas kernels, call(): pl.pallas_call(kernel, out_shape=[jax.ShapeDtypeStruct(s, d) for s, d in...  26 us
    ppermute x6, starting transfers between devices, swap(): return lax.ppermute(x, 'space', [(i, i ^ bit) for i in range(space)])  17.5 us
    ppermute x10, starting transfers between devices, along(): lax.ppermute(x, 'space', [(i, (i + distance) % space) for i in range(spac...  14.6 us
    ppermute x2, starting transfers between devices, diagonal(): return lax.ppermute(x, ('tm', 'space'), route)  7.78 us
    ppermute x6, waiting for transfers between devices, swap(): return lax.ppermute(x, 'space', [(i, i ^ bit) for i in range(space)])  7.6 us
    ppermute x2, waiting for transfers between devices, next_frames(): return lax.ppermute(x, 'tm', [(i, (i + 1) % times) for i in range(times)])  5.41 us
    ppermute x10, waiting for transfers between devices, along(): lax.ppermute(x, 'space', [(i, (i + distance) % space) for i in range(spac...  3.85 us
    ppermute x2, starting transfers between devices, next_frames(): return lax.ppermute(x, 'tm', [(i, (i + 1) % times) for i in range(times)])  3.46 us
  transfers between devices with their start and end apart: 20, of which 6 were waited for; matrix products, arithmetic and copies ran while one was open for 0% of the time, Pallas kernels for 22%

profile of v2, /device:TPU:1, one launch (start us, length us, event | category | flops | bytes accessed | tf_op | source)
XLA Modules:
  0.0 89.2 jit_solution(474242553991092853)
XLA Ops:
  0.0 2.0 %collective-permute-start = (bf16[2,8,128,128]{3,2,1,0:T(8,128)(2,1)}, bf16[2,8,128,128]{3,2,1,0:T(8,128)(2,1)S(1)}, u32[]{:S(2)}, u32[]{:S(2)}) collective-permute-start(bf16[2,8,128,128]{3,2,1,0:T(8,128)(2,1)} %video.1), channel_id=1, source_target_pairs={{0,32},{32,64},{64,96},{96,128},{128,160},{160,192},{192,224},{224... | collective-permute-start | bytes 1572872 | tf_op jit(solution)/shard_map/ppermute | solution.py:377
  4.3 7.8 %collective-permute-start.4 = (bf16[2,2,128,128]{3,2,1,0:T(8,128)(2,1)S(1)}, bf16[2,2,128,128]{3,2,1,0:T(8,128)(2,1)S(1)}, u32[]{:S(2)}, u32[]{:S(2)}) collective-permute-start(bf16[2,2,128,128]{3,2,1,0:T(8,128)(2,1)S(1)} %get-tuple-element.41), channel_id=1, source_target_pairs={{0,63},{1,32},{2,33},{3,34},{4,35},{5,36},{6,37},{7,38},{8,39},{9,... | collective-permute-start | bytes 393224 | tf_op jit(solution)/shard_map/ppermute | solution.py:388
  12.1 4.2 %shard_map.109 = (f32[1152,256]{1,0:T(8,128)S(1)}, bf16[3,3,256,256]{3,2,1,0:T(8,128)(2,1)S(1)}, bf16[3,3,256,256]{3,2,1,0:T(8,128)(2,1)S(1)}, bf16[3,3,3,128,25...) custom-call(bf16[2,8,128,128]{3,2,1,0:T(8,128)(2,1)} %video.1, ...), custom_call_target="tpu_custom_call" | custom-call | flops 1358954496 | bytes 6000000 | tf_op jit(solution)/shard_map/pallas_call | solution.py:28
  16.4 3.1 %shard_map.110.acc_in = f32[1152,256]{1,0:T(8,128)S(1)} custom-call(f32[3]{0:T(128)S(1)} %add_convert_fusion.flags, f32[1152,256]{1,0:T(8,128)S(1)} %get-tuple-element.37.acc_in, bf16[2,8,128,128]{3,2,1,0:T(8,128)(2,1)S(1)} %collective-permute-done.halo, f32[1,128]{1,0:T(1,128)S(1)} %get-tuple-element.38.gain, ...), custom_call_target="tpu_custom_call" | custom-call | flops 1358954496 | bytes 5000000 | tf_op jit(solution)/shard_map/pallas_call | solution.py:28
  19.5 2.7 %collective-permute-done.3.far_above = bf16[2,1,128,128]{3,2,1,0:T(8,128)(2,1)S(1)} collective-permute-done((bf16[2,1,128,128]{3,2,1,0:T(8,128)(2,1)S(1)}, bf16[2,1,128,128]{3,2,1,0:T(8,128)(2,1)S(1)}, u32[]{:S(2)}, u32[]{:S(2)}) %collective-permute-start.3) | collective-permute-done | bytes 65568 | tf_op jit(solution)/shard_map/ppermute | solution.py:388
  22.2 3.2 %shard_map.112 = (bf16[2,256,256]{2,1,0:T(8,128)(2,1)S(1)}, bf16[3,576,256]{2,1,0:T(8,128)(2,1)S(1)}) custom-call(f32[3]{0:T(128)S(1)} %add_convert_fusion.flags, f32[1152,256]{1,0:T(8,128)S(1)} %shard_map.110.acc_in, bf16[2,1,128,128]{3,2,1,0:T(8,128)(2,1)S(1)} %collective-permute-done.1.above, bf16[2,2,128,128]{3,2,1,0:T(8,128)(2,1)S(1)} %collective-permute-done.2.below, ...), custom_call_target="tpu_custom_call" | custom-call | flops 603979776 | bytes 5000000 | tf_op jit(solution)/shard_map/pallas_call | solution.py:28
  25.5 1.4 %collective-permute-start.5 = (bf16[2,256,256]{2,1,0:T(8,128)(2,1)S(1)}, bf16[2,256,256]{2,1,0:T(8,128)(2,1)S(1)}, u32[]{:S(2)}, u32[]{:S(2)}) collective-permute-start(bf16[2,256,256]{2,1,0:T(8,128)(2,1)S(1)} %get-tuple-element.46), channel_id=1, source_target_pairs={{0,32},{32,64},{64,96},{96,128},{128,160},{160,192},{192,224},{224... | collective-permute-start | bytes 786440 | tf_op jit(solution)/shard_map/ppermute | solution.py:377
  27.7 5.4 %collective-permute-done.5.received = bf16[2,256,256]{2,1,0:T(8,128)(2,1)S(1)} collective-permute-done((bf16[2,256,256]{2,1,0:T(8,128)(2,1)S(1)}, bf16[2,256,256]{2,1,0:T(8,128)(2,1)S(1)}, u32[]{:S(2)}, u32[]{:S(2)}) %collective-permute-start.5) | collective-permute-done | bytes 262176 | tf_op jit(solution)/shard_map/ppermute | solution.py:377
  35.0 3.8 %collective-permute-start.10 = (bf16[2,256,256]{2,1,0:T(8,128)(2,1)S(1)}, bf16[2,256,256]{2,1,0:T(8,128)(2,1)S(1)}, u32[]{:S(2)}, u32[]{:S(2)}) collective-permute-start(bf16[2,256,256]{2,1,0:T(8,128)(2,1)S(1)} %get-tuple-element.49.normed.refs_4_), channel_id=1, source_target_pairs={{0,28},{1,29},{2,30},{3,31},{4,0},{5,1},{6,2},{7,3},{8,4},{9,5},{1... | collective-permute-start | bytes 786440 | tf_op jit(solution)/shard_map/ppermute | solution.py:380
  39.0 3.4 %collective-permute-done.6.refs_5_ = bf16[2,256,256]{2,1,0:T(8,128)(2,1)S(1)} collective-permute-done((bf16[2,256,256]{2,1,0:T(8,128)(2,1)S(1)}, bf16[2,256,256]{2,1,0:T(8,128)(2,1)S(1)}, u32[]{:S(2)}, u32[]{:S(2)}) %collective-permute-start.6) | collective-permute-done | bytes 262176 | tf_op jit(solution)/shard_map/ppermute | solution.py:380
  42.5 5.2 %collective-permute-start.8 = (bf16[2,256,256]{2,1,0:T(8,128)(2,1)S(1)}, bf16[2,256,256]{2,1,0:T(8,128)(2,1)S(1)}, u32[]{:S(2)}, u32[]{:S(2)}) collective-permute-start(bf16[2,256,256]{2,1,0:T(8,128)(2,1)S(1)} %shard_map.115.refs_0_), channel_id=1, source_target_pairs={{0,2},{1,3},{2,0},{3,1},{4,6},{5,7},{6,4},{7,5},{8,10},{9,11},{10,... | collective-permute-start | bytes 786440 | tf_op jit(solution)/shard_map/ppermute | solution.py:391
  47.6 2.7 %collective-permute-start.13 = (bf16[2,256,256]{2,1,0:T(8,128)(2,1)S(1)}, bf16[2,256,256]{2,1,0:T(8,128)(2,1)S(1)}, u32[]{:S(2)}, u32[]{:S(2)}) collective-permute-start(bf16[2,256,256]{2,1,0:T(8,128)(2,1)S(1)} %collective-permute-done.10.refs_6_), channel_id=1, source_target_pairs={{0,28},{1,29},{2,30},{3,31},{4,0},{5,1},{6,2},{7,3},{8,4},{9,5},{1... | collective-permute-start | bytes 786440 | tf_op jit(solution)/shard_map/ppermute | solution.py:380
  50.3 3.9 %collective-permute-start.7 = (bf16[2,256,256]{2,1,0:T(8,128)(2,1)S(1)}, bf16[2,256,256]{2,1,0:T(8,128)(2,1)S(1)}, u32[]{:S(2)}, u32[]{:S(2)}) collective-permute-start(bf16[2,256,256]{2,1,0:T(8,128)(2,1)S(1)} %shard_map.115.refs_0_), channel_id=1, source_target_pairs={{0,1},{1,0},{2,3},{3,2},{4,5},{5,4},{6,7},{7,6},{8,9},{9,8},{10,11... | collective-permute-start | bytes 786440 | tf_op jit(solution)/shard_map/ppermute | solution.py:391
  55.4 2.7 %collective-permute-start.14 = (bf16[2,256,256]{2,1,0:T(8,128)(2,1)S(1)}, bf16[2,256,256]{2,1,0:T(8,128)(2,1)S(1)}, u32[]{:S(2)}, u32[]{:S(2)}) collective-permute-start(bf16[2,256,256]{2,1,0:T(8,128)(2,1)S(1)} %collective-permute-done.13.refs_3_), channel_id=1, source_target_pairs={{0,28},{1,29},{2,30},{3,31},{4,0},{5,1},{6,2},{7,3},{8,4},{9,5},{1... | collective-permute-start | bytes 786440 | tf_op jit(solution)/shard_map/ppermute | solution.py:380
  58.0 1.7 %shard_map.117 = (bf16[4,256,256]{2,1,0:T(8,128)(2,1)S(1)}, f32[4,272,256]{2,1,0:T(8,128)S(1)}) custom-call(bf16[2,256,256]{2,1,0:T(8,128)(2,1)S(1)} %shard_map.115.refs_0_, bf16[2,256,256]{2,1,0:T(8,128)(2,1)S(1)} %collective-permute-done.7.refs_1_, bf16[2,256,256]{2,1,0:T(8,128)(2,1)S(1)} %collective-permute-done.8.refs_2_, ...), custom_call_target="tpu_custom_call" | custom-call | flops 1006632960 | bytes 4000000 | tf_op jit(solution)/shard_map/pallas_call | solution.py:28
  59.7 1.7 %shard_map.116 = (bf16[4,256,256]{2,1,0:T(8,128)(2,1)S(1)}, f32[4,272,256]{2,1,0:T(8,128)S(1)}) custom-call(bf16[2,256,256]{2,1,0:T(8,128)(2,1)S(1)} %shard_map.115.refs_0_, bf16[2,256,256]{2,1,0:T(8,128)(2,1)S(1)} %collective-permute-done.7.refs_1_, bf16[2,256,256]{2,1,0:T(8,128)(2,1)S(1)} %collective-permute-done.8.refs_2_, ...), custom_call_target="tpu_custom_call" | custom-call | flops 1006632960 | bytes 4000000 | tf_op jit(solution)/shard_map/pallas_call | solution.py:28
  61.9 3.0 %collective-permute-start.16 = (bf16[256,256]{1,0:T(8,128)(2,1)S(1)}, bf16[256,256]{1,0:T(8,128)(2,1)S(1)}, u32[]{:S(2)}, u32[]{:S(2)}) collective-permute-start(bf16[256,256]{1,0:T(8,128)(2,1)S(1)} %get-tuple-element.63), channel_id=1, source_target_pairs={{0,28},{1,29},{2,30},{3,31},{4,0},{5,1},{6,2},{7,3},{8,4},{9,5},{1... | collective-permute-start | bytes 393224 | tf_op jit(solution)/shard_map/ppermute | solution.py:380
  64.9 1.5 %shard_map.120.refs_1_ = f32[4,272,256]{2,1,0:T(8,128)S(1)} custom-call(bf16[4,256,256]{2,1,0:T(8,128)(2,1)S(1)} %get-tuple-element.55.refs_0_.refs_1_, f32[4,272,256]{2,1,0:T(8,128)S(1)} %get-tuple-element.61.refs_1_, bf16[2,256,256]{2,1,0:T(8,128)(2,1)S(1)} %collective-permute-done.11.refs_2_, ...), custom_call_target="tpu_custom_call", output_to_operand_aliasing={{}: (1, {})} | custom-call | flops 671088640 | bytes 4000000 | tf_op jit(solution)/shard_map/pallas_call | solution.py:28
  66.3 1.5 %shard_map.121.refs_3_ = f32[4,272,256]{2,1,0:T(8,128)S(1)} custom-call(bf16[4,256,256]{2,1,0:T(8,128)(2,1)S(1)} %get-tuple-element.55.refs_0_.refs_1_, f32[4,272,256]{2,1,0:T(8,128)S(1)} %shard_map.120.refs_1_, bf16[2,256,256]{2,1,0:T(8,128)(2,1)S(1)} %collective-permute-done.12.refs_2_.plus, ...), custom_call_target="tpu_custom_call", output_to_operand_aliasing={{}: (1, {})} | custom-call | flops 671088640 | bytes 4000000 | tf_op jit(solution)/shard_map/pallas_call | solution.py:28
  67.8 1.5 %shard_map.118.refs_1_ = f32[4,272,256]{2,1,0:T(8,128)S(1)} custom-call(bf16[4,256,256]{2,1,0:T(8,128)(2,1)S(1)} %get-tuple-element.54.refs_0_, f32[4,272,256]{2,1,0:T(8,128)S(1)} %get-tuple-element.58.refs_1_, bf16[2,256,256]{2,1,0:T(8,128)(2,1)S(1)} %collective-permute-done.11.refs_2_, ...), custom_call_target="tpu_custom_call", output_to_operand_aliasing={{}: (1, {})} | custom-call | flops 671088640 | bytes 4000000 | tf_op jit(solution)/shard_map/pallas_call | solution.py:28
  69.3 1.5 %shard_map.119.refs_2_ = f32[4,272,256]{2,1,0:T(8,128)S(1)} custom-call(bf16[4,256,256]{2,1,0:T(8,128)(2,1)S(1)} %get-tuple-element.54.refs_0_, f32[4,272,256]{2,1,0:T(8,128)S(1)} %shard_map.118.refs_1_, bf16[2,256,256]{2,1,0:T(8,128)(2,1)S(1)} %collective-permute-done.12.refs_2_.plus, ...), custom_call_target="tpu_custom_call", output_to_operand_aliasing={{}: (1, {})} | custom-call | flops 671088640 | bytes 4000000 | tf_op jit(solution)/shard_map/pallas_call | solution.py:28
  71.9 5.0 %collective-permute-start.18 = (f32[2,272,256]{2,1,0:T(8,128)S(1)}, f32[2,272,256]{2,1,0:T(8,128)S(1)}, u32[]{:S(2)}, u32[]{:S(2)}) collective-permute-start(f32[2,272,256]{2,1,0:T(8,128)S(1)} %get-tuple-element.67), channel_id=1, source_target_pairs={{0,1},{1,0},{2,3},{3,2},{4,5},{5,4},{6,7},{7,6},{8,9},{9,8},{10,11... | collective-permute-start | bytes 1671176 | tf_op jit(solution)/shard_map/ppermute | solution.py:391
  78.6 2.2 %collective-permute-start.19 = (bf16[2,272,256]{2,1,0:T(8,128)(2,1)S(1)}, bf16[2,272,256]{2,1,0:T(8,128)(2,1)S(1)}, u32[]{:S(2)}, u32[]{:S(2)}) collective-permute-start(bf16[2,272,256]{2,1,0:T(8,128)(2,1)S(1)} %shard_map.126), channel_id=1, source_target_pairs={{0,2},{1,3},{2,0},{3,1},{4,6},{5,7},{6,4},{7,5},{8,10},{9,11},{10,... | collective-permute-start | bytes 835592 | tf_op jit(solution)/shard_map/ppermute | solution.py:391
  80.8 7.2 %collective-permute-done.19.received = bf16[2,272,256]{2,1,0:T(8,128)(2,1)S(1)} collective-permute-done((bf16[2,272,256]{2,1,0:T(8,128)(2,1)S(1)}, bf16[2,272,256]{2,1,0:T(8,128)(2,1)S(1)}, u32[]{:S(2)}, u32[]{:S(2)}) %collective-permute-start.19) | collective-permute-done | bytes 278560 | tf_op jit(solution)/shard_map/ppermute | solution.py:391
  (36 shorter events, 10.8 us)
Async XLA Ops:
  0.0 16.4 %collective-permute-start = (bf16[2,8,128,128]{3,2,1,0:T(8,128)(2,1)}, bf16[2,8,128,128]{3,2,1,0:T(8,128)(2,1)S(1)}, u32[]{:S(2)}, u32[]{:S(2)}) collective-permute-start(bf16[2,8,128,128]{3,2,1,0:T(8,128)(2,1)} %video.1), channel_id=1, source_target_pairs={{0,32},{32,64},{64,96},{96,128},{128,160},{160,192},{192,224},{224... | collective-permute-start | bytes 1572872 | tf_op jit(solution)/shard_map/ppermute | solution.py:377
  3.0 19.2 %collective-permute-start.2 = (bf16[2,2,128,128]{3,2,1,0:T(8,128)(2,1)S(1)}, bf16[2,2,128,128]{3,2,1,0:T(8,128)(2,1)S(1)}, u32[]{:S(2)}, u32[]{:S(2)}) collective-permute-start(bf16[2,2,128,128]{3,2,1,0:T(8,128)(2,1)S(1)} %get-tuple-element.41), channel_id=1, source_target_pairs={{0,31},{1,0},{2,1},{3,2},{4,3},{5,4},{6,5},{7,6},{8,7},{9,8},{10,9... | collective-permute-start | bytes 393224 | tf_op jit(solution)/shard_map/ppermute | solution.py:380
  4.3 18.0 %collective-permute-start.4 = (bf16[2,2,128,128]{3,2,1,0:T(8,128)(2,1)S(1)}, bf16[2,2,128,128]{3,2,1,0:T(8,128)(2,1)S(1)}, u32[]{:S(2)}, u32[]{:S(2)}) collective-permute-start(bf16[2,2,128,128]{3,2,1,0:T(8,128)(2,1)S(1)} %get-tuple-element.41), channel_id=1, source_target_pairs={{0,63},{1,32},{2,33},{3,34},{4,35},{5,36},{6,37},{7,38},{8,39},{9,... | collective-permute-start | bytes 393224 | tf_op jit(solution)/shard_map/ppermute | solution.py:388
  12.1 7.4 %collective-permute-start.1 = (bf16[2,1,128,128]{3,2,1,0:T(8,128)(2,1)S(1)}, bf16[2,1,128,128]{3,2,1,0:T(8,128)(2,1)S(1)}, u32[]{:S(2)}, u32[]{:S(2)}) collective-permute-start(bf16[2,1,128,128]{3,2,1,0:T(8,128)(2,1)S(1)} %get-tuple-element.40), channel_id=1, source_target_pairs={{0,1},{1,2},{2,3},{3,4},{4,5},{5,6},{6,7},{7,8},{8,9},{9,10},{10,1... | collective-permute-start | bytes 196616 | tf_op jit(solution)/shard_map/ppermute | solution.py:380
  12.1 10.2 %collective-permute-start.3 = (bf16[2,1,128,128]{3,2,1,0:T(8,128)(2,1)S(1)}, bf16[2,1,128,128]{3,2,1,0:T(8,128)(2,1)S(1)}, u32[]{:S(2)}, u32[]{:S(2)}) collective-permute-start(bf16[2,1,128,128]{3,2,1,0:T(8,128)(2,1)S(1)} %get-tuple-element.40), channel_id=1, source_target_pairs={{0,33},{1,34},{2,35},{3,36},{4,37},{5,38},{6,39},{7,40},{8,41},{9,... | collective-permute-start | bytes 196616 | tf_op jit(solution)/shard_map/ppermute | solution.py:388
  25.5 7.6 %collective-permute-start.5 = (bf16[2,256,256]{2,1,0:T(8,128)(2,1)S(1)}, bf16[2,256,256]{2,1,0:T(8,128)(2,1)S(1)}, u32[]{:S(2)}, u32[]{:S(2)}) collective-permute-start(bf16[2,256,256]{2,1,0:T(8,128)(2,1)S(1)} %get-tuple-element.46), channel_id=1, source_target_pairs={{0,32},{32,64},{64,96},{96,128},{128,160},{160,192},{192,224},{224... | collective-permute-start | bytes 786440 | tf_op jit(solution)/shard_map/ppermute | solution.py:377
  33.9 8.6 %collective-permute-start.6 = (bf16[2,256,256]{2,1,0:T(8,128)(2,1)S(1)}, bf16[2,256,256]{2,1,0:T(8,128)(2,1)S(1)}, u32[]{:S(2)}, u32[]{:S(2)}) collective-permute-start(bf16[2,256,256]{2,1,0:T(8,128)(2,1)S(1)} %get-tuple-element.49.normed.refs_4_), channel_id=1, source_target_pairs={{0,4},{1,5},{2,6},{3,7},{4,8},{5,9},{6,10},{7,11},{8,12},{9,13},{1... | collective-permute-start | bytes 786440 | tf_op jit(solution)/shard_map/ppermute | solution.py:380
  35.0 12.6 %collective-permute-start.10 = (bf16[2,256,256]{2,1,0:T(8,128)(2,1)S(1)}, bf16[2,256,256]{2,1,0:T(8,128)(2,1)S(1)}, u32[]{:S(2)}, u32[]{:S(2)}) collective-permute-start(bf16[2,256,256]{2,1,0:T(8,128)(2,1)S(1)} %get-tuple-element.49.normed.refs_4_), channel_id=1, source_target_pairs={{0,28},{1,29},{2,30},{3,31},{4,0},{5,1},{6,2},{7,3},{8,4},{9,5},{1... | collective-permute-start | bytes 786440 | tf_op jit(solution)/shard_map/ppermute | solution.py:380
  42.5 11.8 %collective-permute-start.8 = (bf16[2,256,256]{2,1,0:T(8,128)(2,1)S(1)}, bf16[2,256,256]{2,1,0:T(8,128)(2,1)S(1)}, u32[]{:S(2)}, u32[]{:S(2)}) collective-permute-start(bf16[2,256,256]{2,1,0:T(8,128)(2,1)S(1)} %shard_map.115.refs_0_), channel_id=1, source_target_pairs={{0,2},{1,3},{2,0},{3,1},{4,6},{5,7},{6,4},{7,5},{8,10},{9,11},{10,... | collective-permute-start | bytes 786440 | tf_op jit(solution)/shard_map/ppermute | solution.py:391
  47.6 7.7 %collective-permute-start.11 = (bf16[2,256,256]{2,1,0:T(8,128)(2,1)S(1)}, bf16[2,256,256]{2,1,0:T(8,128)(2,1)S(1)}, u32[]{:S(2)}, u32[]{:S(2)}) collective-permute-start(bf16[2,256,256]{2,1,0:T(8,128)(2,1)S(1)} %collective-permute-done.6.refs_5_), channel_id=1, source_target_pairs={{0,4},{1,5},{2,6},{3,7},{4,8},{5,9},{6,10},{7,11},{8,12},{9,13},{1... | collective-permute-start | bytes 786440 | tf_op jit(solution)/shard_map/ppermute | solution.py:380
  47.6 7.7 %collective-permute-start.13 = (bf16[2,256,256]{2,1,0:T(8,128)(2,1)S(1)}, bf16[2,256,256]{2,1,0:T(8,128)(2,1)S(1)}, u32[]{:S(2)}, u32[]{:S(2)}) collective-permute-start(bf16[2,256,256]{2,1,0:T(8,128)(2,1)S(1)} %collective-permute-done.10.refs_6_), channel_id=1, source_target_pairs={{0,28},{1,29},{2,30},{3,31},{4,0},{5,1},{6,2},{7,3},{8,4},{9,5},{1... | collective-permute-start | bytes 786440 | tf_op jit(solution)/shard_map/ppermute | solution.py:380
  50.3 7.7 %collective-permute-start.7 = (bf16[2,256,256]{2,1,0:T(8,128)(2,1)S(1)}, bf16[2,256,256]{2,1,0:T(8,128)(2,1)S(1)}, u32[]{:S(2)}, u32[]{:S(2)}) collective-permute-start(bf16[2,256,256]{2,1,0:T(8,128)(2,1)S(1)} %shard_map.115.refs_0_), channel_id=1, source_target_pairs={{0,1},{1,0},{2,3},{3,2},{4,5},{5,4},{6,7},{7,6},{8,9},{9,8},{10,11... | collective-permute-start | bytes 786440 | tf_op jit(solution)/shard_map/ppermute | solution.py:391
  54.2 3.8 %collective-permute-start.9 = (bf16[2,256,256]{2,1,0:T(8,128)(2,1)S(1)}, bf16[2,256,256]{2,1,0:T(8,128)(2,1)S(1)}, u32[]{:S(2)}, u32[]{:S(2)}) collective-permute-start(bf16[2,256,256]{2,1,0:T(8,128)(2,1)S(1)} %collective-permute-done.8.refs_2_), channel_id=1, source_target_pairs={{0,1},{1,0},{2,3},{3,2},{4,5},{5,4},{6,7},{7,6},{8,9},{9,8},{10,11... | collective-permute-start | bytes 786440 | tf_op jit(solution)/shard_map/ppermute | solution.py:391
  55.3 6.4 %collective-permute-start.12 = (bf16[2,256,256]{2,1,0:T(8,128)(2,1)S(1)}, bf16[2,256,256]{2,1,0:T(8,128)(2,1)S(1)}, u32[]{:S(2)}, u32[]{:S(2)}) collective-permute-start(bf16[2,256,256]{2,1,0:T(8,128)(2,1)S(1)} %collective-permute-done.11.refs_2_), channel_id=1, source_target_pairs={{0,4},{1,5},{2,6},{3,7},{4,8},{5,9},{6,10},{7,11},{8,12},{9,13},{1... | collective-permute-start | bytes 786440 | tf_op jit(solution)/shard_map/ppermute | solution.py:380
  55.4 6.4 %collective-permute-start.14 = (bf16[2,256,256]{2,1,0:T(8,128)(2,1)S(1)}, bf16[2,256,256]{2,1,0:T(8,128)(2,1)S(1)}, u32[]{:S(2)}, u32[]{:S(2)}) collective-permute-start(bf16[2,256,256]{2,1,0:T(8,128)(2,1)S(1)} %collective-permute-done.13.refs_3_), channel_id=1, source_target_pairs={{0,28},{1,29},{2,30},{3,31},{4,0},{5,1},{6,2},{7,3},{8,4},{9,5},{1... | collective-permute-start | bytes 786440 | tf_op jit(solution)/shard_map/ppermute | solution.py:380
  61.8 8.9 %collective-permute-start.15 = (bf16[256,256]{1,0:T(8,128)(2,1)S(1)}, bf16[256,256]{1,0:T(8,128)(2,1)S(1)}, u32[]{:S(2)}, u32[]{:S(2)}) collective-permute-start(bf16[256,256]{1,0:T(8,128)(2,1)S(1)} %get-tuple-element.62), channel_id=1, source_target_pairs={{0,4},{1,5},{2,6},{3,7},{4,8},{5,9},{6,10},{7,11},{8,12},{9,13},{1... | collective-permute-start | bytes 393224 | tf_op jit(solution)/shard_map/ppermute | solution.py:380
  61.9 8.8 %collective-permute-start.16 = (bf16[256,256]{1,0:T(8,128)(2,1)S(1)}, bf16[256,256]{1,0:T(8,128)(2,1)S(1)}, u32[]{:S(2)}, u32[]{:S(2)}) collective-permute-start(bf16[256,256]{1,0:T(8,128)(2,1)S(1)} %get-tuple-element.63), channel_id=1, source_target_pairs={{0,28},{1,29},{2,30},{3,31},{4,0},{5,1},{6,2},{7,3},{8,4},{9,5},{1... | collective-permute-start | bytes 393224 | tf_op jit(solution)/shard_map/ppermute | solution.py:380
  71.9 6.6 %collective-permute-start.18 = (f32[2,272,256]{2,1,0:T(8,128)S(1)}, f32[2,272,256]{2,1,0:T(8,128)S(1)}, u32[]{:S(2)}, u32[]{:S(2)}) collective-permute-start(f32[2,272,256]{2,1,0:T(8,128)S(1)} %get-tuple-element.67), channel_id=1, source_target_pairs={{0,1},{1,0},{2,3},{3,2},{4,5},{5,4},{6,7},{7,6},{8,9},{9,8},{10,11... | collective-permute-start | bytes 1671176 | tf_op jit(solution)/shard_map/ppermute | solution.py:391
  78.0 2.8 %collective-permute-start.17 = (f32[2,272,256]{2,1,0:T(8,128)S(1)}, f32[2,272,256]{2,1,0:T(8,128)S(1)}, u32[]{:S(2)}, u32[]{:S(2)}) collective-permute-start(f32[2,272,256]{2,1,0:T(8,128)S(1)} %get-tuple-element.65), channel_id=1, source_target_pairs={{0,1},{1,0},{2,3},{3,2},{4,5},{5,4},{6,7},{7,6},{8,9},{9,8},{10,11... | collective-permute-start | bytes 1671176 | tf_op jit(solution)/shard_map/ppermute | solution.py:391
  78.6 9.5 %collective-permute-start.19 = (bf16[2,272,256]{2,1,0:T(8,128)(2,1)S(1)}, bf16[2,272,256]{2,1,0:T(8,128)(2,1)S(1)}, u32[]{:S(2)}, u32[]{:S(2)}) collective-permute-start(bf16[2,272,256]{2,1,0:T(8,128)(2,1)S(1)} %shard_map.126), channel_id=1, source_target_pairs={{0,2},{1,3},{2,0},{3,1},{4,6},{5,7},{6,4},{7,5},{8,10},{9,11},{10,... | collective-permute-start | bytes 835592 | tf_op jit(solution)/shard_map/ppermute | solution.py:391

commit v3 on v2

--- a/solution.py
+++ b/solution.py
@@ -73,12 +73,16 @@
     return jnp.concatenate([ref[0, i], ref[1, i]], axis=1)
 
 
-def fill_taps(taps, rows, gain_ref):
+def fill_taps(taps, rows, gain_ref, batch):
     gain2 = jnp.concatenate([gain_ref[...], gain_ref[...]], axis=1)
     mean_of = averaging()
-    for row, ref, i, factor in rows:
-        act = activate(pair_of(ref, i), gain2, mean_of)
-        store_shifted(taps, row, act if factor is None else act * factor)
+    for start in range(0, len(rows), batch):
+        some = rows[start : start + batch]
+        pairs = jnp.concatenate([pair_of(ref, i) for _, ref, i, _ in some], axis=0)
+        acts = activate(pairs, gain2, mean_of)
+        for place, (row, _, _, factor) in enumerate(some):
+            act = acts[place * COLS : (place + 1) * COLS]
+            store_shifted(taps, row, act if factor is None else act * factor)
 
 
 SIZE = (ROWS + 1) * COLS
@@ -127,7 +131,7 @@
     blank_edges(taps)
     for copy in copies[:3]:
         copy.wait()
-    fill_taps(taps, [(row + 1, video, row, None) for row in range(ROWS)], gain)
+    fill_taps(taps, [(row + 1, video, row, None) for row in range(ROWS)], gain, 4)
     copies[3].wait()
     none = jnp.zeros((C1, C1), bf16)
     for kr in range(3):
@@ -150,41 +154,51 @@
 
 def halo_kernel(flags, acc_in, halo, gain, weight, acc, taps):
     blank_edges(taps)
-    fill_taps(taps, [(row + 1, halo, row, flags[0]) for row in range(ROWS)], gain)
+    fill_taps(taps, [(row + 1, halo, row, flags[0]) for row in range(ROWS)], gain, 4)
     conv1_taps(taps, weight, acc, lambda: acc_in[...])
 
 
+TAPS = [(kr, kc) for kr in range(3) for kc in range(3)]
+
+
+def down_taps(half_taps, lanes):
+    starts = (0, 5 * HALF, HALF)
+    tiles = [half_taps[kc, starts[kr] : starts[kr] + QUERIES, lanes] for kr, kc in TAPS]
+    return jnp.concatenate(tiles, axis=1)
+
+
+def down_weights(down, times):
+    return jnp.concatenate([down[kt, kr, kc] for kr, kc in TAPS for kt in times], axis=0)
+
+
 def sum_kernel(
-    flags, acc_in, above, below, far_above, far_below, gain, now, before, down,
-    send, half_taps, acc, taps, far_taps, wide,
+    flags, acc, above, below, far_above, far_below, gain, now, before, down,
+    send, half_taps, taps, wide,
 ):
     past = flags[0]
     edges = [(0, above, 0, flags[1]), (1, below, 0, flags[2]), (2, below, 1, flags[2])]
-    fill_taps(taps, edges, gain)
-    edges = [(0, far_above, 0, flags[1]), (1, far_below, 0, flags[2]), (2, far_below, 1, flags[2])]
-    fill_taps(far_taps, [(row, ref, i, factor * past) for row, ref, i, factor in edges], gain)
-
-    def add(kr, taps_row, count, row):
+    far = [(3, far_above, 0, flags[1]), (4, far_below, 0, flags[2]), (5, far_below, 1, flags[2])]
+    fill_taps(taps, edges + [(row, ref, i, factor * past) for row, ref, i, factor in far], gain, 3)
+
+    def extra(kr, row, count):
         tile = jnp.concatenate(
             [
-                source[kc, taps_row * COLS : (taps_row + count) * COLS, :]
-                for source in (taps, far_taps)
+                taps[kc, (base + row) * COLS : (base + row + count) * COLS, :]
+                for base in (0, 3)
                 for kc in range(3)
             ],
             axis=1,
         )
         weight = jnp.concatenate([now[kr].reshape(3 * C2, C2), before[kr].reshape(3 * C2, C2)], axis=0)
-        at = pl.ds(row * COLS, count * COLS)
-        acc[at, :] += dot(tile, weight)
-
-    acc[...] = acc_in[...]
-    acc[pl.ds(ROWS * COLS, COLS), :] += pair_of(below, 0).astype(f32)
-    add(0, 0, 1, 0)
-    add(1, 1, 1, ROWS)
-    add(2, 1, 2, ROWS - 1)
+        return dot(tile, weight)
+
+    last = extra(2, 1, 2)
+    extras = {0: extra(0, 0, 1), ROWS - 1: last[:COLS]}
+    extras[ROWS] = last[COLS:] + extra(1, 1, 1) + pair_of(below, 0).astype(f32)
     for row in range(ROWS + 1):
         at = pl.ds(row * COLS, COLS)
-        summed = acc[at, :].astype(bf16).astype(f32)
+        summed = acc[at, :] + extras[row] if row in extras else acc[at, :]
+        summed = summed.astype(bf16).astype(f32)
         if row == ROWS:
             summed = summed * flags[2]
         wide[0, at, :] = summed[:, :C1]
@@ -201,38 +215,24 @@
             half_taps[0, at, lanes] = even.astype(bf16)
             half_taps[1, at, lanes] = odd.astype(bf16)
             half_taps[2, at, lanes] = after.astype(bf16)
-    first = jnp.zeros((QUERIES, C2), f32)
-    second = jnp.zeros((QUERIES, C2), f32)
-    for kr in range(3):
-        start = (0, 5 * HALF, HALF)[kr]
-        for kc in range(3):
-            tile = half_taps[kc, start : start + QUERIES, :]
-            first += dot(tile, jnp.concatenate([down[0, kr, kc], down[1, kr, kc]], axis=0))
-            second += dot(tile[:, C1:], down[0, kr, kc])
-    send[0] = first.astype(bf16)
-    send[1] = second.astype(bf16)
+    send[0] = dot(down_taps(half_taps, slice(None)), down_weights(down, (0, 1))).astype(bf16)
+    send[1] = dot(down_taps(half_taps, slice(C1, None)), down_weights(down, (0,))).astype(bf16)
 
 
 def down_kernel(half_taps, down, bias, out):
-    first = jnp.zeros((QUERIES, C2), f32) + bias[...]
-    second = jnp.zeros((QUERIES, C2), f32) + bias[...]
-    for kr in range(3):
-        start = (0, 5 * HALF, HALF)[kr]
-        for kc in range(3):
-            tile = half_taps[kc, start : start + QUERIES, :]
-            first += dot(tile[:, :C1], down[2, kr, kc])
-            second += dot(tile, jnp.concatenate([down[1, kr, kc], down[2, kr, kc]], axis=0))
-    out[0] = first
-    out[1] = second
-
-
-def norm_kernel(flags, part, received, gain, reduced, normed):
+    out[0] = dot(down_taps(half_taps, slice(0, C1)), down_weights(down, (2,))) + bias[...]
+    out[1] = dot(down_taps(half_taps, slice(None)), down_weights(down, (1, 2))) + bias[...]
+
+
+def norm_kernel(flags, part, received, gain, query_weight, reduced, normed, queries):
+    value = part[...] + received[...].astype(f32) * flags[0]
+    reduced[...] = value
+    centred = value - jnp.mean(value, axis=2, keepdims=True)
+    spread = jnp.mean(centred * centred, axis=2, keepdims=True)
+    result = (centred * lax.rsqrt(spread + epsilon) * gain[...]).astype(bf16)
+    normed[...] = result
     for frame in range(2):
-        value = part[frame] + received[frame].astype(f32) * flags[0]
-        reduced[frame] = value
-        centred = value - jnp.mean(value, axis=1, keepdims=True)
-        spread = jnp.mean(centred * centred, axis=1, keepdims=True)
-        normed[frame] = (centred * lax.rsqrt(spread + epsilon) * gain[...]).astype(bf16)
+        queries[frame] = (dot(result[frame], query_weight[...]).astype(bf16) * (C2**-0.5)).astype(bf16)
 
 
 GROUPS = 4
@@ -261,11 +261,6 @@
         out, place = outs(group)
         out[place, : C2 + 8, :] = product
         out[place, C2 + 8 :, :] = jnp.broadcast_to(highest, (8, C2))
-
-
-def query_kernel(normed, weight, queries):
-    for frame in range(2):
-        queries[frame] = (dot(normed[frame], weight[...]).astype(bf16) * (C2**-0.5)).astype(bf16)
 
 
 def first_attend_kernel(
@@ -443,7 +438,7 @@
         sum_kernel,
         [((2, QUERIES, C2), bf16), ((3, 9 * HALF, C2), bf16)],
         [flags, acc, above, below, far_above, far_below, gain, now, before, down_weight],
-        [pltpu.VMEM(*whole)] + [pltpu.VMEM((3, 3 * COLS, C2), bf16)] * 2 + [pltpu.VMEM((2, SIZE, C1), f32)],
+        [pltpu.VMEM((3, 6 * COLS, C2), bf16), pltpu.VMEM((2, SIZE, C1), f32)],
         scalar,
         flops=2 * 18 * 256 * 256 * 256,
         nbytes=5_000_000,
@@ -457,20 +452,18 @@
         nbytes=3_000_000,
     )
     pixels = ((2, QUERIES, C2), bf16)
-    reduced, normed = call(
+    reduced, normed, own = call(
         norm_kernel,
-        [((2, QUERIES, C2), f32), pixels],
-        [flags, part, received, attention_gain],
+        [((2, QUERIES, C2), f32), pixels, pixels],
+        [flags, part, received, attention_gain, query_weight],
         spaces=scalar,
         nbytes=2_000_000,
     )
     plus, minus = [along(normed, 4)], [along(normed, -4)]
-    (own,) = call(query_kernel, [pixels], [normed, query_weight], nbytes=600_000)
     for step in range(2):
         plus.append(along(plus[step], 4))
         minus.append(along(minus[step], -4))
-    given, _ = lax.optimization_barrier((own, plus[0]))
-    sibling, across = swap(given, 1), swap(given, 2)
+    sibling, across = swap(own, 1), swap(own, 2)
     both = swap(across, 1)
     state = [((GROUPS, STATE, C2), f32)]
     flops = 2 * QUERIES * 256 * (512 + 2 * GROUPS * QUERIES)
@@ -484,10 +477,7 @@
             flops=3 * flops,
             nbytes=4_000_000,
         )
-    (plus[2], minus[2]), carry = lax.optimization_barrier(((plus[2], minus[2]), carry))
-    ends = call(cut_kernel, [((QUERIES, C2), bf16)] * 2, [plus[2], minus[2]], nbytes=500_000)
-    ends = [along(ends[0], 4), along(ends[1], -4)]
-    for step in range(1, 3):
+    def step_on(step):
         for frame in range(2):
             (carry[frame],) = call(
                 lambda *refs: attend_kernel(frame, *refs),
@@ -497,6 +487,12 @@
                 flops=2 * flops,
                 nbytes=4_000_000,
             )
+
+    step_on(1)
+    (plus[2], minus[2]), carry = lax.optimization_barrier(((plus[2], minus[2]), carry))
+    ends = call(cut_kernel, [((QUERIES, C2), bf16)] * 2, [plus[2], minus[2]], nbytes=500_000)
+    ends = [along(ends[0], 4), along(ends[1], -4)]
+    step_on(2)
     pair = ((2, STATE, C2), f32)
 
     def finish(groups):

time: 89.2 us -> 84.8 us (0.951)
  waiting for transfers between devices: 19.6 us -> 15.8 us
  Pallas kernels: 26 us -> 24.6 us
    ppermute x10, waiting for transfers between devices: 3.85 us -> 0.03 us  [along(): lax.ppermute(x, 'space', [(i, (i + distance) % space) for i in range(spac...]
    pallas_call x19 -> x18, Pallas kernels: 26 us -> 24.6 us  [call(): pl.pallas_call(kernel, out_shape=[jax.ShapeDtypeStruct(s, d) for s, d in...]
  transfers between devices with their start and end apart: 20 -> 20, of which waited for: 6 -> 4; matrix products, arithmetic and copies ran while one was open for 0% -> 0% of each run, Pallas kernels for 22% -> 22%
where the time goes in v3:
time: 84.8 us; the launch traced here: 84.7 us
  starting transfers between devices  44 us (52%)
  Pallas kernels  24.6 us (29%)
  waiting for transfers between devices  15.8 us (19%)
    pallas_call x18, Pallas kernels, call(): pl.pallas_call(kernel, out_shape=[jax.ShapeDtypeStruct(s, d) for s, d in...  24.6 us
    ppermute x6, starting transfers between devices, swap(): return lax.ppermute(x, 'space', [(i, i ^ bit) for i in range(space)])  18.1 us
    ppermute x10, starting transfers between devices, along(): lax.ppermute(x, 'space', [(i, (i + distance) % space) for i in range(spac...  14.8 us
    ppermute x2, starting transfers between devices, diagonal(): return lax.ppermute(x, ('tm', 'space'), route)  7.78 us
    ppermute x6, waiting for transfers between devices, swap(): return lax.ppermute(x, 'space', [(i, i ^ bit) for i in range(space)])  7.03 us
    ppermute x2, waiting for transfers between devices, next_frames(): return lax.ppermute(x, 'tm', [(i, (i + 1) % times) for i in range(times)])  5.57 us
    ppermute x2, starting transfers between devices, next_frames(): return lax.ppermute(x, 'tm', [(i, (i + 1) % times) for i in range(times)])  3.29 us
    ppermute x2, waiting for transfers between devices, diagonal(): return lax.ppermute(x, ('tm', 'space'), route)  3.21 us
  transfers between devices with their start and end apart: 20, of which 4 were waited for; matrix products, arithmetic and copies ran while one was open for 0% of the time, Pallas kernels for 22%

profile of v3, /device:TPU:1, one launch (start us, length us, event | category | flops | bytes accessed | tf_op | source)
XLA Modules:
  0.0 84.7 jit_solution(18002496687053399511)
XLA Ops:
  0.0 2.0 %collective-permute-start = (bf16[2,8,128,128]{3,2,1,0:T(8,128)(2,1)}, bf16[2,8,128,128]{3,2,1,0:T(8,128)(2,1)S(1)}, u32[]{:S(2)}, u32[]{:S(2)}) collective-permute-start(bf16[2,8,128,128]{3,2,1,0:T(8,128)(2,1)} %video.1), channel_id=1, source_target_pairs={{0,32},{32,64},{64,96},{96,128},{128,160},{160,192},{192,224},{224... | collective-permute-start | bytes 1572872 | tf_op jit(solution)/shard_map/ppermute | solution.py:372
  3.0 1.3 %collective-permute-start.2 = (bf16[2,2,128,128]{3,2,1,0:T(8,128)(2,1)S(1)}, bf16[2,2,128,128]{3,2,1,0:T(8,128)(2,1)S(1)}, u32[]{:S(2)}, u32[]{:S(2)}) collective-permute-start(bf16[2,2,128,128]{3,2,1,0:T(8,128)(2,1)S(1)} %get-tuple-element.41), channel_id=1, source_target_pairs={{0,31},{1,0},{2,1},{3,2},{4,3},{5,4},{6,5},{7,6},{8,7},{9,8},{10,9... | collective-permute-start | bytes 393224 | tf_op jit(solution)/shard_map/ppermute | solution.py:375
  4.3 7.8 %collective-permute-start.4 = (bf16[2,2,128,128]{3,2,1,0:T(8,128)(2,1)S(1)}, bf16[2,2,128,128]{3,2,1,0:T(8,128)(2,1)S(1)}, u32[]{:S(2)}, u32[]{:S(2)}) collective-permute-start(bf16[2,2,128,128]{3,2,1,0:T(8,128)(2,1)S(1)} %get-tuple-element.41), channel_id=1, source_target_pairs={{0,63},{1,32},{2,33},{3,34},{4,35},{5,36},{6,37},{7,38},{8,39},{9,... | collective-permute-start | bytes 393224 | tf_op jit(solution)/shard_map/ppermute | solution.py:383
  12.1 4.0 %shard_map.109 = (f32[1152,256]{1,0:T(8,128)S(1)}, bf16[3,3,256,256]{3,2,1,0:T(8,128)(2,1)S(1)}, bf16[3,3,256,256]{3,2,1,0:T(8,128)(2,1)S(1)}, bf16[3,3,3,128,25...) custom-call(bf16[2,8,128,128]{3,2,1,0:T(8,128)(2,1)} %video.1, ...), custom_call_target="tpu_custom_call" | custom-call | flops 1358954496 | bytes 6000000 | tf_op jit(solution)/shard_map/pallas_call | solution.py:28
  16.2 2.8 %shard_map.110.acc = f32[1152,256]{1,0:T(8,128)S(1)} custom-call(f32[3]{0:T(128)S(1)} %add_convert_fusion.flags, f32[1152,256]{1,0:T(8,128)S(1)} %get-tuple-element.37.acc_in, bf16[2,8,128,128]{3,2,1,0:T(8,128)(2,1)S(1)} %collective-permute-done.halo, f32[1,128]{1,0:T(1,128)S(1)} %get-tuple-element.38.gain, ...), custom_call_target="tpu_custom_call" | custom-call | flops 1358954496 | bytes 5000000 | tf_op jit(solution)/shard_map/pallas_call | solution.py:28
  19.0 3.2 %collective-permute-done.3.far_above = bf16[2,1,128,128]{3,2,1,0:T(8,128)(2,1)S(1)} collective-permute-done((bf16[2,1,128,128]{3,2,1,0:T(8,128)(2,1)S(1)}, bf16[2,1,128,128]{3,2,1,0:T(8,128)(2,1)S(1)}, u32[]{:S(2)}, u32[]{:S(2)}) %collective-permute-start.3) | collective-permute-done | bytes 65568 | tf_op jit(solution)/shard_map/ppermute | solution.py:383
  22.2 2.6 %shard_map.112 = (bf16[2,256,256]{2,1,0:T(8,128)(2,1)S(1)}, bf16[3,576,256]{2,1,0:T(8,128)(2,1)S(1)}) custom-call(f32[3]{0:T(128)S(1)} %add_convert_fusion.flags, f32[1152,256]{1,0:T(8,128)S(1)} %shard_map.110.acc, bf16[2,1,128,128]{3,2,1,0:T(8,128)(2,1)S(1)} %collective-permute-done.1.above, bf16[2,2,128,128]{3,2,1,0:T(8,128)(2,1)S(1)} %collective-permute-done.2.below, ...), custom_call_target="tpu_custom_call" | custom-call | flops 603979776 | bytes 5000000 | tf_op jit(solution)/shard_map/pallas_call | solution.py:28
  26.7 5.5 %collective-permute-done.5.received = bf16[2,256,256]{2,1,0:T(8,128)(2,1)S(1)} collective-permute-done((bf16[2,256,256]{2,1,0:T(8,128)(2,1)S(1)}, bf16[2,256,256]{2,1,0:T(8,128)(2,1)S(1)}, u32[]{:S(2)}, u32[]{:S(2)}) %collective-permute-start.5) | collective-permute-done | bytes 262176 | tf_op jit(solution)/shard_map/ppermute | solution.py:372
  33.1 1.6 %collective-permute-start.9 = (bf16[2,256,256]{2,1,0:T(8,128)(2,1)S(1)}, bf16[2,256,256]{2,1,0:T(8,128)(2,1)S(1)}, u32[]{:S(2)}, u32[]{:S(2)}) collective-permute-start(bf16[2,256,256]{2,1,0:T(8,128)(2,1)S(1)} %get-tuple-element.51.refs_4_), channel_id=1, source_target_pairs={{0,4},{1,5},{2,6},{3,7},{4,8},{5,9},{6,10},{7,11},{8,12},{9,13},{1... | collective-permute-start | bytes 786440 | tf_op jit(solution)/shard_map/ppermute | solution.py:375
  34.8 3.8 %collective-permute-start.10 = (bf16[2,256,256]{2,1,0:T(8,128)(2,1)S(1)}, bf16[2,256,256]{2,1,0:T(8,128)(2,1)S(1)}, u32[]{:S(2)}, u32[]{:S(2)}) collective-permute-start(bf16[2,256,256]{2,1,0:T(8,128)(2,1)S(1)} %get-tuple-element.51.refs_4_), channel_id=1, source_target_pairs={{0,28},{1,29},{2,30},{3,31},{4,0},{5,1},{6,2},{7,3},{8,4},{9,5},{1... | collective-permute-start | bytes 786440 | tf_op jit(solution)/shard_map/ppermute | solution.py:375
  38.6 4.7 %collective-permute-start.7 = (bf16[2,256,256]{2,1,0:T(8,128)(2,1)S(1)}, bf16[2,256,256]{2,1,0:T(8,128)(2,1)S(1)}, u32[]{:S(2)}, u32[]{:S(2)}) collective-permute-start(bf16[2,256,256]{2,1,0:T(8,128)(2,1)S(1)} %get-tuple-element.50.refs_0_), channel_id=1, source_target_pairs={{0,2},{1,3},{2,0},{3,1},{4,6},{5,7},{6,4},{7,5},{8,10},{9,11},{10,... | collective-permute-start | bytes 786440 | tf_op jit(solution)/shard_map/ppermute | solution.py:386
  43.3 2.7 %collective-permute-start.13 = (bf16[2,256,256]{2,1,0:T(8,128)(2,1)S(1)}, bf16[2,256,256]{2,1,0:T(8,128)(2,1)S(1)}, u32[]{:S(2)}, u32[]{:S(2)}) collective-permute-start(bf16[2,256,256]{2,1,0:T(8,128)(2,1)S(1)} %collective-permute-done.10.refs_6_), channel_id=1, source_target_pairs={{0,28},{1,29},{2,30},{3,31},{4,0},{5,1},{6,2},{7,3},{8,4},{9,5},{1... | collective-permute-start | bytes 786440 | tf_op jit(solution)/shard_map/ppermute | solution.py:375
  45.9 3.7 %collective-permute-start.6 = (bf16[2,256,256]{2,1,0:T(8,128)(2,1)S(1)}, bf16[2,256,256]{2,1,0:T(8,128)(2,1)S(1)}, u32[]{:S(2)}, u32[]{:S(2)}) collective-permute-start(bf16[2,256,256]{2,1,0:T(8,128)(2,1)S(1)} %get-tuple-element.50.refs_0_), channel_id=1, source_target_pairs={{0,1},{1,0},{2,3},{3,2},{4,5},{5,4},{6,7},{7,6},{8,9},{9,8},{10,11... | collective-permute-start | bytes 786440 | tf_op jit(solution)/shard_map/ppermute | solution.py:386
  50.5 2.7 %collective-permute-start.14 = (bf16[2,256,256]{2,1,0:T(8,128)(2,1)S(1)}, bf16[2,256,256]{2,1,0:T(8,128)(2,1)S(1)}, u32[]{:S(2)}, u32[]{:S(2)}) collective-permute-start(bf16[2,256,256]{2,1,0:T(8,128)(2,1)S(1)} %collective-permute-done.13.refs_3_), channel_id=1, source_target_pairs={{0,28},{1,29},{2,30},{3,31},{4,0},{5,1},{6,2},{7,3},{8,4},{9,5},{1... | collective-permute-start | bytes 786440 | tf_op jit(solution)/shard_map/ppermute | solution.py:375
  53.2 1.7 %shard_map.116 = (bf16[4,256,256]{2,1,0:T(8,128)(2,1)S(1)}, f32[4,272,256]{2,1,0:T(8,128)S(1)}) custom-call(bf16[2,256,256]{2,1,0:T(8,128)(2,1)S(1)} %get-tuple-element.50.refs_0_, bf16[2,256,256]{2,1,0:T(8,128)(2,1)S(1)} %collective-permute-done.6.refs_1_, bf16[2,256,256]{2,1,0:T(8,128)(2,1)S(1)} %collective-permute-done.7.refs_2_, ...), custom_call_target="tpu_custom_call" | custom-call | flops 1006632960 | bytes 4000000 | tf_op jit(solution)/shard_map/pallas_call | solution.py:28
  54.9 1.5 %shard_map.118.refs_1_ = f32[4,272,256]{2,1,0:T(8,128)S(1)} custom-call(bf16[4,256,256]{2,1,0:T(8,128)(2,1)S(1)} %get-tuple-element.55.refs_0_.refs_1_, f32[4,272,256]{2,1,0:T(8,128)S(1)} %get-tuple-element.57.refs_1_, bf16[2,256,256]{2,1,0:T(8,128)(2,1)S(1)} %collective-permute-done.11.refs_2_, ...), custom_call_target="tpu_custom_call", output_to_operand_aliasing={{}: (1, {})} | custom-call | flops 671088640 | bytes 4000000 | tf_op jit(solution)/shard_map/pallas_call | solution.py:28
  56.3 1.7 %shard_map.115 = (bf16[4,256,256]{2,1,0:T(8,128)(2,1)S(1)}, f32[4,272,256]{2,1,0:T(8,128)S(1)}) custom-call(bf16[2,256,256]{2,1,0:T(8,128)(2,1)S(1)} %get-tuple-element.50.refs_0_, bf16[2,256,256]{2,1,0:T(8,128)(2,1)S(1)} %collective-permute-done.6.refs_1_, bf16[2,256,256]{2,1,0:T(8,128)(2,1)S(1)} %collective-permute-done.7.refs_2_, ...), custom_call_target="tpu_custom_call" | custom-call | flops 1006632960 | bytes 4000000 | tf_op jit(solution)/shard_map/pallas_call | solution.py:28
  58.0 1.5 %shard_map.117.refs_1_ = f32[4,272,256]{2,1,0:T(8,128)S(1)} custom-call(bf16[4,256,256]{2,1,0:T(8,128)(2,1)S(1)} %get-tuple-element.54.refs_0_, f32[4,272,256]{2,1,0:T(8,128)S(1)} %get-tuple-element.56.refs_1_, bf16[2,256,256]{2,1,0:T(8,128)(2,1)S(1)} %collective-permute-done.11.refs_2_, ...), custom_call_target="tpu_custom_call", output_to_operand_aliasing={{}: (1, {})} | custom-call | flops 671088640 | bytes 4000000 | tf_op jit(solution)/shard_map/pallas_call | solution.py:28
  59.6 2.7 %collective-permute-start.16 = (bf16[256,256]{1,0:T(8,128)(2,1)S(1)}, bf16[256,256]{1,0:T(8,128)(2,1)S(1)}, u32[]{:S(2)}, u32[]{:S(2)}) collective-permute-start(bf16[256,256]{1,0:T(8,128)(2,1)S(1)} %get-tuple-element.63), channel_id=1, source_target_pairs={{0,28},{1,29},{2,30},{3,31},{4,0},{5,1},{6,2},{7,3},{8,4},{9,5},{1... | collective-permute-start | bytes 393224 | tf_op jit(solution)/shard_map/ppermute | solution.py:375
  62.3 1.5 %shard_map.120.refs_3_ = f32[4,272,256]{2,1,0:T(8,128)S(1)} custom-call(bf16[4,256,256]{2,1,0:T(8,128)(2,1)S(1)} %get-tuple-element.55.refs_0_.refs_1_, f32[4,272,256]{2,1,0:T(8,128)S(1)} %shard_map.118.refs_1_, bf16[2,256,256]{2,1,0:T(8,128)(2,1)S(1)} %collective-permute-done.12.refs_2_.plus, ...), custom_call_target="tpu_custom_call", output_to_operand_aliasing={{}: (1, {})} | custom-call | flops 671088640 | bytes 4000000 | tf_op jit(solution)/shard_map/pallas_call | solution.py:28
  63.7 1.5 %shard_map.119.refs_2_ = f32[4,272,256]{2,1,0:T(8,128)S(1)} custom-call(bf16[4,256,256]{2,1,0:T(8,128)(2,1)S(1)} %get-tuple-element.54.refs_0_, f32[4,272,256]{2,1,0:T(8,128)S(1)} %shard_map.117.refs_1_, bf16[2,256,256]{2,1,0:T(8,128)(2,1)S(1)} %collective-permute-done.12.refs_2_.plus, ...), custom_call_target="tpu_custom_call", output_to_operand_aliasing={{}: (1, {})} | custom-call | flops 671088640 | bytes 4000000 | tf_op jit(solution)/shard_map/pallas_call | solution.py:28
  66.3 4.6 %collective-permute-start.18 = (f32[2,272,256]{2,1,0:T(8,128)S(1)}, f32[2,272,256]{2,1,0:T(8,128)S(1)}, u32[]{:S(2)}, u32[]{:S(2)}) collective-permute-start(f32[2,272,256]{2,1,0:T(8,128)S(1)} %get-tuple-element.67), channel_id=1, source_target_pairs={{0,1},{1,0},{2,3},{3,2},{4,5},{5,4},{6,7},{7,6},{8,9},{9,8},{10,11... | collective-permute-start | bytes 1671176 | tf_op jit(solution)/shard_map/ppermute | solution.py:386
  72.7 4.2 %collective-permute-start.19 = (bf16[2,272,256]{2,1,0:T(8,128)(2,1)S(1)}, bf16[2,272,256]{2,1,0:T(8,128)(2,1)S(1)}, u32[]{:S(2)}, u32[]{:S(2)}) collective-permute-start(bf16[2,272,256]{2,1,0:T(8,128)(2,1)S(1)} %shard_map.125), channel_id=1, source_target_pairs={{0,2},{1,3},{2,0},{3,1},{4,6},{5,7},{6,4},{7,5},{8,10},{9,11},{10,... | collective-permute-start | bytes 835592 | tf_op jit(solution)/shard_map/ppermute | solution.py:386
  76.9 6.6 %collective-permute-done.19.received = bf16[2,272,256]{2,1,0:T(8,128)(2,1)S(1)} collective-permute-done((bf16[2,272,256]{2,1,0:T(8,128)(2,1)S(1)}, bf16[2,272,256]{2,1,0:T(8,128)(2,1)S(1)}, u32[]{:S(2)}, u32[]{:S(2)}) %collective-permute-start.19) | collective-permute-done | bytes 278560 | tf_op jit(solution)/shard_map/ppermute | solution.py:386
  (35 shorter events, 8.9 us)
Async XLA Ops:
  0.0 16.2 %collective-permute-start = (bf16[2,8,128,128]{3,2,1,0:T(8,128)(2,1)}, bf16[2,8,128,128]{3,2,1,0:T(8,128)(2,1)S(1)}, u32[]{:S(2)}, u32[]{:S(2)}) collective-permute-start(bf16[2,8,128,128]{3,2,1,0:T(8,128)(2,1)} %video.1), channel_id=1, source_target_pairs={{0,32},{32,64},{64,96},{96,128},{128,160},{160,192},{192,224},{224... | collective-permute-start | bytes 1572872 | tf_op jit(solution)/shard_map/ppermute | solution.py:372
  3.0 19.2 %collective-permute-start.2 = (bf16[2,2,128,128]{3,2,1,0:T(8,128)(2,1)S(1)}, bf16[2,2,128,128]{3,2,1,0:T(8,128)(2,1)S(1)}, u32[]{:S(2)}, u32[]{:S(2)}) collective-permute-start(bf16[2,2,128,128]{3,2,1,0:T(8,128)(2,1)S(1)} %get-tuple-element.41), channel_id=1, source_target_pairs={{0,31},{1,0},{2,1},{3,2},{4,3},{5,4},{6,5},{7,6},{8,7},{9,8},{10,9... | collective-permute-start | bytes 393224 | tf_op jit(solution)/shard_map/ppermute | solution.py:375
  4.3 18.0 %collective-permute-start.4 = (bf16[2,2,128,128]{3,2,1,0:T(8,128)(2,1)S(1)}, bf16[2,2,128,128]{3,2,1,0:T(8,128)(2,1)S(1)}, u32[]{:S(2)}, u32[]{:S(2)}) collective-permute-start(bf16[2,2,128,128]{3,2,1,0:T(8,128)(2,1)S(1)} %get-tuple-element.41), channel_id=1, source_target_pairs={{0,63},{1,32},{2,33},{3,34},{4,35},{5,36},{6,37},{7,38},{8,39},{9,... | collective-permute-start | bytes 393224 | tf_op jit(solution)/shard_map/ppermute | solution.py:383
  12.1 7.0 %collective-permute-start.1 = (bf16[2,1,128,128]{3,2,1,0:T(8,128)(2,1)S(1)}, bf16[2,1,128,128]{3,2,1,0:T(8,128)(2,1)S(1)}, u32[]{:S(2)}, u32[]{:S(2)}) collective-permute-start(bf16[2,1,128,128]{3,2,1,0:T(8,128)(2,1)S(1)} %get-tuple-element.40), channel_id=1, source_target_pairs={{0,1},{1,2},{2,3},{3,4},{4,5},{5,6},{6,7},{7,8},{8,9},{9,10},{10,1... | collective-permute-start | bytes 196616 | tf_op jit(solution)/shard_map/ppermute | solution.py:375
  12.1 10.2 %collective-permute-start.3 = (bf16[2,1,128,128]{3,2,1,0:T(8,128)(2,1)S(1)}, bf16[2,1,128,128]{3,2,1,0:T(8,128)(2,1)S(1)}, u32[]{:S(2)}, u32[]{:S(2)}) collective-permute-start(bf16[2,1,128,128]{3,2,1,0:T(8,128)(2,1)S(1)} %get-tuple-element.40), channel_id=1, source_target_pairs={{0,33},{1,34},{2,35},{3,36},{4,37},{5,38},{6,39},{7,40},{8,41},{9,... | collective-permute-start | bytes 196616 | tf_op jit(solution)/shard_map/ppermute | solution.py:383
  24.8 7.4 %collective-permute-start.5 = (bf16[2,256,256]{2,1,0:T(8,128)(2,1)S(1)}, bf16[2,256,256]{2,1,0:T(8,128)(2,1)S(1)}, u32[]{:S(2)}, u32[]{:S(2)}) collective-permute-start(bf16[2,256,256]{2,1,0:T(8,128)(2,1)S(1)} %get-tuple-element.46), channel_id=1, source_target_pairs={{0,32},{32,64},{64,96},{96,128},{128,160},{160,192},{192,224},{224... | collective-permute-start | bytes 786440 | tf_op jit(solution)/shard_map/ppermute | solution.py:372
  33.1 10.1 %collective-permute-start.9 = (bf16[2,256,256]{2,1,0:T(8,128)(2,1)S(1)}, bf16[2,256,256]{2,1,0:T(8,128)(2,1)S(1)}, u32[]{:S(2)}, u32[]{:S(2)}) collective-permute-start(bf16[2,256,256]{2,1,0:T(8,128)(2,1)S(1)} %get-tuple-element.51.refs_4_), channel_id=1, source_target_pairs={{0,4},{1,5},{2,6},{3,7},{4,8},{5,9},{6,10},{7,11},{8,12},{9,13},{1... | collective-permute-start | bytes 786440 | tf_op jit(solution)/shard_map/ppermute | solution.py:375
  34.8 8.5 %collective-permute-start.10 = (bf16[2,256,256]{2,1,0:T(8,128)(2,1)S(1)}, bf16[2,256,256]{2,1,0:T(8,128)(2,1)S(1)}, u32[]{:S(2)}, u32[]{:S(2)}) collective-permute-start(bf16[2,256,256]{2,1,0:T(8,128)(2,1)S(1)} %get-tuple-element.51.refs_4_), channel_id=1, source_target_pairs={{0,28},{1,29},{2,30},{3,31},{4,0},{5,1},{6,2},{7,3},{8,4},{9,5},{1... | collective-permute-start | bytes 786440 | tf_op jit(solution)/shard_map/ppermute | solution.py:375
  38.6 11.0 %collective-permute-start.7 = (bf16[2,256,256]{2,1,0:T(8,128)(2,1)S(1)}, bf16[2,256,256]{2,1,0:T(8,128)(2,1)S(1)}, u32[]{:S(2)}, u32[]{:S(2)}) collective-permute-start(bf16[2,256,256]{2,1,0:T(8,128)(2,1)S(1)} %get-tuple-element.50.refs_0_), channel_id=1, source_target_pairs={{0,2},{1,3},{2,0},{3,1},{4,6},{5,7},{6,4},{7,5},{8,10},{9,11},{10,... | collective-permute-start | bytes 786440 | tf_op jit(solution)/shard_map/ppermute | solution.py:386
  43.2 7.3 %collective-permute-start.11 = (bf16[2,256,256]{2,1,0:T(8,128)(2,1)S(1)}, bf16[2,256,256]{2,1,0:T(8,128)(2,1)S(1)}, u32[]{:S(2)}, u32[]{:S(2)}) collective-permute-start(bf16[2,256,256]{2,1,0:T(8,128)(2,1)S(1)} %collective-permute-done.9.refs_5_), channel_id=1, source_target_pairs={{0,4},{1,5},{2,6},{3,7},{4,8},{5,9},{6,10},{7,11},{8,12},{9,13},{1... | collective-permute-start | bytes 786440 | tf_op jit(solution)/shard_map/ppermute | solution.py:375
  43.3 7.3 %collective-permute-start.13 = (bf16[2,256,256]{2,1,0:T(8,128)(2,1)S(1)}, bf16[2,256,256]{2,1,0:T(8,128)(2,1)S(1)}, u32[]{:S(2)}, u32[]{:S(2)}) collective-permute-start(bf16[2,256,256]{2,1,0:T(8,128)(2,1)S(1)} %collective-permute-done.10.refs_6_), channel_id=1, source_target_pairs={{0,28},{1,29},{2,30},{3,31},{4,0},{5,1},{6,2},{7,3},{8,4},{9,5},{1... | collective-permute-start | bytes 786440 | tf_op jit(solution)/shard_map/ppermute | solution.py:375
  45.9 7.3 %collective-permute-start.6 = (bf16[2,256,256]{2,1,0:T(8,128)(2,1)S(1)}, bf16[2,256,256]{2,1,0:T(8,128)(2,1)S(1)}, u32[]{:S(2)}, u32[]{:S(2)}) collective-permute-start(bf16[2,256,256]{2,1,0:T(8,128)(2,1)S(1)} %get-tuple-element.50.refs_0_), channel_id=1, source_target_pairs={{0,1},{1,0},{2,3},{3,2},{4,5},{5,4},{6,7},{7,6},{8,9},{9,8},{10,11... | collective-permute-start | bytes 786440 | tf_op jit(solution)/shard_map/ppermute | solution.py:386
  49.6 3.6 %collective-permute-start.8 = (bf16[2,256,256]{2,1,0:T(8,128)(2,1)S(1)}, bf16[2,256,256]{2,1,0:T(8,128)(2,1)S(1)}, u32[]{:S(2)}, u32[]{:S(2)}) collective-permute-start(bf16[2,256,256]{2,1,0:T(8,128)(2,1)S(1)} %collective-permute-done.7.refs_2_), channel_id=1, source_target_pairs={{0,1},{1,0},{2,3},{3,2},{4,5},{5,4},{6,7},{7,6},{8,9},{9,8},{10,11... | collective-permute-start | bytes 786440 | tf_op jit(solution)/shard_map/ppermute | solution.py:386
  50.5 9.0 %collective-permute-start.12 = (bf16[2,256,256]{2,1,0:T(8,128)(2,1)S(1)}, bf16[2,256,256]{2,1,0:T(8,128)(2,1)S(1)}, u32[]{:S(2)}, u32[]{:S(2)}) collective-permute-start(bf16[2,256,256]{2,1,0:T(8,128)(2,1)S(1)} %collective-permute-done.11.refs_2_), channel_id=1, source_target_pairs={{0,4},{1,5},{2,6},{3,7},{4,8},{5,9},{6,10},{7,11},{8,12},{9,13},{1... | collective-permute-start | bytes 786440 | tf_op jit(solution)/shard_map/ppermute | solution.py:375
  50.5 9.0 %collective-permute-start.14 = (bf16[2,256,256]{2,1,0:T(8,128)(2,1)S(1)}, bf16[2,256,256]{2,1,0:T(8,128)(2,1)S(1)}, u32[]{:S(2)}, u32[]{:S(2)}) collective-permute-start(bf16[2,256,256]{2,1,0:T(8,128)(2,1)S(1)} %collective-permute-done.13.refs_3_), channel_id=1, source_target_pairs={{0,28},{1,29},{2,30},{3,31},{4,0},{5,1},{6,2},{7,3},{8,4},{9,5},{1... | collective-permute-start | bytes 786440 | tf_op jit(solution)/shard_map/ppermute | solution.py:375
  59.5 5.7 %collective-permute-start.15 = (bf16[256,256]{1,0:T(8,128)(2,1)S(1)}, bf16[256,256]{1,0:T(8,128)(2,1)S(1)}, u32[]{:S(2)}, u32[]{:S(2)}) collective-permute-start(bf16[256,256]{1,0:T(8,128)(2,1)S(1)} %get-tuple-element.62), channel_id=1, source_target_pairs={{0,4},{1,5},{2,6},{3,7},{4,8},{5,9},{6,10},{7,11},{8,12},{9,13},{1... | collective-permute-start | bytes 393224 | tf_op jit(solution)/shard_map/ppermute | solution.py:375
  59.6 5.6 %collective-permute-start.16 = (bf16[256,256]{1,0:T(8,128)(2,1)S(1)}, bf16[256,256]{1,0:T(8,128)(2,1)S(1)}, u32[]{:S(2)}, u32[]{:S(2)}) collective-permute-start(bf16[256,256]{1,0:T(8,128)(2,1)S(1)} %get-tuple-element.63), channel_id=1, source_target_pairs={{0,28},{1,29},{2,30},{3,31},{4,0},{5,1},{6,2},{7,3},{8,4},{9,5},{1... | collective-permute-start | bytes 393224 | tf_op jit(solution)/shard_map/ppermute | solution.py:375
  66.3 6.2 %collective-permute-start.18 = (f32[2,272,256]{2,1,0:T(8,128)S(1)}, f32[2,272,256]{2,1,0:T(8,128)S(1)}, u32[]{:S(2)}, u32[]{:S(2)}) collective-permute-start(f32[2,272,256]{2,1,0:T(8,128)S(1)} %get-tuple-element.67), channel_id=1, source_target_pairs={{0,1},{1,0},{2,3},{3,2},{4,5},{5,4},{6,7},{7,6},{8,9},{9,8},{10,11... | collective-permute-start | bytes 1671176 | tf_op jit(solution)/shard_map/ppermute | solution.py:386
  72.1 4.8 %collective-permute-start.17 = (f32[2,272,256]{2,1,0:T(8,128)S(1)}, f32[2,272,256]{2,1,0:T(8,128)S(1)}, u32[]{:S(2)}, u32[]{:S(2)}) collective-permute-start(f32[2,272,256]{2,1,0:T(8,128)S(1)} %get-tuple-element.65), channel_id=1, source_target_pairs={{0,1},{1,0},{2,3},{3,2},{4,5},{5,4},{6,7},{7,6},{8,9},{9,8},{10,11... | collective-permute-start | bytes 1671176 | tf_op jit(solution)/shard_map/ppermute | solution.py:386
  72.7 10.9 %collective-permute-start.19 = (bf16[2,272,256]{2,1,0:T(8,128)(2,1)S(1)}, bf16[2,272,256]{2,1,0:T(8,128)(2,1)S(1)}, u32[]{:S(2)}, u32[]{:S(2)}) collective-permute-start(bf16[2,272,256]{2,1,0:T(8,128)(2,1)S(1)} %shard_map.125), channel_id=1, source_target_pairs={{0,2},{1,3},{2,0},{3,1},{4,6},{5,7},{6,4},{7,5},{8,10},{9,11},{10,... | collective-permute-start | bytes 835592 | tf_op jit(solution)/shard_map/ppermute | solution.py:386

commit v4 on v3

--- a/solution.py
+++ b/solution.py
@@ -89,10 +89,18 @@
 
 
 def conv1_taps(taps, weight, acc, base):
-    for kr in range(3):
-        tile = jnp.concatenate([taps[kc, kr * COLS : kr * COLS + SIZE, :] for kc in range(3)], axis=1)
+    for kr, out, row, count in ((1, 0, 0, ROWS), (0, 1, 0, ROWS), (2, 0, 1, ROWS - 1)):
+        tile = jnp.concatenate(
+            [taps[kc, row * COLS : (row + count) * COLS, :] for kc in range(3)], axis=1
+        )
         part = dot(tile, weight[kr].reshape(3 * C2, C2))
-        acc[...] = (acc[...] if kr else base()) + part
+        at = pl.ds(out * COLS, count * COLS)
+        if kr == 1:
+            rest = pl.ds(ROWS * COLS, COLS)
+            acc[at, :] = base(at) + part
+            acc[rest, :] = base(rest)
+        else:
+            acc[at, :] += part
 
 
 def stack(a, b, c, d):
@@ -110,11 +118,6 @@
         copy.wait()
 
 
-def blank_edges(taps):
-    for row in (0, ROWS + 1, ROWS + 2):
-        taps[:, row * COLS : (row + 1) * COLS, :] = jnp.zeros((3, COLS, C2), bf16)
-
-
 def own_kernel(
     video_h, gain_h, bias_h, conv_h, down_h, query_h, key_h, value_h, output_h, down_bias_h, attention_gain_h,
     acc, now, before, down, query, key, value_t, output, gain, down_bias, attention_gain,
@@ -128,10 +131,9 @@
     copies = [pltpu.make_async_copy(src, dst, sem.at[i]) for i, (src, dst) in enumerate(pairs)]
     for copy in copies:
         copy.start()
-    blank_edges(taps)
     for copy in copies[:3]:
         copy.wait()
-    fill_taps(taps, [(row + 1, video, row, None) for row in range(ROWS)], gain, 4)
+    fill_taps(taps, [(row, video, row, None) for row in range(ROWS)], gain, 4)
     copies[3].wait()
     none = jnp.zeros((C1, C1), bf16)
     for kr in range(3):
@@ -140,10 +142,11 @@
             now[kr, kc] = stack(w2, w1, none, w2)
             before[kr, kc] = stack(w0, none, w1, w0)
 
-    def base():
+    def base(at):
         bias2 = jnp.concatenate([bias[...], bias[...]], axis=1)
-        rows = [pair_of(video, i).astype(f32) for i in range(ROWS)] + [jnp.zeros((COLS, C2), f32)]
-        return jnp.concatenate(rows, axis=0) + bias2
+        if at.start:
+            return jnp.broadcast_to(bias2, (COLS, C2))
+        return jnp.concatenate([pair_of(video, i).astype(f32) for i in range(ROWS)], axis=0) + bias2
 
     conv1_taps(taps, now, acc, base)
     copies[4].wait()
@@ -153,9 +156,8 @@
 
 
 def halo_kernel(flags, acc_in, halo, gain, weight, acc, taps):
-    blank_edges(taps)
-    fill_taps(taps, [(row + 1, halo, row, flags[0]) for row in range(ROWS)], gain, 4)
-    conv1_taps(taps, weight, acc, lambda: acc_in[...])
+    fill_taps(taps, [(row, halo, row, flags[0]) for row in range(ROWS)], gain, 4)
+    conv1_taps(taps, weight, acc, lambda at: acc_in[at, :])
 
 
 TAPS = [(kr, kc) for kr in range(3) for kc in range(3)]
@@ -263,13 +265,21 @@
         out[place, C2 + 8 :, :] = jnp.broadcast_to(highest, (8, C2))
 
 
+def early_attend_kernel(frame, own, across, block, plus, minus, key_weight, value_weight_t, state):
+    blocks = [ref.at[frame] for ref in (block, plus, minus)]
+    queries = {0: own[frame], 1: across[frame]}
+    attend(queries, None, lambda g: (state, g), blocks, key_weight, value_weight_t, (0, 1))
+
+
 def first_attend_kernel(
-    frame, own, sibling, across, both, block, plus, minus, key_weight, value_weight_t, queries, state
+    frame, own, sibling, across, both, early, block, plus, minus, key_weight, value_weight_t, queries, state
 ):
     for group, source in enumerate((own, sibling, across, both)):
         queries[group] = source[frame]
+    state[0] = early[0]
+    state[2] = early[1]
     blocks = [ref.at[frame] for ref in (block, plus, minus)]
-    attend(queries, None, lambda g: (state, g), blocks, key_weight, value_weight_t)
+    attend(queries, None, lambda g: (state, g), blocks, key_weight, value_weight_t, (1, 3))
 
 
 def attend_kernel(frame, queries, before, plus, minus, key_weight, value_weight_t, state):
@@ -399,7 +409,7 @@
     far_above, far_below = diagonal(bottom, 1), diagonal(top, -1)
 
     square = (C2, C2)
-    taps = pltpu.VMEM((3, (ROWS + 3) * COLS, C2), bf16)
+    taps = pltpu.VMEM((3, ROWS * COLS, C2), bf16)
     whole = ((SIZE, C2), f32)
     prepared = (3, 3) + square
     (
@@ -460,39 +470,52 @@
         nbytes=2_000_000,
     )
     plus, minus = [along(normed, 4)], [along(normed, -4)]
-    for step in range(2):
-        plus.append(along(plus[step], 4))
-        minus.append(along(minus[step], -4))
+    plus.append(along(plus[0], 4))
+    minus.append(along(minus[0], -4))
     sibling, across = swap(own, 1), swap(own, 2)
     both = swap(across, 1)
     state = [((GROUPS, STATE, C2), f32)]
     flops = 2 * QUERIES * 256 * (512 + 2 * GROUPS * QUERIES)
     carry, queries = [0, 0], [0, 0]
     weights = [key_weight, value_weight]
+    early = [0, 0]
+    for frame in range(2):
+        (early[frame],) = call(
+            lambda *refs: early_attend_kernel(frame, *refs),
+            [((2, STATE, C2), f32)],
+            [own, across, normed, plus[0], minus[0]] + weights,
+            flops=2 * flops,
+            nbytes=3_000_000,
+        )
+    (sent, other), early = lax.optimization_barrier(((plus[1], minus[1]), early))
+    plus.append(along(sent, 4))
+    minus.append(along(other, -4))
     for frame in range(2):
         queries[frame], carry[frame] = call(
             lambda *refs: first_attend_kernel(frame, *refs),
             [((GROUPS, QUERIES, C2), bf16)] + state,
-            [own, sibling, across, both, normed, plus[0], minus[0]] + weights,
-            flops=3 * flops,
+            [own, sibling, across, both, early[frame], normed, plus[0], minus[0]] + weights,
+            flops=2 * flops,
             nbytes=4_000_000,
         )
-    def step_on(step):
-        for frame in range(2):
-            (carry[frame],) = call(
-                lambda *refs: attend_kernel(frame, *refs),
-                state,
-                [queries[frame], carry[frame], plus[step], minus[step]] + weights,
-                aliases={1: 0},
-                flops=2 * flops,
-                nbytes=4_000_000,
-            )
-
-    step_on(1)
+
+    def step_on(step, frame):
+        (carry[frame],) = call(
+            lambda *refs: attend_kernel(frame, *refs),
+            state,
+            [queries[frame], carry[frame], plus[step], minus[step]] + weights,
+            aliases={1: 0},
+            flops=2 * flops,
+            nbytes=4_000_000,
+        )
+
+    step_on(1, 0)
     (plus[2], minus[2]), carry = lax.optimization_barrier(((plus[2], minus[2]), carry))
     ends = call(cut_kernel, [((QUERIES, C2), bf16)] * 2, [plus[2], minus[2]], nbytes=500_000)
     ends = [along(ends[0], 4), along(ends[1], -4)]
-    step_on(2)
+    step_on(1, 1)
+    step_on(2, 0)
+    step_on(2, 1)
     pair = ((2, STATE, C2), f32)
 
     def finish(groups):

time: 84.8 us -> 84.4 us (level)
  starting transfers between devices: 44 us -> 41.3 us
  waiting for transfers between devices: 15.8 us -> 17.4 us
    ppermute x6, starting transfers between devices: 18.1 us -> 15.3 us  [swap(): return lax.ppermute(x, 'space', [(i, i ^ bit) for i in range(space)])]
    ppermute x10, waiting for transfers between devices: 0.03 us -> 1.48 us  [along(): lax.ppermute(x, 'space', [(i, (i + distance) % space) for i in range(spac...]
    pallas_call x18 -> x20, Pallas kernels: 24.6 us -> 25.4 us  [call(): pl.pallas_call(kernel, out_shape=[jax.ShapeDtypeStruct(s, d) for s, d in...]
  transfers between devices with their start and end apart: 20 -> 20, of which waited for: 4 -> 6; matrix products, arithmetic and copies ran while one was open for 0% -> 0% of each run, Pallas kernels for 22% -> 23%
where the time goes in v4:
time: 84.4 us; the launch traced here: 84.3 us
  starting transfers between devices  41.3 us (49%)
  Pallas kernels  25.4 us (30%)
  waiting for transfers between devices  17.4 us (21%)
    pallas_call x20, Pallas kernels, call(): pl.pallas_call(kernel, out_shape=[jax.ShapeDtypeStruct(s, d) for s, d in...  25.4 us
    ppermute x6, starting transfers between devices, swap(): return lax.ppermute(x, 'space', [(i, i ^ bit) for i in range(space)])  15.3 us
    ppermute x10, starting transfers between devices, along(): lax.ppermute(x, 'space', [(i, (i + distance) % space) for i in range(spac...  14.9 us
    ppermute x2, starting transfers between devices, diagonal(): return lax.ppermute(x, ('tm', 'space'), route)  7.78 us
    ppermute x6, waiting for transfers between devices, swap(): return lax.ppermute(x, 'space', [(i, i ^ bit) for i in range(space)])  6.94 us
    ppermute x2, waiting for transfers between devices, next_frames(): return lax.ppermute(x, 'tm', [(i, (i + 1) % times) for i in range(times)])  5.76 us
    ppermute x2, starting transfers between devices, next_frames(): return lax.ppermute(x, 'tm', [(i, (i + 1) % times) for i in range(times)])  3.28 us
    ppermute x2, waiting for transfers between devices, diagonal(): return lax.ppermute(x, ('tm', 'space'), route)  3.24 us
  transfers between devices with their start and end apart: 20, of which 6 were waited for; matrix products, arithmetic and copies ran while one was open for 0% of the time, Pallas kernels for 23%

profile of v4, /device:TPU:1, one launch (start us, length us, event | category | flops | bytes accessed | tf_op | source)
XLA Modules:
  0.0 84.3 jit_solution(2004894507358019147)
XLA Ops:
  0.0 2.0 %collective-permute-start = (bf16[2,8,128,128]{3,2,1,0:T(8,128)(2,1)}, bf16[2,8,128,128]{3,2,1,0:T(8,128)(2,1)S(1)}, u32[]{:S(2)}, u32[]{:S(2)}) collective-permute-start(bf16[2,8,128,128]{3,2,1,0:T(8,128)(2,1)} %video.1), channel_id=1, source_target_pairs={{0,32},{32,64},{64,96},{96,128},{128,160},{160,192},{192,224},{224... | collective-permute-start | bytes 1572872 | tf_op jit(solution)/shard_map/ppermute | solution.py:382
  3.0 1.3 %collective-permute-start.2 = (bf16[2,2,128,128]{3,2,1,0:T(8,128)(2,1)S(1)}, bf16[2,2,128,128]{3,2,1,0:T(8,128)(2,1)S(1)}, u32[]{:S(2)}, u32[]{:S(2)}) collective-permute-start(bf16[2,2,128,128]{3,2,1,0:T(8,128)(2,1)S(1)} %get-tuple-element.45), channel_id=1, source_target_pairs={{0,31},{1,0},{2,1},{3,2},{4,3},{5,4},{6,5},{7,6},{8,7},{9,8},{10,9... | collective-permute-start | bytes 393224 | tf_op jit(solution)/shard_map/ppermute | solution.py:385
  4.3 7.8 %collective-permute-start.4 = (bf16[2,2,128,128]{3,2,1,0:T(8,128)(2,1)S(1)}, bf16[2,2,128,128]{3,2,1,0:T(8,128)(2,1)S(1)}, u32[]{:S(2)}, u32[]{:S(2)}) collective-permute-start(bf16[2,2,128,128]{3,2,1,0:T(8,128)(2,1)S(1)} %get-tuple-element.45), channel_id=1, source_target_pairs={{0,63},{1,32},{2,33},{3,34},{4,35},{5,36},{6,37},{7,38},{8,39},{9,... | collective-permute-start | bytes 393224 | tf_op jit(solution)/shard_map/ppermute | solution.py:393
  12.1 3.8 %shard_map.109 = (f32[1152,256]{1,0:T(8,128)S(1)}, bf16[3,3,256,256]{3,2,1,0:T(8,128)(2,1)S(1)}, bf16[3,3,256,256]{3,2,1,0:T(8,128)(2,1)S(1)}, bf16[3,3,3,128,25...) custom-call(bf16[2,8,128,128]{3,2,1,0:T(8,128)(2,1)} %video.1, ...), custom_call_target="tpu_custom_call" | custom-call | flops 1358954496 | bytes 6000000 | tf_op jit(solution)/shard_map/pallas_call | solution.py:28
  16.2 2.8 %shard_map.110.acc = f32[1152,256]{1,0:T(8,128)S(1)} custom-call(f32[3]{0:T(128)S(1)} %add_convert_fusion.flags, f32[1152,256]{1,0:T(8,128)S(1)} %get-tuple-element.41.acc_in, bf16[2,8,128,128]{3,2,1,0:T(8,128)(2,1)S(1)} %collective-permute-done.halo, f32[1,128]{1,0:T(1,128)S(1)} %get-tuple-element.42.gain, ...), custom_call_target="tpu_custom_call" | custom-call | flops 1358954496 | bytes 5000000 | tf_op jit(solution)/shard_map/pallas_call | solution.py:28
  19.0 3.2 %collective-permute-done.3.far_above = bf16[2,1,128,128]{3,2,1,0:T(8,128)(2,1)S(1)} collective-permute-done((bf16[2,1,128,128]{3,2,1,0:T(8,128)(2,1)S(1)}, bf16[2,1,128,128]{3,2,1,0:T(8,128)(2,1)S(1)}, u32[]{:S(2)}, u32[]{:S(2)}) %collective-permute-start.3) | collective-permute-done | bytes 65568 | tf_op jit(solution)/shard_map/ppermute | solution.py:393
  22.2 2.5 %shard_map.112 = (bf16[2,256,256]{2,1,0:T(8,128)(2,1)S(1)}, bf16[3,576,256]{2,1,0:T(8,128)(2,1)S(1)}) custom-call(f32[3]{0:T(128)S(1)} %add_convert_fusion.flags, f32[1152,256]{1,0:T(8,128)S(1)} %shard_map.110.acc, bf16[2,1,128,128]{3,2,1,0:T(8,128)(2,1)S(1)} %collective-permute-done.1.above, bf16[2,2,128,128]{3,2,1,0:T(8,128)(2,1)S(1)} %collective-permute-done.2.below, ...), custom_call_target="tpu_custom_call" | custom-call | flops 603979776 | bytes 5000000 | tf_op jit(solution)/shard_map/pallas_call | solution.py:28
  24.7 1.2 %collective-permute-start.5 = (bf16[2,256,256]{2,1,0:T(8,128)(2,1)S(1)}, bf16[2,256,256]{2,1,0:T(8,128)(2,1)S(1)}, u32[]{:S(2)}, u32[]{:S(2)}) collective-permute-start(bf16[2,256,256]{2,1,0:T(8,128)(2,1)S(1)} %get-tuple-element.50), channel_id=1, source_target_pairs={{0,32},{32,64},{64,96},{96,128},{128,160},{160,192},{192,224},{224... | collective-permute-start | bytes 786440 | tf_op jit(solution)/shard_map/ppermute | solution.py:382
  26.6 5.5 %collective-permute-done.5.received = bf16[2,256,256]{2,1,0:T(8,128)(2,1)S(1)} collective-permute-done((bf16[2,256,256]{2,1,0:T(8,128)(2,1)S(1)}, bf16[2,256,256]{2,1,0:T(8,128)(2,1)S(1)}, u32[]{:S(2)}, u32[]{:S(2)}) %collective-permute-start.5) | collective-permute-done | bytes 262176 | tf_op jit(solution)/shard_map/ppermute | solution.py:382
  33.0 1.7 %collective-permute-start.9 = (bf16[2,256,256]{2,1,0:T(8,128)(2,1)S(1)}, bf16[2,256,256]{2,1,0:T(8,128)(2,1)S(1)}, u32[]{:S(2)}, u32[]{:S(2)}) collective-permute-start(bf16[2,256,256]{2,1,0:T(8,128)(2,1)S(1)} %get-tuple-element.55.refs_2_.refs_5_), channel_id=1, source_target_pairs={{0,4},{1,5},{2,6},{3,7},{4,8},{5,9},{6,10},{7,11},{8,12},{9,13},{1... | collective-permute-start | bytes 786440 | tf_op jit(solution)/shard_map/ppermute | solution.py:385
  34.7 3.8 %collective-permute-start.11 = (bf16[2,256,256]{2,1,0:T(8,128)(2,1)S(1)}, bf16[2,256,256]{2,1,0:T(8,128)(2,1)S(1)}, u32[]{:S(2)}, u32[]{:S(2)}) collective-permute-start(bf16[2,256,256]{2,1,0:T(8,128)(2,1)S(1)} %get-tuple-element.55.refs_2_.refs_5_), channel_id=1, source_target_pairs={{0,28},{1,29},{2,30},{3,31},{4,0},{5,1},{6,2},{7,3},{8,4},{9,5},{1... | collective-permute-start | bytes 786440 | tf_op jit(solution)/shard_map/ppermute | solution.py:385
  38.5 4.7 %collective-permute-start.7 = (bf16[2,256,256]{2,1,0:T(8,128)(2,1)S(1)}, bf16[2,256,256]{2,1,0:T(8,128)(2,1)S(1)}, u32[]{:S(2)}, u32[]{:S(2)}) collective-permute-start(bf16[2,256,256]{2,1,0:T(8,128)(2,1)S(1)} %get-tuple-element.54.refs_0_), channel_id=1, source_target_pairs={{0,2},{1,3},{2,0},{3,1},{4,6},{5,7},{6,4},{7,5},{8,10},{9,11},{10,... | collective-permute-start | bytes 786440 | tf_op jit(solution)/shard_map/ppermute | solution.py:396
  43.2 2.7 %collective-permute-start.12 = (bf16[2,256,256]{2,1,0:T(8,128)(2,1)S(1)}, bf16[2,256,256]{2,1,0:T(8,128)(2,1)S(1)}, u32[]{:S(2)}, u32[]{:S(2)}) collective-permute-start(bf16[2,256,256]{2,1,0:T(8,128)(2,1)S(1)} %collective-permute-done.11.refs_4_.refs_7_), channel_id=1, source_target_pairs={{0,28},{1,29},{2,30},{3,31},{4,0},{5,1},{6,2},{7,3},{8,4},{9,5},{1... | collective-permute-start | bytes 786440 | tf_op jit(solution)/shard_map/ppermute | solution.py:385
  45.9 3.6 %collective-permute-start.6 = (bf16[2,256,256]{2,1,0:T(8,128)(2,1)S(1)}, bf16[2,256,256]{2,1,0:T(8,128)(2,1)S(1)}, u32[]{:S(2)}, u32[]{:S(2)}) collective-permute-start(bf16[2,256,256]{2,1,0:T(8,128)(2,1)S(1)} %get-tuple-element.54.refs_0_), channel_id=1, source_target_pairs={{0,1},{1,0},{2,3},{3,2},{4,5},{5,4},{6,7},{7,6},{8,9},{9,8},{10,11... | collective-permute-start | bytes 786440 | tf_op jit(solution)/shard_map/ppermute | solution.py:396
  52.7 2.7 %collective-permute-start.14 = (bf16[2,256,256]{2,1,0:T(8,128)(2,1)S(1)}, bf16[2,256,256]{2,1,0:T(8,128)(2,1)S(1)}, u32[]{:S(2)}, u32[]{:S(2)}) collective-permute-start(bf16[2,256,256]{2,1,0:T(8,128)(2,1)S(1)} %collective-permute-done.12.refs_3_), channel_id=1, source_target_pairs={{0,28},{1,29},{2,30},{3,31},{4,0},{5,1},{6,2},{7,3},{8,4},{9,5},{1... | collective-permute-start | bytes 786440 | tf_op jit(solution)/shard_map/ppermute | solution.py:385
  57.7 1.5 %shard_map.119.refs_1_ = f32[4,272,256]{2,1,0:T(8,128)S(1)} custom-call(bf16[4,256,256]{2,1,0:T(8,128)(2,1)S(1)} %get-tuple-element.59.refs_0_, f32[4,272,256]{2,1,0:T(8,128)S(1)} %get-tuple-element.64.refs_1_, bf16[2,256,256]{2,1,0:T(8,128)(2,1)S(1)} %collective-permute-done.10.refs_2_, ...), custom_call_target="tpu_custom_call", output_to_operand_aliasing={{}: (1, {})} | custom-call | flops 671088640 | bytes 4000000 | tf_op jit(solution)/shard_map/pallas_call | solution.py:28
  59.2 1.5 %collective-permute-done.13.refs_2_.plus = bf16[2,256,256]{2,1,0:T(8,128)(2,1)S(1)} collective-permute-done((bf16[2,256,256]{2,1,0:T(8,128)(2,1)S(1)}, bf16[2,256,256]{2,1,0:T(8,128)(2,1)S(1)}, u32[]{:S(2)}, u32[]{:S(2)}) %collective-permute-start.13) | collective-permute-done | bytes 262176 | tf_op jit(solution)/shard_map/ppermute | solution.py:385
  60.7 2.7 %collective-permute-start.16 = (bf16[256,256]{1,0:T(8,128)(2,1)S(1)}, bf16[256,256]{1,0:T(8,128)(2,1)S(1)}, u32[]{:S(2)}, u32[]{:S(2)}) collective-permute-start(bf16[256,256]{1,0:T(8,128)(2,1)S(1)} %get-tuple-element.71), channel_id=1, source_target_pairs={{0,28},{1,29},{2,30},{3,31},{4,0},{5,1},{6,2},{7,3},{8,4},{9,5},{1... | collective-permute-start | bytes 393224 | tf_op jit(solution)/shard_map/ppermute | solution.py:385
  63.4 1.4 %shard_map.121.refs_1_ = f32[4,272,256]{2,1,0:T(8,128)S(1)} custom-call(bf16[4,256,256]{2,1,0:T(8,128)(2,1)S(1)} %get-tuple-element.61.refs_0_.refs_1_, f32[4,272,256]{2,1,0:T(8,128)S(1)} %get-tuple-element.69.refs_1_, bf16[2,256,256]{2,1,0:T(8,128)(2,1)S(1)} %collective-permute-done.10.refs_2_, ...), custom_call_target="tpu_custom_call", output_to_operand_aliasing={{}: (1, {})} | custom-call | flops 671088640 | bytes 4000000 | tf_op jit(solution)/shard_map/pallas_call | solution.py:28
  64.9 1.5 %shard_map.122.refs_3_ = f32[4,272,256]{2,1,0:T(8,128)S(1)} custom-call(bf16[4,256,256]{2,1,0:T(8,128)(2,1)S(1)} %get-tuple-element.61.refs_0_.refs_1_, f32[4,272,256]{2,1,0:T(8,128)S(1)} %shard_map.121.refs_1_, bf16[2,256,256]{2,1,0:T(8,128)(2,1)S(1)} %collective-permute-done.13.refs_2_.plus, ...), custom_call_target="tpu_custom_call", output_to_operand_aliasing={{}: (1, {})} | custom-call | flops 671088640 | bytes 4000000 | tf_op jit(solution)/shard_map/pallas_call | solution.py:28
  66.3 1.5 %shard_map.120.refs_2_ = f32[4,272,256]{2,1,0:T(8,128)S(1)} custom-call(bf16[4,256,256]{2,1,0:T(8,128)(2,1)S(1)} %get-tuple-element.59.refs_0_, f32[4,272,256]{2,1,0:T(8,128)S(1)} %shard_map.119.refs_1_, bf16[2,256,256]{2,1,0:T(8,128)(2,1)S(1)} %collective-permute-done.13.refs_2_.plus, ...), custom_call_target="tpu_custom_call", output_to_operand_aliasing={{}: (1, {})} | custom-call | flops 671088640 | bytes 4000000 | tf_op jit(solution)/shard_map/pallas_call | solution.py:28
  68.9 2.7 %collective-permute-start.18 = (f32[2,272,256]{2,1,0:T(8,128)S(1)}, f32[2,272,256]{2,1,0:T(8,128)S(1)}, u32[]{:S(2)}, u32[]{:S(2)}) collective-permute-start(f32[2,272,256]{2,1,0:T(8,128)S(1)} %get-tuple-element.75), channel_id=1, source_target_pairs={{0,1},{1,0},{2,3},{3,2},{4,5},{5,4},{6,7},{7,6},{8,9},{9,8},{10,11... | collective-permute-start | bytes 1671176 | tf_op jit(solution)/shard_map/ppermute | solution.py:396
  73.3 3.2 %collective-permute-start.19 = (bf16[2,272,256]{2,1,0:T(8,128)(2,1)S(1)}, bf16[2,272,256]{2,1,0:T(8,128)(2,1)S(1)}, u32[]{:S(2)}, u32[]{:S(2)}) collective-permute-start(bf16[2,272,256]{2,1,0:T(8,128)(2,1)S(1)} %shard_map.127), channel_id=1, source_target_pairs={{0,2},{1,3},{2,0},{3,1},{4,6},{5,7},{6,4},{7,5},{8,10},{9,11},{10,... | collective-permute-start | bytes 835592 | tf_op jit(solution)/shard_map/ppermute | solution.py:396
  76.6 6.5 %collective-permute-done.19.received = bf16[2,272,256]{2,1,0:T(8,128)(2,1)S(1)} collective-permute-done((bf16[2,272,256]{2,1,0:T(8,128)(2,1)S(1)}, bf16[2,272,256]{2,1,0:T(8,128)(2,1)S(1)}, u32[]{:S(2)}, u32[]{:S(2)}) %collective-permute-start.19) | collective-permute-done | bytes 278560 | tf_op jit(solution)/shard_map/ppermute | solution.py:396
  (37 shorter events, 12.5 us)
Async XLA Ops:
  0.0 16.2 %collective-permute-start = (bf16[2,8,128,128]{3,2,1,0:T(8,128)(2,1)}, bf16[2,8,128,128]{3,2,1,0:T(8,128)(2,1)S(1)}, u32[]{:S(2)}, u32[]{:S(2)}) collective-permute-start(bf16[2,8,128,128]{3,2,1,0:T(8,128)(2,1)} %video.1), channel_id=1, source_target_pairs={{0,32},{32,64},{64,96},{96,128},{128,160},{160,192},{192,224},{224... | collective-permute-start | bytes 1572872 | tf_op jit(solution)/shard_map/ppermute | solution.py:382
  3.0 19.2 %collective-permute-start.2 = (bf16[2,2,128,128]{3,2,1,0:T(8,128)(2,1)S(1)}, bf16[2,2,128,128]{3,2,1,0:T(8,128)(2,1)S(1)}, u32[]{:S(2)}, u32[]{:S(2)}) collective-permute-start(bf16[2,2,128,128]{3,2,1,0:T(8,128)(2,1)S(1)} %get-tuple-element.45), channel_id=1, source_target_pairs={{0,31},{1,0},{2,1},{3,2},{4,3},{5,4},{6,5},{7,6},{8,7},{9,8},{10,9... | collective-permute-start | bytes 393224 | tf_op jit(solution)/shard_map/ppermute | solution.py:385
  4.3 18.0 %collective-permute-start.4 = (bf16[2,2,128,128]{3,2,1,0:T(8,128)(2,1)S(1)}, bf16[2,2,128,128]{3,2,1,0:T(8,128)(2,1)S(1)}, u32[]{:S(2)}, u32[]{:S(2)}) collective-permute-start(bf16[2,2,128,128]{3,2,1,0:T(8,128)(2,1)S(1)} %get-tuple-element.45), channel_id=1, source_target_pairs={{0,63},{1,32},{2,33},{3,34},{4,35},{5,36},{6,37},{7,38},{8,39},{9,... | collective-permute-start | bytes 393224 | tf_op jit(solution)/shard_map/ppermute | solution.py:393
  12.1 6.9 %collective-permute-start.1 = (bf16[2,1,128,128]{3,2,1,0:T(8,128)(2,1)S(1)}, bf16[2,1,128,128]{3,2,1,0:T(8,128)(2,1)S(1)}, u32[]{:S(2)}, u32[]{:S(2)}) collective-permute-start(bf16[2,1,128,128]{3,2,1,0:T(8,128)(2,1)S(1)} %get-tuple-element.44), channel_id=1, source_target_pairs={{0,1},{1,2},{2,3},{3,4},{4,5},{5,6},{6,7},{7,8},{8,9},{9,10},{10,1... | collective-permute-start | bytes 196616 | tf_op jit(solution)/shard_map/ppermute | solution.py:385
  12.1 10.2 %collective-permute-start.3 = (bf16[2,1,128,128]{3,2,1,0:T(8,128)(2,1)S(1)}, bf16[2,1,128,128]{3,2,1,0:T(8,128)(2,1)S(1)}, u32[]{:S(2)}, u32[]{:S(2)}) collective-permute-start(bf16[2,1,128,128]{3,2,1,0:T(8,128)(2,1)S(1)} %get-tuple-element.44), channel_id=1, source_target_pairs={{0,33},{1,34},{2,35},{3,36},{4,37},{5,38},{6,39},{7,40},{8,41},{9,... | collective-permute-start | bytes 196616 | tf_op jit(solution)/shard_map/ppermute | solution.py:393
  24.7 7.4 %collective-permute-start.5 = (bf16[2,256,256]{2,1,0:T(8,128)(2,1)S(1)}, bf16[2,256,256]{2,1,0:T(8,128)(2,1)S(1)}, u32[]{:S(2)}, u32[]{:S(2)}) collective-permute-start(bf16[2,256,256]{2,1,0:T(8,128)(2,1)S(1)} %get-tuple-element.50), channel_id=1, source_target_pairs={{0,32},{32,64},{64,96},{96,128},{128,160},{160,192},{192,224},{224... | collective-permute-start | bytes 786440 | tf_op jit(solution)/shard_map/ppermute | solution.py:382
  33.0 10.1 %collective-permute-start.9 = (bf16[2,256,256]{2,1,0:T(8,128)(2,1)S(1)}, bf16[2,256,256]{2,1,0:T(8,128)(2,1)S(1)}, u32[]{:S(2)}, u32[]{:S(2)}) collective-permute-start(bf16[2,256,256]{2,1,0:T(8,128)(2,1)S(1)} %get-tuple-element.55.refs_2_.refs_5_), channel_id=1, source_target_pairs={{0,4},{1,5},{2,6},{3,7},{4,8},{5,9},{6,10},{7,11},{8,12},{9,13},{1... | collective-permute-start | bytes 786440 | tf_op jit(solution)/shard_map/ppermute | solution.py:385
  34.7 8.5 %collective-permute-start.11 = (bf16[2,256,256]{2,1,0:T(8,128)(2,1)S(1)}, bf16[2,256,256]{2,1,0:T(8,128)(2,1)S(1)}, u32[]{:S(2)}, u32[]{:S(2)}) collective-permute-start(bf16[2,256,256]{2,1,0:T(8,128)(2,1)S(1)} %get-tuple-element.55.refs_2_.refs_5_), channel_id=1, source_target_pairs={{0,28},{1,29},{2,30},{3,31},{4,0},{5,1},{6,2},{7,3},{8,4},{9,5},{1... | collective-permute-start | bytes 786440 | tf_op jit(solution)/shard_map/ppermute | solution.py:385
  38.5 11.0 %collective-permute-start.7 = (bf16[2,256,256]{2,1,0:T(8,128)(2,1)S(1)}, bf16[2,256,256]{2,1,0:T(8,128)(2,1)S(1)}, u32[]{:S(2)}, u32[]{:S(2)}) collective-permute-start(bf16[2,256,256]{2,1,0:T(8,128)(2,1)S(1)} %get-tuple-element.54.refs_0_), channel_id=1, source_target_pairs={{0,2},{1,3},{2,0},{3,1},{4,6},{5,7},{6,4},{7,5},{8,10},{9,11},{10,... | collective-permute-start | bytes 786440 | tf_op jit(solution)/shard_map/ppermute | solution.py:396
  43.2 9.5 %collective-permute-start.10 = (bf16[2,256,256]{2,1,0:T(8,128)(2,1)S(1)}, bf16[2,256,256]{2,1,0:T(8,128)(2,1)S(1)}, u32[]{:S(2)}, u32[]{:S(2)}) collective-permute-start(bf16[2,256,256]{2,1,0:T(8,128)(2,1)S(1)} %collective-permute-done.9.refs_3_.refs_6_), channel_id=1, source_target_pairs={{0,4},{1,5},{2,6},{3,7},{4,8},{5,9},{6,10},{7,11},{8,12},{9,13},{1... | collective-permute-start | bytes 786440 | tf_op jit(solution)/shard_map/ppermute | solution.py:385
  43.2 9.5 %collective-permute-start.12 = (bf16[2,256,256]{2,1,0:T(8,128)(2,1)S(1)}, bf16[2,256,256]{2,1,0:T(8,128)(2,1)S(1)}, u32[]{:S(2)}, u32[]{:S(2)}) collective-permute-start(bf16[2,256,256]{2,1,0:T(8,128)(2,1)S(1)} %collective-permute-done.11.refs_4_.refs_7_), channel_id=1, source_target_pairs={{0,28},{1,29},{2,30},{3,31},{4,0},{5,1},{6,2},{7,3},{8,4},{9,5},{1... | collective-permute-start | bytes 786440 | tf_op jit(solution)/shard_map/ppermute | solution.py:385
  45.9 9.5 %collective-permute-start.6 = (bf16[2,256,256]{2,1,0:T(8,128)(2,1)S(1)}, bf16[2,256,256]{2,1,0:T(8,128)(2,1)S(1)}, u32[]{:S(2)}, u32[]{:S(2)}) collective-permute-start(bf16[2,256,256]{2,1,0:T(8,128)(2,1)S(1)} %get-tuple-element.54.refs_0_), channel_id=1, source_target_pairs={{0,1},{1,0},{2,3},{3,2},{4,5},{5,4},{6,7},{7,6},{8,9},{9,8},{10,11... | collective-permute-start | bytes 786440 | tf_op jit(solution)/shard_map/ppermute | solution.py:396
  49.5 5.9 %collective-permute-start.8 = (bf16[2,256,256]{2,1,0:T(8,128)(2,1)S(1)}, bf16[2,256,256]{2,1,0:T(8,128)(2,1)S(1)}, u32[]{:S(2)}, u32[]{:S(2)}) collective-permute-start(bf16[2,256,256]{2,1,0:T(8,128)(2,1)S(1)} %collective-permute-done.7.refs_1_.refs_2_), channel_id=1, source_target_pairs={{0,1},{1,0},{2,3},{3,2},{4,5},{5,4},{6,7},{7,6},{8,9},{9,8},{10,11... | collective-permute-start | bytes 786440 | tf_op jit(solution)/shard_map/ppermute | solution.py:396
  52.6 8.0 %collective-permute-start.13 = (bf16[2,256,256]{2,1,0:T(8,128)(2,1)S(1)}, bf16[2,256,256]{2,1,0:T(8,128)(2,1)S(1)}, u32[]{:S(2)}, u32[]{:S(2)}) collective-permute-start(bf16[2,256,256]{2,1,0:T(8,128)(2,1)S(1)} %collective-permute-done.10.refs_2_), channel_id=1, source_target_pairs={{0,4},{1,5},{2,6},{3,7},{4,8},{5,9},{6,10},{7,11},{8,12},{9,13},{1... | collective-permute-start | bytes 786440 | tf_op jit(solution)/shard_map/ppermute | solution.py:385
  52.7 7.9 %collective-permute-start.14 = (bf16[2,256,256]{2,1,0:T(8,128)(2,1)S(1)}, bf16[2,256,256]{2,1,0:T(8,128)(2,1)S(1)}, u32[]{:S(2)}, u32[]{:S(2)}) collective-permute-start(bf16[2,256,256]{2,1,0:T(8,128)(2,1)S(1)} %collective-permute-done.12.refs_3_), channel_id=1, source_target_pairs={{0,28},{1,29},{2,30},{3,31},{4,0},{5,1},{6,2},{7,3},{8,4},{9,5},{1... | collective-permute-start | bytes 786440 | tf_op jit(solution)/shard_map/ppermute | solution.py:385
  60.7 7.1 %collective-permute-start.15 = (bf16[256,256]{1,0:T(8,128)(2,1)S(1)}, bf16[256,256]{1,0:T(8,128)(2,1)S(1)}, u32[]{:S(2)}, u32[]{:S(2)}) collective-permute-start(bf16[256,256]{1,0:T(8,128)(2,1)S(1)} %get-tuple-element.70), channel_id=1, source_target_pairs={{0,4},{1,5},{2,6},{3,7},{4,8},{5,9},{6,10},{7,11},{8,12},{9,13},{1... | collective-permute-start | bytes 393224 | tf_op jit(solution)/shard_map/ppermute | solution.py:385
  60.7 7.1 %collective-permute-start.16 = (bf16[256,256]{1,0:T(8,128)(2,1)S(1)}, bf16[256,256]{1,0:T(8,128)(2,1)S(1)}, u32[]{:S(2)}, u32[]{:S(2)}) collective-permute-start(bf16[256,256]{1,0:T(8,128)(2,1)S(1)} %get-tuple-element.71), channel_id=1, source_target_pairs={{0,28},{1,29},{2,30},{3,31},{4,0},{5,1},{6,2},{7,3},{8,4},{9,5},{1... | collective-permute-start | bytes 393224 | tf_op jit(solution)/shard_map/ppermute | solution.py:385
  68.9 4.3 %collective-permute-start.18 = (f32[2,272,256]{2,1,0:T(8,128)S(1)}, f32[2,272,256]{2,1,0:T(8,128)S(1)}, u32[]{:S(2)}, u32[]{:S(2)}) collective-permute-start(f32[2,272,256]{2,1,0:T(8,128)S(1)} %get-tuple-element.75), channel_id=1, source_target_pairs={{0,1},{1,0},{2,3},{3,2},{4,5},{5,4},{6,7},{7,6},{8,9},{9,8},{10,11... | collective-permute-start | bytes 1671176 | tf_op jit(solution)/shard_map/ppermute | solution.py:396
  72.7 3.8 %collective-permute-start.17 = (f32[2,272,256]{2,1,0:T(8,128)S(1)}, f32[2,272,256]{2,1,0:T(8,128)S(1)}, u32[]{:S(2)}, u32[]{:S(2)}) collective-permute-start(f32[2,272,256]{2,1,0:T(8,128)S(1)} %get-tuple-element.73), channel_id=1, source_target_pairs={{0,1},{1,0},{2,3},{3,2},{4,5},{5,4},{6,7},{7,6},{8,9},{9,8},{10,11... | collective-permute-start | bytes 1671176 | tf_op jit(solution)/shard_map/ppermute | solution.py:396
  73.3 9.9 %collective-permute-start.19 = (bf16[2,272,256]{2,1,0:T(8,128)(2,1)S(1)}, bf16[2,272,256]{2,1,0:T(8,128)(2,1)S(1)}, u32[]{:S(2)}, u32[]{:S(2)}) collective-permute-start(bf16[2,272,256]{2,1,0:T(8,128)(2,1)S(1)} %shard_map.127), channel_id=1, source_target_pairs={{0,2},{1,3},{2,0},{3,1},{4,6},{5,7},{6,4},{7,5},{8,10},{9,11},{10,... | collective-permute-start | bytes 835592 | tf_op jit(solution)/shard_map/ppermute | solution.py:396

commit v5 on v4

--- a/solution.py
+++ b/solution.py
@@ -155,11 +155,6 @@
         copy.wait()
 
 
-def halo_kernel(flags, acc_in, halo, gain, weight, acc, taps):
-    fill_taps(taps, [(row, halo, row, flags[0]) for row in range(ROWS)], gain, 4)
-    conv1_taps(taps, weight, acc, lambda at: acc_in[at, :])
-
-
 TAPS = [(kr, kc) for kr in range(3) for kc in range(3)]
 
 
@@ -169,44 +164,14 @@
     return jnp.concatenate(tiles, axis=1)
 
 
-def down_weights(down, times):
-    return jnp.concatenate([down[kt, kr, kc] for kr, kc in TAPS for kt in times], axis=0)
-
-
-def sum_kernel(
-    flags, acc, above, below, far_above, far_below, gain, now, before, down,
-    send, half_taps, taps, wide,
-):
-    past = flags[0]
-    edges = [(0, above, 0, flags[1]), (1, below, 0, flags[2]), (2, below, 1, flags[2])]
-    far = [(3, far_above, 0, flags[1]), (4, far_below, 0, flags[2]), (5, far_below, 1, flags[2])]
-    fill_taps(taps, edges + [(row, ref, i, factor * past) for row, ref, i, factor in far], gain, 3)
-
-    def extra(kr, row, count):
-        tile = jnp.concatenate(
-            [
-                taps[kc, (base + row) * COLS : (base + row + count) * COLS, :]
-                for base in (0, 3)
-                for kc in range(3)
-            ],
-            axis=1,
-        )
-        weight = jnp.concatenate([now[kr].reshape(3 * C2, C2), before[kr].reshape(3 * C2, C2)], axis=0)
-        return dot(tile, weight)
-
-    last = extra(2, 1, 2)
-    extras = {0: extra(0, 0, 1), ROWS - 1: last[:COLS]}
-    extras[ROWS] = last[COLS:] + extra(1, 1, 1) + pair_of(below, 0).astype(f32)
-    for row in range(ROWS + 1):
+def fill_half_taps(half_taps, wide, rows, value):
+    for row in rows:
         at = pl.ds(row * COLS, COLS)
-        summed = acc[at, :] + extras[row] if row in extras else acc[at, :]
-        summed = summed.astype(bf16).astype(f32)
-        if row == ROWS:
-            summed = summed * flags[2]
+        summed = value(row).astype(bf16).astype(f32)
         wide[0, at, :] = summed[:, :C1]
         wide[1, at, :] = summed[:, C1:]
     j = lax.broadcasted_iota(jnp.int32, (HALF, C1), 0)
-    for row in range(ROWS + 1):
+    for row in rows:
         place = row // 2 if row % 2 == 0 else 5 + row // 2
         for frame in range(2):
             even = wide[frame, pl.ds(row * COLS, HALF, stride=2), :]
@@ -217,17 +182,75 @@
             half_taps[0, at, lanes] = even.astype(bf16)
             half_taps[1, at, lanes] = odd.astype(bf16)
             half_taps[2, at, lanes] = after.astype(bf16)
-    send[0] = dot(down_taps(half_taps, slice(None)), down_weights(down, (0, 1))).astype(bf16)
-    send[1] = dot(down_taps(half_taps, slice(C1, None)), down_weights(down, (0,))).astype(bf16)
-
-
-def down_kernel(half_taps, down, bias, out):
+
+
+def send_down(send, half_taps, down, places):
+    def tile(lanes):
+        columns = [
+            jnp.concatenate([half_taps[kc, p * HALF : (p + 1) * HALF, lanes] for p in places[kr]], axis=0)
+            for kr, kc in TAPS
+        ]
+        return jnp.concatenate(columns, axis=1)
+
+    send[0] = dot(tile(slice(None)), down_weights(down, (0, 1))).astype(bf16)
+    send[1] = dot(tile(slice(C1, None)), down_weights(down, (0,))).astype(bf16)
+
+
+def down_weights(down, times):
+    return jnp.concatenate([down[kt, kr, kc] for kr, kc in TAPS for kt in times], axis=0)
+
+
+def halo_kernel(flags, acc_in, halo, gain, weight, down, acc, send, taps, wide, half_taps):
+    fill_taps(taps, [(row, halo, row, flags[0]) for row in range(ROWS)], gain, 4)
+    conv1_taps(taps, weight, acc, lambda at: acc_in[at, :])
+    fill_half_taps(half_taps, wide, range(2, ROWS - 1), lambda row: acc[pl.ds(row * COLS, COLS), :])
+    send_down(send, half_taps, down, ((1, 2), (6, 7), (2, 3)))
+
+
+def sum_kernel(
+    flags, acc, above, below, far_above, far_below, gain, now, before, down,
+    send, half_taps, taps, wide,
+):
+    past = flags[0]
+    edges = [(0, above, 0, flags[1]), (1, below, 0, flags[2]), (2, below, 1, flags[2])]
+    far = [(3, far_above, 0, flags[1]), (4, far_below, 0, flags[2]), (5, far_below, 1, flags[2])]
+    fill_taps(taps, edges + [(row, ref, i, factor * past) for row, ref, i, factor in far], gain, 3)
+
+    def extra(kr, row, count):
+        tile = jnp.concatenate(
+            [
+                taps[kc, (base + row) * COLS : (base + row + count) * COLS, :]
+                for base in (0, 3)
+                for kc in range(3)
+            ],
+            axis=1,
+        )
+        weight = jnp.concatenate([now[kr].reshape(3 * C2, C2), before[kr].reshape(3 * C2, C2)], axis=0)
+        return dot(tile, weight)
+
+    last = extra(2, 1, 2)
+    extras = {0: extra(0, 0, 1), ROWS - 1: last[:COLS]}
+    extras[ROWS] = last[COLS:] + extra(1, 1, 1) + pair_of(below, 0).astype(f32)
+    def value(row):
+        at = pl.ds(row * COLS, COLS)
+        total = acc[at, :] + extras[row] if row in extras else acc[at, :]
+        return total * flags[2] if row == ROWS else total
+
+    fill_half_taps(half_taps, wide, range(ROWS + 1), value)
+    send_down(send, half_taps, down, ((0, 3), (5, 8), (1, 4)))
+
+
+def down_kernel(flags, half_taps, down, bias, inner, out):
     out[0] = dot(down_taps(half_taps, slice(0, C1)), down_weights(down, (2,))) + bias[...]
     out[1] = dot(down_taps(half_taps, slice(None)), down_weights(down, (1, 2))) + bias[...]
-
-
-def norm_kernel(flags, part, received, gain, query_weight, reduced, normed, queries):
-    value = part[...] + received[...].astype(f32) * flags[0]
+    at = pl.ds(HALF, 2 * HALF)
+    out[:, at, :] += inner[...].astype(f32) * flags[0]
+
+
+def norm_kernel(flags, part, outer, gain, query_weight, reduced, normed, queries):
+    more = outer[...].astype(f32) * flags[0]
+    pieces = [part[:, :HALF] + more[:, :HALF], part[:, HALF : 3 * HALF], part[:, 3 * HALF :] + more[:, HALF:]]
+    value = jnp.concatenate(pieces, axis=1)
     reduced[...] = value
     centred = value - jnp.mean(value, axis=2, keepdims=True)
     spread = jnp.mean(centred * centred, axis=2, keepdims=True)
@@ -435,20 +458,24 @@
         flops=2 * 9 * SIZE * 256 * 256,
         nbytes=6_000_000,
     )
-    (acc,) = call(
+    wide = pltpu.VMEM((2, SIZE, C1), f32)
+    half = ((3, 9 * HALF, C2), bf16)
+    some = ((2, QUERIES // 2, C2), bf16)
+    acc, send_inner = call(
         halo_kernel,
-        [whole],
-        [flags, acc, halo, gain, before],
-        [taps],
+        [whole, some],
+        [flags, acc, halo, gain, before, down_weight],
+        [taps, wide, pltpu.VMEM(*half)],
         scalar,
         flops=2 * 9 * SIZE * 256 * 256,
         nbytes=5_000_000,
     )
+    received_inner = next_frames(send_inner)
     send, half_taps = call(
         sum_kernel,
-        [((2, QUERIES, C2), bf16), ((3, 9 * HALF, C2), bf16)],
+        [some, half],
         [flags, acc, above, below, far_above, far_below, gain, now, before, down_weight],
-        [pltpu.VMEM((3, 6 * COLS, C2), bf16), pltpu.VMEM((2, SIZE, C1), f32)],
+        [pltpu.VMEM((3, 6 * COLS, C2), bf16), wide],
         scalar,
         flops=2 * 18 * 256 * 256 * 256,
         nbytes=5_000_000,
@@ -457,7 +484,8 @@
     (part,) = call(
         down_kernel,
         [((2, QUERIES, C2), f32)],
-        [half_taps, down_weight, down_bias],
+        [flags, half_taps, down_weight, down_bias, received_inner],
+        spaces=scalar,
         flops=2 * 18 * 256 * 256 * 256,
         nbytes=3_000_000,
     )

time: 84.4 us -> 83.1 us (0.985)
  waiting for transfers between devices: 17.4 us -> 14.2 us
  starting transfers between devices: 41.3 us -> 42.2 us
  Pallas kernels: 25.4 us -> 26.3 us
    ppermute x2, waiting for transfers between devices: 3.24 us -> 1.33 us  [diagonal(): return lax.ppermute(x, ('tm', 'space'), route)]
    ppermute x2 -> x3, starting transfers between devices: 3.28 us -> 4.82 us  [next_frames(): return lax.ppermute(x, 'tm', [(i, (i + 1) % times) for i in range(times)])]
    ppermute x2 -> x3, waiting for transfers between devices: 5.76 us -> 4.35 us  [next_frames(): return lax.ppermute(x, 'tm', [(i, (i + 1) % times) for i in range(times)])]
    ppermute x6, starting transfers between devices: 15.3 us -> 14.2 us  [swap(): return lax.ppermute(x, 'space', [(i, i ^ bit) for i in range(space)])]
    pallas_call x20, Pallas kernels: 25.4 us -> 26.3 us  [call(): pl.pallas_call(kernel, out_shape=[jax.ShapeDtypeStruct(s, d) for s, d in...]
  transfers between devices with their start and end apart: 20 -> 21, of which waited for: 6 -> 7; matrix products, arithmetic and copies ran while one was open for 0% -> 0% of each run, Pallas kernels for 23% -> 28%
where the time goes in v5:
time: 83.1 us; the launch traced here: 83 us
  starting transfers between devices  42.2 us (51%)
  Pallas kernels  26.3 us (32%)
  waiting for transfers between devices  14.2 us (17%)
    pallas_call x20, Pallas kernels, call(): pl.pallas_call(kernel, out_shape=[jax.ShapeDtypeStruct(s, d) for s, d in...  26.3 us
    ppermute x10, starting transfers between devices, along(): lax.ppermute(x, 'space', [(i, (i + distance) % space) for i in range(spac...  15.5 us
    ppermute x6, starting transfers between devices, swap(): return lax.ppermute(x, 'space', [(i, i ^ bit) for i in range(space)])  14.2 us
    ppermute x2, starting transfers between devices, diagonal(): return lax.ppermute(x, ('tm', 'space'), route)  7.78 us
    ppermute x6, waiting for transfers between devices, swap(): return lax.ppermute(x, 'space', [(i, i ^ bit) for i in range(space)])  6.94 us
    ppermute x3, starting transfers between devices, next_frames(): return lax.ppermute(x, 'tm', [(i, (i + 1) % times) for i in range(times)])  4.82 us
    ppermute x3, waiting for transfers between devices, next_frames(): return lax.ppermute(x, 'tm', [(i, (i + 1) % times) for i in range(times)])  4.35 us
  transfers between devices with their start and end apart: 21, of which 7 were waited for; matrix products, arithmetic and copies ran while one was open for 0% of the time, Pallas kernels for 28%

profile of v5, /device:TPU:1, one launch (start us, length us, event | category | flops | bytes accessed | tf_op | source)
XLA Modules:
  0.0 83.0 jit_solution(10878340266176509616)
XLA Ops:
  0.0 2.0 %collective-permute-start = (bf16[2,8,128,128]{3,2,1,0:T(8,128)(2,1)}, bf16[2,8,128,128]{3,2,1,0:T(8,128)(2,1)S(1)}, u32[]{:S(2)}, u32[]{:S(2)}) collective-permute-start(bf16[2,8,128,128]{3,2,1,0:T(8,128)(2,1)} %video.1), channel_id=1, source_target_pairs={{0,32},{32,64},{64,96},{96,128},{128,160},{160,192},{192,224},{224... | collective-permute-start | bytes 1572872 | tf_op jit(solution)/shard_map/ppermute | solution.py:405
  3.0 1.3 %collective-permute-start.2 = (bf16[2,2,128,128]{3,2,1,0:T(8,128)(2,1)S(1)}, bf16[2,2,128,128]{3,2,1,0:T(8,128)(2,1)S(1)}, u32[]{:S(2)}, u32[]{:S(2)}) collective-permute-start(bf16[2,2,128,128]{3,2,1,0:T(8,128)(2,1)S(1)} %get-tuple-element.49), channel_id=1, source_target_pairs={{0,31},{1,0},{2,1},{3,2},{4,3},{5,4},{6,5},{7,6},{8,7},{9,8},{10,9... | collective-permute-start | bytes 393224 | tf_op jit(solution)/shard_map/ppermute | solution.py:408
  4.3 7.8 %collective-permute-start.4 = (bf16[2,2,128,128]{3,2,1,0:T(8,128)(2,1)S(1)}, bf16[2,2,128,128]{3,2,1,0:T(8,128)(2,1)S(1)}, u32[]{:S(2)}, u32[]{:S(2)}) collective-permute-start(bf16[2,2,128,128]{3,2,1,0:T(8,128)(2,1)S(1)} %get-tuple-element.49), channel_id=1, source_target_pairs={{0,63},{1,32},{2,33},{3,34},{4,35},{5,36},{6,37},{7,38},{8,39},{9,... | collective-permute-start | bytes 393224 | tf_op jit(solution)/shard_map/ppermute | solution.py:416
  12.1 3.8 %shard_map.109 = (f32[1152,256]{1,0:T(8,128)S(1)}, bf16[3,3,256,256]{3,2,1,0:T(8,128)(2,1)S(1)}, bf16[3,3,256,256]{3,2,1,0:T(8,128)(2,1)S(1)}, bf16[3,3,3,128,25...) custom-call(bf16[2,8,128,128]{3,2,1,0:T(8,128)(2,1)} %video.1, ...), custom_call_target="tpu_custom_call" | custom-call | flops 1358954496 | bytes 6000000 | tf_op jit(solution)/shard_map/pallas_call | solution.py:28
  16.2 3.4 %shard_map.110 = (f32[1152,256]{1,0:T(8,128)S(1)}, bf16[2,128,256]{2,1,0:T(8,128)(2,1)S(1)}) custom-call(f32[3]{0:T(128)S(1)} %add_convert_fusion.flags, f32[1152,256]{1,0:T(8,128)S(1)} %get-tuple-element.43.acc_in, bf16[2,8,128,128]{3,2,1,0:T(8,128)(2,1)S(1)} %collective-permute-done.halo, f32[1,128]{1,0:T(1,128)S(1)} %get-tuple-element.44.gain, ...), custom_call_target="tpu_custom_call" | custom-call | flops 1358954496 | bytes 5000000 | tf_op jit(solution)/shard_map/pallas_call | solution.py:28
  19.6 1.4 %collective-permute-start.5 = (bf16[2,128,256]{2,1,0:T(8,128)(2,1)S(1)}, bf16[2,128,256]{2,1,0:T(8,128)(2,1)S(1)}, u32[]{:S(2)}, u32[]{:S(2)}) collective-permute-start(bf16[2,128,256]{2,1,0:T(8,128)(2,1)S(1)} %get-tuple-element.53), channel_id=1, source_target_pairs={{0,32},{32,64},{64,96},{96,128},{128,160},{160,192},{192,224},{224... | collective-permute-start | bytes 393224 | tf_op jit(solution)/shard_map/ppermute | solution.py:405
  20.9 1.3 %collective-permute-done.3.far_above = bf16[2,1,128,128]{3,2,1,0:T(8,128)(2,1)S(1)} collective-permute-done((bf16[2,1,128,128]{3,2,1,0:T(8,128)(2,1)S(1)}, bf16[2,1,128,128]{3,2,1,0:T(8,128)(2,1)S(1)}, u32[]{:S(2)}, u32[]{:S(2)}) %collective-permute-start.3) | collective-permute-done | bytes 65568 | tf_op jit(solution)/shard_map/ppermute | solution.py:416
  22.2 2.3 %shard_map.112 = (bf16[2,128,256]{2,1,0:T(8,128)(2,1)S(1)}, bf16[3,576,256]{2,1,0:T(8,128)(2,1)S(1)}) custom-call(f32[3]{0:T(128)S(1)} %add_convert_fusion.flags, f32[1152,256]{1,0:T(8,128)S(1)} %get-tuple-element.47.acc, bf16[2,1,128,128]{3,2,1,0:T(8,128)(2,1)S(1)} %collective-permute-done.1.above, ...), custom_call_target="tpu_custom_call" | custom-call | flops 603979776 | bytes 5000000 | tf_op jit(solution)/shard_map/pallas_call | solution.py:28
  24.5 1.4 %collective-permute-start.6 = (bf16[2,128,256]{2,1,0:T(8,128)(2,1)S(1)}, bf16[2,128,256]{2,1,0:T(8,128)(2,1)S(1)}, u32[]{:S(2)}, u32[]{:S(2)}) collective-permute-start(bf16[2,128,256]{2,1,0:T(8,128)(2,1)S(1)} %get-tuple-element.54), channel_id=1, source_target_pairs={{0,32},{32,64},{64,96},{96,128},{128,160},{160,192},{192,224},{224... | collective-permute-start | bytes 393224 | tf_op jit(solution)/shard_map/ppermute | solution.py:405
  27.1 4.1 %collective-permute-done.6.outer = bf16[2,128,256]{2,1,0:T(8,128)(2,1)S(1)} collective-permute-done((bf16[2,128,256]{2,1,0:T(8,128)(2,1)S(1)}, bf16[2,128,256]{2,1,0:T(8,128)(2,1)S(1)}, u32[]{:S(2)}, u32[]{:S(2)}) %collective-permute-start.6) | collective-permute-done | bytes 131104 | tf_op jit(solution)/shard_map/ppermute | solution.py:405
  32.2 2.3 %collective-permute-start.10 = (bf16[2,256,256]{2,1,0:T(8,128)(2,1)S(1)}, bf16[2,256,256]{2,1,0:T(8,128)(2,1)S(1)}, u32[]{:S(2)}, u32[]{:S(2)}) collective-permute-start(bf16[2,256,256]{2,1,0:T(8,128)(2,1)S(1)} %get-tuple-element.59.refs_2_.refs_5_), channel_id=1, source_target_pairs={{0,4},{1,5},{2,6},{3,7},{4,8},{5,9},{6,10},{7,11},{8,12},{9,13},{1... | collective-permute-start | bytes 786440 | tf_op jit(solution)/shard_map/ppermute | solution.py:408
  34.5 3.8 %collective-permute-start.12 = (bf16[2,256,256]{2,1,0:T(8,128)(2,1)S(1)}, bf16[2,256,256]{2,1,0:T(8,128)(2,1)S(1)}, u32[]{:S(2)}, u32[]{:S(2)}) collective-permute-start(bf16[2,256,256]{2,1,0:T(8,128)(2,1)S(1)} %get-tuple-element.59.refs_2_.refs_5_), channel_id=1, source_target_pairs={{0,28},{1,29},{2,30},{3,31},{4,0},{5,1},{6,2},{7,3},{8,4},{9,5},{1... | collective-permute-start | bytes 786440 | tf_op jit(solution)/shard_map/ppermute | solution.py:408
  38.3 3.6 %collective-permute-start.8 = (bf16[2,256,256]{2,1,0:T(8,128)(2,1)S(1)}, bf16[2,256,256]{2,1,0:T(8,128)(2,1)S(1)}, u32[]{:S(2)}, u32[]{:S(2)}) collective-permute-start(bf16[2,256,256]{2,1,0:T(8,128)(2,1)S(1)} %get-tuple-element.58.refs_0_), channel_id=1, source_target_pairs={{0,2},{1,3},{2,0},{3,1},{4,6},{5,7},{6,4},{7,5},{8,10},{9,11},{10,... | collective-permute-start | bytes 786440 | tf_op jit(solution)/shard_map/ppermute | solution.py:419
  42.4 2.7 %collective-permute-start.13 = (bf16[2,256,256]{2,1,0:T(8,128)(2,1)S(1)}, bf16[2,256,256]{2,1,0:T(8,128)(2,1)S(1)}, u32[]{:S(2)}, u32[]{:S(2)}) collective-permute-start(bf16[2,256,256]{2,1,0:T(8,128)(2,1)S(1)} %collective-permute-done.12.refs_4_.refs_7_), channel_id=1, source_target_pairs={{0,28},{1,29},{2,30},{3,31},{4,0},{5,1},{6,2},{7,3},{8,4},{9,5},{1... | collective-permute-start | bytes 786440 | tf_op jit(solution)/shard_map/ppermute | solution.py:408
  45.1 3.5 %collective-permute-start.7 = (bf16[2,256,256]{2,1,0:T(8,128)(2,1)S(1)}, bf16[2,256,256]{2,1,0:T(8,128)(2,1)S(1)}, u32[]{:S(2)}, u32[]{:S(2)}) collective-permute-start(bf16[2,256,256]{2,1,0:T(8,128)(2,1)S(1)} %get-tuple-element.58.refs_0_), channel_id=1, source_target_pairs={{0,1},{1,0},{2,3},{3,2},{4,5},{5,4},{6,7},{7,6},{8,9},{9,8},{10,11... | collective-permute-start | bytes 786440 | tf_op jit(solution)/shard_map/ppermute | solution.py:419
  51.5 2.7 %collective-permute-start.15 = (bf16[2,256,256]{2,1,0:T(8,128)(2,1)S(1)}, bf16[2,256,256]{2,1,0:T(8,128)(2,1)S(1)}, u32[]{:S(2)}, u32[]{:S(2)}) collective-permute-start(bf16[2,256,256]{2,1,0:T(8,128)(2,1)S(1)} %collective-permute-done.13.refs_3_), channel_id=1, source_target_pairs={{0,28},{1,29},{2,30},{3,31},{4,0},{5,1},{6,2},{7,3},{8,4},{9,5},{1... | collective-permute-start | bytes 786440 | tf_op jit(solution)/shard_map/ppermute | solution.py:408
  56.4 1.5 %shard_map.119.refs_1_ = f32[4,272,256]{2,1,0:T(8,128)S(1)} custom-call(bf16[4,256,256]{2,1,0:T(8,128)(2,1)S(1)} %get-tuple-element.63.refs_0_, f32[4,272,256]{2,1,0:T(8,128)S(1)} %get-tuple-element.68.refs_1_, bf16[2,256,256]{2,1,0:T(8,128)(2,1)S(1)} %collective-permute-done.11.refs_2_, ...), custom_call_target="tpu_custom_call", output_to_operand_aliasing={{}: (1, {})} | custom-call | flops 671088640 | bytes 4000000 | tf_op jit(solution)/shard_map/pallas_call | solution.py:28
  59.0 2.7 %collective-permute-start.17 = (bf16[256,256]{1,0:T(8,128)(2,1)S(1)}, bf16[256,256]{1,0:T(8,128)(2,1)S(1)}, u32[]{:S(2)}, u32[]{:S(2)}) collective-permute-start(bf16[256,256]{1,0:T(8,128)(2,1)S(1)} %get-tuple-element.75), channel_id=1, source_target_pairs={{0,28},{1,29},{2,30},{3,31},{4,0},{5,1},{6,2},{7,3},{8,4},{9,5},{1... | collective-permute-start | bytes 393224 | tf_op jit(solution)/shard_map/ppermute | solution.py:408
  61.7 1.5 %shard_map.121.refs_1_ = f32[4,272,256]{2,1,0:T(8,128)S(1)} custom-call(bf16[4,256,256]{2,1,0:T(8,128)(2,1)S(1)} %get-tuple-element.65.refs_0_.refs_1_, f32[4,272,256]{2,1,0:T(8,128)S(1)} %get-tuple-element.73.refs_1_, bf16[2,256,256]{2,1,0:T(8,128)(2,1)S(1)} %collective-permute-done.11.refs_2_, ...), custom_call_target="tpu_custom_call", output_to_operand_aliasing={{}: (1, {})} | custom-call | flops 671088640 | bytes 4000000 | tf_op jit(solution)/shard_map/pallas_call | solution.py:28
  63.1 1.5 %shard_map.122.refs_3_ = f32[4,272,256]{2,1,0:T(8,128)S(1)} custom-call(bf16[4,256,256]{2,1,0:T(8,128)(2,1)S(1)} %get-tuple-element.65.refs_0_.refs_1_, f32[4,272,256]{2,1,0:T(8,128)S(1)} %shard_map.121.refs_1_, bf16[2,256,256]{2,1,0:T(8,128)(2,1)S(1)} %collective-permute-done.14.refs_2_.plus, ...), custom_call_target="tpu_custom_call", output_to_operand_aliasing={{}: (1, {})} | custom-call | flops 671088640 | bytes 4000000 | tf_op jit(solution)/shard_map/pallas_call | solution.py:28
  64.6 1.5 %shard_map.120.refs_2_ = f32[4,272,256]{2,1,0:T(8,128)S(1)} custom-call(bf16[4,256,256]{2,1,0:T(8,128)(2,1)S(1)} %get-tuple-element.63.refs_0_, f32[4,272,256]{2,1,0:T(8,128)S(1)} %shard_map.119.refs_1_, bf16[2,256,256]{2,1,0:T(8,128)(2,1)S(1)} %collective-permute-done.14.refs_2_.plus, ...), custom_call_target="tpu_custom_call", output_to_operand_aliasing={{}: (1, {})} | custom-call | flops 671088640 | bytes 4000000 | tf_op jit(solution)/shard_map/pallas_call | solution.py:28
  67.1 3.1 %collective-permute-start.19 = (f32[2,272,256]{2,1,0:T(8,128)S(1)}, f32[2,272,256]{2,1,0:T(8,128)S(1)}, u32[]{:S(2)}, u32[]{:S(2)}) collective-permute-start(f32[2,272,256]{2,1,0:T(8,128)S(1)} %get-tuple-element.79), channel_id=1, source_target_pairs={{0,1},{1,0},{2,3},{3,2},{4,5},{5,4},{6,7},{7,6},{8,9},{9,8},{10,11... | collective-permute-start | bytes 1671176 | tf_op jit(solution)/shard_map/ppermute | solution.py:419
  72.0 3.2 %collective-permute-start.20 = (bf16[2,272,256]{2,1,0:T(8,128)(2,1)S(1)}, bf16[2,272,256]{2,1,0:T(8,128)(2,1)S(1)}, u32[]{:S(2)}, u32[]{:S(2)}) collective-permute-start(bf16[2,272,256]{2,1,0:T(8,128)(2,1)S(1)} %shard_map.127), channel_id=1, source_target_pairs={{0,2},{1,3},{2,0},{3,1},{4,6},{5,7},{6,4},{7,5},{8,10},{9,11},{10,... | collective-permute-start | bytes 835592 | tf_op jit(solution)/shard_map/ppermute | solution.py:419
  75.3 6.5 %collective-permute-done.20.received = bf16[2,272,256]{2,1,0:T(8,128)(2,1)S(1)} collective-permute-done((bf16[2,272,256]{2,1,0:T(8,128)(2,1)S(1)}, bf16[2,272,256]{2,1,0:T(8,128)(2,1)S(1)}, u32[]{:S(2)}, u32[]{:S(2)}) %collective-permute-start.20) | collective-permute-done | bytes 278560 | tf_op jit(solution)/shard_map/ppermute | solution.py:419
  (39 shorter events, 14.1 us)
Async XLA Ops:
  0.0 16.2 %collective-permute-start = (bf16[2,8,128,128]{3,2,1,0:T(8,128)(2,1)}, bf16[2,8,128,128]{3,2,1,0:T(8,128)(2,1)S(1)}, u32[]{:S(2)}, u32[]{:S(2)}) collective-permute-start(bf16[2,8,128,128]{3,2,1,0:T(8,128)(2,1)} %video.1), channel_id=1, source_target_pairs={{0,32},{32,64},{64,96},{96,128},{128,160},{160,192},{192,224},{224... | collective-permute-start | bytes 1572872 | tf_op jit(solution)/shard_map/ppermute | solution.py:405
  3.0 19.2 %collective-permute-start.2 = (bf16[2,2,128,128]{3,2,1,0:T(8,128)(2,1)S(1)}, bf16[2,2,128,128]{3,2,1,0:T(8,128)(2,1)S(1)}, u32[]{:S(2)}, u32[]{:S(2)}) collective-permute-start(bf16[2,2,128,128]{3,2,1,0:T(8,128)(2,1)S(1)} %get-tuple-element.49), channel_id=1, source_target_pairs={{0,31},{1,0},{2,1},{3,2},{4,3},{5,4},{6,5},{7,6},{8,7},{9,8},{10,9... | collective-permute-start | bytes 393224 | tf_op jit(solution)/shard_map/ppermute | solution.py:408
  4.3 18.0 %collective-permute-start.4 = (bf16[2,2,128,128]{3,2,1,0:T(8,128)(2,1)S(1)}, bf16[2,2,128,128]{3,2,1,0:T(8,128)(2,1)S(1)}, u32[]{:S(2)}, u32[]{:S(2)}) collective-permute-start(bf16[2,2,128,128]{3,2,1,0:T(8,128)(2,1)S(1)} %get-tuple-element.49), channel_id=1, source_target_pairs={{0,63},{1,32},{2,33},{3,34},{4,35},{5,36},{6,37},{7,38},{8,39},{9,... | collective-permute-start | bytes 393224 | tf_op jit(solution)/shard_map/ppermute | solution.py:416
  12.1 8.8 %collective-permute-start.1 = (bf16[2,1,128,128]{3,2,1,0:T(8,128)(2,1)S(1)}, bf16[2,1,128,128]{3,2,1,0:T(8,128)(2,1)S(1)}, u32[]{:S(2)}, u32[]{:S(2)}) collective-permute-start(bf16[2,1,128,128]{3,2,1,0:T(8,128)(2,1)S(1)} %get-tuple-element.48), channel_id=1, source_target_pairs={{0,1},{1,2},{2,3},{3,4},{4,5},{5,6},{6,7},{7,8},{8,9},{9,10},{10,1... | collective-permute-start | bytes 196616 | tf_op jit(solution)/shard_map/ppermute | solution.py:408
  12.1 10.2 %collective-permute-start.3 = (bf16[2,1,128,128]{3,2,1,0:T(8,128)(2,1)S(1)}, bf16[2,1,128,128]{3,2,1,0:T(8,128)(2,1)S(1)}, u32[]{:S(2)}, u32[]{:S(2)}) collective-permute-start(bf16[2,1,128,128]{3,2,1,0:T(8,128)(2,1)S(1)} %get-tuple-element.48), channel_id=1, source_target_pairs={{0,33},{1,34},{2,35},{3,36},{4,37},{5,38},{6,39},{7,40},{8,41},{9,... | collective-permute-start | bytes 196616 | tf_op jit(solution)/shard_map/ppermute | solution.py:416
  19.6 6.4 %collective-permute-start.5 = (bf16[2,128,256]{2,1,0:T(8,128)(2,1)S(1)}, bf16[2,128,256]{2,1,0:T(8,128)(2,1)S(1)}, u32[]{:S(2)}, u32[]{:S(2)}) collective-permute-start(bf16[2,128,256]{2,1,0:T(8,128)(2,1)S(1)} %get-tuple-element.53), channel_id=1, source_target_pairs={{0,32},{32,64},{64,96},{96,128},{128,160},{160,192},{192,224},{224... | collective-permute-start | bytes 393224 | tf_op jit(solution)/shard_map/ppermute | solution.py:405
  24.5 6.7 %collective-permute-start.6 = (bf16[2,128,256]{2,1,0:T(8,128)(2,1)S(1)}, bf16[2,128,256]{2,1,0:T(8,128)(2,1)S(1)}, u32[]{:S(2)}, u32[]{:S(2)}) collective-permute-start(bf16[2,128,256]{2,1,0:T(8,128)(2,1)S(1)} %get-tuple-element.54), channel_id=1, source_target_pairs={{0,32},{32,64},{64,96},{96,128},{128,160},{160,192},{192,224},{224... | collective-permute-start | bytes 393224 | tf_op jit(solution)/shard_map/ppermute | solution.py:405
  32.2 10.2 %collective-permute-start.10 = (bf16[2,256,256]{2,1,0:T(8,128)(2,1)S(1)}, bf16[2,256,256]{2,1,0:T(8,128)(2,1)S(1)}, u32[]{:S(2)}, u32[]{:S(2)}) collective-permute-start(bf16[2,256,256]{2,1,0:T(8,128)(2,1)S(1)} %get-tuple-element.59.refs_2_.refs_5_), channel_id=1, source_target_pairs={{0,4},{1,5},{2,6},{3,7},{4,8},{5,9},{6,10},{7,11},{8,12},{9,13},{1... | collective-permute-start | bytes 786440 | tf_op jit(solution)/shard_map/ppermute | solution.py:408
  34.5 8.0 %collective-permute-start.12 = (bf16[2,256,256]{2,1,0:T(8,128)(2,1)S(1)}, bf16[2,256,256]{2,1,0:T(8,128)(2,1)S(1)}, u32[]{:S(2)}, u32[]{:S(2)}) collective-permute-start(bf16[2,256,256]{2,1,0:T(8,128)(2,1)S(1)} %get-tuple-element.59.refs_2_.refs_5_), channel_id=1, source_target_pairs={{0,28},{1,29},{2,30},{3,31},{4,0},{5,1},{6,2},{7,3},{8,4},{9,5},{1... | collective-permute-start | bytes 786440 | tf_op jit(solution)/shard_map/ppermute | solution.py:408
  38.3 10.4 %collective-permute-start.8 = (bf16[2,256,256]{2,1,0:T(8,128)(2,1)S(1)}, bf16[2,256,256]{2,1,0:T(8,128)(2,1)S(1)}, u32[]{:S(2)}, u32[]{:S(2)}) collective-permute-start(bf16[2,256,256]{2,1,0:T(8,128)(2,1)S(1)} %get-tuple-element.58.refs_0_), channel_id=1, source_target_pairs={{0,2},{1,3},{2,0},{3,1},{4,6},{5,7},{6,4},{7,5},{8,10},{9,11},{10,... | collective-permute-start | bytes 786440 | tf_op jit(solution)/shard_map/ppermute | solution.py:419
  42.4 8.9 %collective-permute-start.11 = (bf16[2,256,256]{2,1,0:T(8,128)(2,1)S(1)}, bf16[2,256,256]{2,1,0:T(8,128)(2,1)S(1)}, u32[]{:S(2)}, u32[]{:S(2)}) collective-permute-start(bf16[2,256,256]{2,1,0:T(8,128)(2,1)S(1)} %collective-permute-done.10.refs_3_.refs_6_), channel_id=1, source_target_pairs={{0,4},{1,5},{2,6},{3,7},{4,8},{5,9},{6,10},{7,11},{8,12},{9,13},{1... | collective-permute-start | bytes 786440 | tf_op jit(solution)/shard_map/ppermute | solution.py:408
  42.4 8.9 %collective-permute-start.13 = (bf16[2,256,256]{2,1,0:T(8,128)(2,1)S(1)}, bf16[2,256,256]{2,1,0:T(8,128)(2,1)S(1)}, u32[]{:S(2)}, u32[]{:S(2)}) collective-permute-start(bf16[2,256,256]{2,1,0:T(8,128)(2,1)S(1)} %collective-permute-done.12.refs_4_.refs_7_), channel_id=1, source_target_pairs={{0,28},{1,29},{2,30},{3,31},{4,0},{5,1},{6,2},{7,3},{8,4},{9,5},{1... | collective-permute-start | bytes 786440 | tf_op jit(solution)/shard_map/ppermute | solution.py:408
  45.1 9.0 %collective-permute-start.7 = (bf16[2,256,256]{2,1,0:T(8,128)(2,1)S(1)}, bf16[2,256,256]{2,1,0:T(8,128)(2,1)S(1)}, u32[]{:S(2)}, u32[]{:S(2)}) collective-permute-start(bf16[2,256,256]{2,1,0:T(8,128)(2,1)S(1)} %get-tuple-element.58.refs_0_), channel_id=1, source_target_pairs={{0,1},{1,0},{2,3},{3,2},{4,5},{5,4},{6,7},{7,6},{8,9},{9,8},{10,11... | collective-permute-start | bytes 786440 | tf_op jit(solution)/shard_map/ppermute | solution.py:419
  48.7 5.5 %collective-permute-start.9 = (bf16[2,256,256]{2,1,0:T(8,128)(2,1)S(1)}, bf16[2,256,256]{2,1,0:T(8,128)(2,1)S(1)}, u32[]{:S(2)}, u32[]{:S(2)}) collective-permute-start(bf16[2,256,256]{2,1,0:T(8,128)(2,1)S(1)} %collective-permute-done.8.refs_1_.refs_2_), channel_id=1, source_target_pairs={{0,1},{1,0},{2,3},{3,2},{4,5},{5,4},{6,7},{7,6},{8,9},{9,8},{10,11... | collective-permute-start | bytes 786440 | tf_op jit(solution)/shard_map/ppermute | solution.py:419
  51.4 7.5 %collective-permute-start.14 = (bf16[2,256,256]{2,1,0:T(8,128)(2,1)S(1)}, bf16[2,256,256]{2,1,0:T(8,128)(2,1)S(1)}, u32[]{:S(2)}, u32[]{:S(2)}) collective-permute-start(bf16[2,256,256]{2,1,0:T(8,128)(2,1)S(1)} %collective-permute-done.11.refs_2_), channel_id=1, source_target_pairs={{0,4},{1,5},{2,6},{3,7},{4,8},{5,9},{6,10},{7,11},{8,12},{9,13},{1... | collective-permute-start | bytes 786440 | tf_op jit(solution)/shard_map/ppermute | solution.py:408
  51.5 7.4 %collective-permute-start.15 = (bf16[2,256,256]{2,1,0:T(8,128)(2,1)S(1)}, bf16[2,256,256]{2,1,0:T(8,128)(2,1)S(1)}, u32[]{:S(2)}, u32[]{:S(2)}) collective-permute-start(bf16[2,256,256]{2,1,0:T(8,128)(2,1)S(1)} %collective-permute-done.13.refs_3_), channel_id=1, source_target_pairs={{0,28},{1,29},{2,30},{3,31},{4,0},{5,1},{6,2},{7,3},{8,4},{9,5},{1... | collective-permute-start | bytes 786440 | tf_op jit(solution)/shard_map/ppermute | solution.py:408
  58.9 7.1 %collective-permute-start.16 = (bf16[256,256]{1,0:T(8,128)(2,1)S(1)}, bf16[256,256]{1,0:T(8,128)(2,1)S(1)}, u32[]{:S(2)}, u32[]{:S(2)}) collective-permute-start(bf16[256,256]{1,0:T(8,128)(2,1)S(1)} %get-tuple-element.74), channel_id=1, source_target_pairs={{0,4},{1,5},{2,6},{3,7},{4,8},{5,9},{6,10},{7,11},{8,12},{9,13},{1... | collective-permute-start | bytes 393224 | tf_op jit(solution)/shard_map/ppermute | solution.py:408
  59.0 7.0 %collective-permute-start.17 = (bf16[256,256]{1,0:T(8,128)(2,1)S(1)}, bf16[256,256]{1,0:T(8,128)(2,1)S(1)}, u32[]{:S(2)}, u32[]{:S(2)}) collective-permute-start(bf16[256,256]{1,0:T(8,128)(2,1)S(1)} %get-tuple-element.75), channel_id=1, source_target_pairs={{0,28},{1,29},{2,30},{3,31},{4,0},{5,1},{6,2},{7,3},{8,4},{9,5},{1... | collective-permute-start | bytes 393224 | tf_op jit(solution)/shard_map/ppermute | solution.py:408
  67.1 4.7 %collective-permute-start.19 = (f32[2,272,256]{2,1,0:T(8,128)S(1)}, f32[2,272,256]{2,1,0:T(8,128)S(1)}, u32[]{:S(2)}, u32[]{:S(2)}) collective-permute-start(f32[2,272,256]{2,1,0:T(8,128)S(1)} %get-tuple-element.79), channel_id=1, source_target_pairs={{0,1},{1,0},{2,3},{3,2},{4,5},{5,4},{6,7},{7,6},{8,9},{9,8},{10,11... | collective-permute-start | bytes 1671176 | tf_op jit(solution)/shard_map/ppermute | solution.py:419
  71.4 3.8 %collective-permute-start.18 = (f32[2,272,256]{2,1,0:T(8,128)S(1)}, f32[2,272,256]{2,1,0:T(8,128)S(1)}, u32[]{:S(2)}, u32[]{:S(2)}) collective-permute-start(f32[2,272,256]{2,1,0:T(8,128)S(1)} %get-tuple-element.77), channel_id=1, source_target_pairs={{0,1},{1,0},{2,3},{3,2},{4,5},{5,4},{6,7},{7,6},{8,9},{9,8},{10,11... | collective-permute-start | bytes 1671176 | tf_op jit(solution)/shard_map/ppermute | solution.py:419
  72.0 9.9 %collective-permute-start.20 = (bf16[2,272,256]{2,1,0:T(8,128)(2,1)S(1)}, bf16[2,272,256]{2,1,0:T(8,128)(2,1)S(1)}, u32[]{:S(2)}, u32[]{:S(2)}) collective-permute-start(bf16[2,272,256]{2,1,0:T(8,128)(2,1)S(1)} %shard_map.127), channel_id=1, source_target_pairs={{0,2},{1,3},{2,0},{3,1},{4,6},{5,7},{6,4},{7,5},{8,10},{9,11},{10,... | collective-permute-start | bytes 835592 | tf_op jit(solution)/shard_map/ppermute | solution.py:419

commit v6 on v5

--- a/solution.py
+++ b/solution.py
@@ -19,7 +19,7 @@
 QUERIES = 256
 
 
-def call(kernel, outs, ins, scratch=(), spaces=None, aliases=None, flops=0, nbytes=0):
+def call(kernel, outs, ins, scratch=(), spaces=None, aliases=None, flops=0, nbytes=0, out_space=VMEM):
     spaces = spaces or {}
     ins = [
         pltpu.with_memory_space_constraint(x, pltpu.HBM) if spaces.get(i) is HBM else x
@@ -29,7 +29,7 @@
         kernel,
         out_shape=[jax.ShapeDtypeStruct(s, d) for s, d in outs],
         in_specs=[spaces.get(i, VMEM) for i in range(len(ins))],
-        out_specs=[VMEM] * len(outs),
+        out_specs=[out_space] * len(outs),
         scratch_shapes=list(scratch),
         input_output_aliases=aliases or {},
         compiler_params=pltpu.CompilerParams(vmem_limit_bytes=24 * 1024 * 1024),
@@ -240,24 +240,41 @@
     send_down(send, half_taps, down, ((0, 3), (5, 8), (1, 4)))
 
 
-def down_kernel(flags, half_taps, down, bias, inner, out):
-    out[0] = dot(down_taps(half_taps, slice(0, C1)), down_weights(down, (2,))) + bias[...]
-    out[1] = dot(down_taps(half_taps, slice(None)), down_weights(down, (1, 2))) + bias[...]
-    at = pl.ds(HALF, 2 * HALF)
-    out[:, at, :] += inner[...].astype(f32) * flags[0]
-
-
-def norm_kernel(flags, part, outer, gain, query_weight, reduced, normed, queries):
-    more = outer[...].astype(f32) * flags[0]
-    pieces = [part[:, :HALF] + more[:, :HALF], part[:, HALF : 3 * HALF], part[:, 3 * HALF :] + more[:, HALF:]]
-    value = jnp.concatenate(pieces, axis=1)
-    reduced[...] = value
+def normalise(value, gain, query_weight):
     centred = value - jnp.mean(value, axis=2, keepdims=True)
     spread = jnp.mean(centred * centred, axis=2, keepdims=True)
     result = (centred * lax.rsqrt(spread + epsilon) * gain[...]).astype(bf16)
-    normed[...] = result
+    query = [(dot(result[i], query_weight[...]).astype(bf16) * (C2**-0.5)).astype(bf16) for i in range(2)]
+    return result, query
+
+
+INNER = slice(HALF, 3 * HALF)
+
+
+def down_kernel(flags, half_taps, down, bias, inner, gain, query_weight, out, normed, queries):
+    out[0] = dot(down_taps(half_taps, slice(0, C1)), down_weights(down, (2,))) + bias[...]
+    out[1] = dot(down_taps(half_taps, slice(None)), down_weights(down, (1, 2))) + bias[...]
+    value = out[:, INNER, :] + inner[...].astype(f32) * flags[0]
+    out[:, INNER, :] = value
+    normed[...], query = normalise(value, gain, query_weight)
+    queries[0], queries[1] = query
+
+
+def norm_kernel(
+    flags, part, outer, inner_normed, inner_queries, gain, query_weight, reduced, normed, queries
+):
+    value = jnp.concatenate([part[:, :HALF], part[:, 3 * HALF :]], axis=1)
+    value = value + outer[...].astype(f32) * flags[0]
+    result, query = normalise(value, gain, query_weight)
     for frame in range(2):
-        queries[frame] = (dot(result[frame], query_weight[...]).astype(bf16) * (C2**-0.5)).astype(bf16)
+        for ref, edge, middle in (
+            (reduced, value[frame], part[frame, INNER, :]),
+            (normed, result[frame], inner_normed[frame]),
+            (queries, query[frame], inner_queries[frame]),
+        ):
+            ref[frame, :HALF, :] = edge[:HALF]
+            ref[frame, INNER, :] = middle
+            ref[frame, 3 * HALF :, :] = edge[HALF:]
 
 
 GROUPS = 4
@@ -363,7 +380,8 @@
         send[frame, C2:, :] = jnp.concatenate(rows, axis=0).astype(bf16)
 
 
-def last_kernel(reduced, state, received, weight, out):
+def last_kernel(reduced, state, received, weight, out, held, sem):
+    copies = []
     for frame in range(2):
         rows = received[frame, C2:, :].astype(f32)
         top_a, mass_a = state[frame, C2 + 8 : C2 + 9, :], state[frame, C2 : C2 + 1, :]
@@ -378,7 +396,11 @@
         mixed = lax.dot_general(
             attended.astype(bf16), weight[...], (((0,), (0,)), ((), ())), preferred_element_type=f32
         )
-        out[frame] = reduced[frame] + mixed
+        held[frame] = reduced[frame] + mixed
+        copies.append(pltpu.make_async_copy(held.at[frame], out.at[frame], sem.at[frame]))
+        copies[frame].start()
+    for copy in copies:
+        copy.wait()
 
 
 def body(
@@ -481,10 +503,10 @@
         nbytes=5_000_000,
     )
     received = next_frames(send)
-    (part,) = call(
+    part, *inner = call(
         down_kernel,
-        [((2, QUERIES, C2), f32)],
-        [flags, half_taps, down_weight, down_bias, received_inner],
+        [((2, QUERIES, C2), f32), some, some],
+        [flags, half_taps, down_weight, down_bias, received_inner, attention_gain, query_weight],
         spaces=scalar,
         flops=2 * 18 * 256 * 256 * 256,
         nbytes=3_000_000,
@@ -493,7 +515,7 @@
     reduced, normed, own = call(
         norm_kernel,
         [((2, QUERIES, C2), f32), pixels, pixels],
-        [flags, part, received, attention_gain, query_weight],
+        [flags, part, received, *inner, attention_gain, query_weight],
         spaces=scalar,
         nbytes=2_000_000,
     )
@@ -565,6 +587,8 @@
         last_kernel,
         [((2, QUERIES, C2), f32)],
         [reduced, kept, received, output_weight],
+        [pltpu.VMEM((2, QUERIES, C2), f32), pltpu.SemaphoreType.DMA((2,))],
+        out_space=HBM,
         nbytes=2_000_000,
     )
     return encoded.reshape(2, ROWS // 2, HALF, C2)

time: 83.1 us -> 83.2 us (level)
  no operation moved by 1% of the time
where the time goes in v6:
time: 83.2 us; the launch traced here: 83.1 us
  starting transfers between devices  42.4 us (51%)
  Pallas kernels  26.5 us (32%)
  waiting for transfers between devices  13.8 us (17%)
    pallas_call x20, Pallas kernels, call(): pl.pallas_call(kernel, out_shape=[jax.ShapeDtypeStruct(s, d) for s, d in...  26.5 us
    ppermute x10, starting transfers between devices, along(): lax.ppermute(x, 'space', [(i, (i + distance) % space) for i in range(spac...  15.5 us
    ppermute x6, starting transfers between devices, swap(): return lax.ppermute(x, 'space', [(i, i ^ bit) for i in range(space)])  14.3 us
    ppermute x2, starting transfers between devices, diagonal(): return lax.ppermute(x, ('tm', 'space'), route)  7.78 us
    ppermute x6, waiting for transfers between devices, swap(): return lax.ppermute(x, 'space', [(i, i ^ bit) for i in range(space)])  6.93 us
    ppermute x3, starting transfers between devices, next_frames(): return lax.ppermute(x, 'tm', [(i, (i + 1) % times) for i in range(times)])  4.82 us
    ppermute x3, waiting for transfers between devices, next_frames(): return lax.ppermute(x, 'tm', [(i, (i + 1) % times) for i in range(times)])  4.02 us
  transfers between devices with their start and end apart: 21, of which 7 were waited for; matrix products, arithmetic and copies ran while one was open for 0% of the time, Pallas kernels for 28%

profile of v6, /device:TPU:1, one launch (start us, length us, event | category | flops | bytes accessed | tf_op | source)
XLA Modules:
  0.0 83.1 jit_solution(13491949651425954743)
XLA Ops:
  0.0 2.0 %collective-permute-start = (bf16[2,8,128,128]{3,2,1,0:T(8,128)(2,1)}, bf16[2,8,128,128]{3,2,1,0:T(8,128)(2,1)S(1)}, u32[]{:S(2)}, u32[]{:S(2)}) collective-permute-start(bf16[2,8,128,128]{3,2,1,0:T(8,128)(2,1)} %video.1), channel_id=1, source_target_pairs={{0,32},{32,64},{64,96},{96,128},{128,160},{160,192},{192,224},{224... | collective-permute-start | bytes 1572872 | tf_op jit(solution)/shard_map/ppermute | solution.py:427
  4.3 7.8 %collective-permute-start.4 = (bf16[2,2,128,128]{3,2,1,0:T(8,128)(2,1)S(1)}, bf16[2,2,128,128]{3,2,1,0:T(8,128)(2,1)S(1)}, u32[]{:S(2)}, u32[]{:S(2)}) collective-permute-start(bf16[2,2,128,128]{3,2,1,0:T(8,128)(2,1)S(1)} %get-tuple-element.52), channel_id=1, source_target_pairs={{0,63},{1,32},{2,33},{3,34},{4,35},{5,36},{6,37},{7,38},{8,39},{9,... | collective-permute-start | bytes 393224 | tf_op jit(solution)/shard_map/ppermute | solution.py:438
  12.1 3.8 %shard_map.109 = (f32[1152,256]{1,0:T(8,128)S(1)}, bf16[3,3,256,256]{3,2,1,0:T(8,128)(2,1)S(1)}, bf16[3,3,256,256]{3,2,1,0:T(8,128)(2,1)S(1)}, bf16[3,3,3,128,25...) custom-call(bf16[2,8,128,128]{3,2,1,0:T(8,128)(2,1)} %video.1, ...), custom_call_target="tpu_custom_call" | custom-call | flops 1358954496 | bytes 6000000 | tf_op jit(solution)/shard_map/pallas_call | solution.py:28
  16.2 3.4 %shard_map.110 = (f32[1152,256]{1,0:T(8,128)S(1)}, bf16[2,128,256]{2,1,0:T(8,128)(2,1)S(1)}) custom-call(f32[3]{0:T(128)S(1)} %add_convert_fusion.flags, f32[1152,256]{1,0:T(8,128)S(1)} %get-tuple-element.46.acc_in, bf16[2,8,128,128]{3,2,1,0:T(8,128)(2,1)S(1)} %collective-permute-done.halo, f32[1,128]{1,0:T(1,128)S(1)} %get-tuple-element.47.gain, ...), custom_call_target="tpu_custom_call" | custom-call | flops 1358954496 | bytes 5000000 | tf_op jit(solution)/shard_map/pallas_call | solution.py:28
  19.6 1.4 %collective-permute-start.5 = (bf16[2,128,256]{2,1,0:T(8,128)(2,1)S(1)}, bf16[2,128,256]{2,1,0:T(8,128)(2,1)S(1)}, u32[]{:S(2)}, u32[]{:S(2)}) collective-permute-start(bf16[2,128,256]{2,1,0:T(8,128)(2,1)S(1)} %get-tuple-element.56), channel_id=1, source_target_pairs={{0,32},{32,64},{64,96},{96,128},{128,160},{160,192},{192,224},{224... | collective-permute-start | bytes 393224 | tf_op jit(solution)/shard_map/ppermute | solution.py:427
  20.9 1.3 %collective-permute-done.3.far_above = bf16[2,1,128,128]{3,2,1,0:T(8,128)(2,1)S(1)} collective-permute-done((bf16[2,1,128,128]{3,2,1,0:T(8,128)(2,1)S(1)}, bf16[2,1,128,128]{3,2,1,0:T(8,128)(2,1)S(1)}, u32[]{:S(2)}, u32[]{:S(2)}) %collective-permute-start.3) | collective-permute-done | bytes 65568 | tf_op jit(solution)/shard_map/ppermute | solution.py:438
  22.2 2.2 %shard_map.112 = (bf16[2,128,256]{2,1,0:T(8,128)(2,1)S(1)}, bf16[3,576,256]{2,1,0:T(8,128)(2,1)S(1)}) custom-call(f32[3]{0:T(128)S(1)} %add_convert_fusion.flags, f32[1152,256]{1,0:T(8,128)S(1)} %get-tuple-element.50.acc, bf16[2,1,128,128]{3,2,1,0:T(8,128)(2,1)S(1)} %collective-permute-done.1.above, ...), custom_call_target="tpu_custom_call" | custom-call | flops 603979776 | bytes 5000000 | tf_op jit(solution)/shard_map/pallas_call | solution.py:28
  24.5 1.4 %collective-permute-start.6 = (bf16[2,128,256]{2,1,0:T(8,128)(2,1)S(1)}, bf16[2,128,256]{2,1,0:T(8,128)(2,1)S(1)}, u32[]{:S(2)}, u32[]{:S(2)}) collective-permute-start(bf16[2,128,256]{2,1,0:T(8,128)(2,1)S(1)} %get-tuple-element.60), channel_id=1, source_target_pairs={{0,32},{32,64},{64,96},{96,128},{128,160},{160,192},{192,224},{224... | collective-permute-start | bytes 393224 | tf_op jit(solution)/shard_map/ppermute | solution.py:427
  25.9 1.5 %shard_map.113 = (f32[2,256,256]{2,1,0:T(8,128)S(1)}, bf16[2,128,256]{2,1,0:T(8,128)(2,1)S(1)}, bf16[2,128,256]{2,1,0:T(8,128)(2,1)S(1)}) custom-call(f32[3]{0:T(128)S(1)} %add_convert_fusion.flags, bf16[3,576,256]{2,1,0:T(8,128)(2,1)S(1)} %get-tuple-element.54.half_taps, bf16[3,3,3,128,256]{4,3,2,1,0:T(8,128)(2,1)S(1)} %get-tuple-element.49.down, ...), custom_call_target="tpu_custom_call" | custom-call | flops 603979776 | bytes 3000000 | tf_op jit(solution)/shard_map/pallas_call | solution.py:28
  27.4 3.8 %collective-permute-done.6.outer = bf16[2,128,256]{2,1,0:T(8,128)(2,1)S(1)} collective-permute-done((bf16[2,128,256]{2,1,0:T(8,128)(2,1)S(1)}, bf16[2,128,256]{2,1,0:T(8,128)(2,1)S(1)}, u32[]{:S(2)}, u32[]{:S(2)}) %collective-permute-start.6) | collective-permute-done | bytes 131104 | tf_op jit(solution)/shard_map/ppermute | solution.py:427
  32.1 2.2 %collective-permute-start.10 = (bf16[2,256,256]{2,1,0:T(8,128)(2,1)S(1)}, bf16[2,256,256]{2,1,0:T(8,128)(2,1)S(1)}, u32[]{:S(2)}, u32[]{:S(2)}) collective-permute-start(bf16[2,256,256]{2,1,0:T(8,128)(2,1)S(1)} %get-tuple-element.65.refs_2_.refs_5_), channel_id=1, source_target_pairs={{0,4},{1,5},{2,6},{3,7},{4,8},{5,9},{6,10},{7,11},{8,12},{9,13},{1... | collective-permute-start | bytes 786440 | tf_op jit(solution)/shard_map/ppermute | solution.py:430
  34.3 3.8 %collective-permute-start.12 = (bf16[2,256,256]{2,1,0:T(8,128)(2,1)S(1)}, bf16[2,256,256]{2,1,0:T(8,128)(2,1)S(1)}, u32[]{:S(2)}, u32[]{:S(2)}) collective-permute-start(bf16[2,256,256]{2,1,0:T(8,128)(2,1)S(1)} %get-tuple-element.65.refs_2_.refs_5_), channel_id=1, source_target_pairs={{0,28},{1,29},{2,30},{3,31},{4,0},{5,1},{6,2},{7,3},{8,4},{9,5},{1... | collective-permute-start | bytes 786440 | tf_op jit(solution)/shard_map/ppermute | solution.py:430
  38.1 3.8 %collective-permute-start.8 = (bf16[2,256,256]{2,1,0:T(8,128)(2,1)S(1)}, bf16[2,256,256]{2,1,0:T(8,128)(2,1)S(1)}, u32[]{:S(2)}, u32[]{:S(2)}) collective-permute-start(bf16[2,256,256]{2,1,0:T(8,128)(2,1)S(1)} %get-tuple-element.64.refs_0_), channel_id=1, source_target_pairs={{0,2},{1,3},{2,0},{3,1},{4,6},{5,7},{6,4},{7,5},{8,10},{9,11},{10,... | collective-permute-start | bytes 786440 | tf_op jit(solution)/shard_map/ppermute | solution.py:441
  42.3 2.7 %collective-permute-start.13 = (bf16[2,256,256]{2,1,0:T(8,128)(2,1)S(1)}, bf16[2,256,256]{2,1,0:T(8,128)(2,1)S(1)}, u32[]{:S(2)}, u32[]{:S(2)}) collective-permute-start(bf16[2,256,256]{2,1,0:T(8,128)(2,1)S(1)} %collective-permute-done.12.refs_4_.refs_7_), channel_id=1, source_target_pairs={{0,28},{1,29},{2,30},{3,31},{4,0},{5,1},{6,2},{7,3},{8,4},{9,5},{1... | collective-permute-start | bytes 786440 | tf_op jit(solution)/shard_map/ppermute | solution.py:430
  45.0 3.6 %collective-permute-start.7 = (bf16[2,256,256]{2,1,0:T(8,128)(2,1)S(1)}, bf16[2,256,256]{2,1,0:T(8,128)(2,1)S(1)}, u32[]{:S(2)}, u32[]{:S(2)}) collective-permute-start(bf16[2,256,256]{2,1,0:T(8,128)(2,1)S(1)} %get-tuple-element.64.refs_0_), channel_id=1, source_target_pairs={{0,1},{1,0},{2,3},{3,2},{4,5},{5,4},{6,7},{7,6},{8,9},{9,8},{10,11... | collective-permute-start | bytes 786440 | tf_op jit(solution)/shard_map/ppermute | solution.py:441
  51.4 2.7 %collective-permute-start.15 = (bf16[2,256,256]{2,1,0:T(8,128)(2,1)S(1)}, bf16[2,256,256]{2,1,0:T(8,128)(2,1)S(1)}, u32[]{:S(2)}, u32[]{:S(2)}) collective-permute-start(bf16[2,256,256]{2,1,0:T(8,128)(2,1)S(1)} %collective-permute-done.13.refs_3_), channel_id=1, source_target_pairs={{0,28},{1,29},{2,30},{3,31},{4,0},{5,1},{6,2},{7,3},{8,4},{9,5},{1... | collective-permute-start | bytes 786440 | tf_op jit(solution)/shard_map/ppermute | solution.py:430
  56.4 1.5 %shard_map.119.refs_1_ = f32[4,272,256]{2,1,0:T(8,128)S(1)} custom-call(bf16[4,256,256]{2,1,0:T(8,128)(2,1)S(1)} %get-tuple-element.69.refs_0_, f32[4,272,256]{2,1,0:T(8,128)S(1)} %get-tuple-element.74.refs_1_, bf16[2,256,256]{2,1,0:T(8,128)(2,1)S(1)} %collective-permute-done.11.refs_2_, ...), custom_call_target="tpu_custom_call", output_to_operand_aliasing={{}: (1, {})} | custom-call | flops 671088640 | bytes 4000000 | tf_op jit(solution)/shard_map/pallas_call | solution.py:28
  59.1 2.7 %collective-permute-start.17 = (bf16[256,256]{1,0:T(8,128)(2,1)S(1)}, bf16[256,256]{1,0:T(8,128)(2,1)S(1)}, u32[]{:S(2)}, u32[]{:S(2)}) collective-permute-start(bf16[256,256]{1,0:T(8,128)(2,1)S(1)} %get-tuple-element.81), channel_id=1, source_target_pairs={{0,28},{1,29},{2,30},{3,31},{4,0},{5,1},{6,2},{7,3},{8,4},{9,5},{1... | collective-permute-start | bytes 393224 | tf_op jit(solution)/shard_map/ppermute | solution.py:430
  61.8 1.5 %shard_map.121.refs_1_ = f32[4,272,256]{2,1,0:T(8,128)S(1)} custom-call(bf16[4,256,256]{2,1,0:T(8,128)(2,1)S(1)} %get-tuple-element.71.refs_0_.refs_1_, f32[4,272,256]{2,1,0:T(8,128)S(1)} %get-tuple-element.79.refs_1_, bf16[2,256,256]{2,1,0:T(8,128)(2,1)S(1)} %collective-permute-done.11.refs_2_, ...), custom_call_target="tpu_custom_call", output_to_operand_aliasing={{}: (1, {})} | custom-call | flops 671088640 | bytes 4000000 | tf_op jit(solution)/shard_map/pallas_call | solution.py:28
  63.2 1.5 %shard_map.122.refs_3_ = f32[4,272,256]{2,1,0:T(8,128)S(1)} custom-call(bf16[4,256,256]{2,1,0:T(8,128)(2,1)S(1)} %get-tuple-element.71.refs_0_.refs_1_, f32[4,272,256]{2,1,0:T(8,128)S(1)} %shard_map.121.refs_1_, bf16[2,256,256]{2,1,0:T(8,128)(2,1)S(1)} %collective-permute-done.14.refs_2_.plus, ...), custom_call_target="tpu_custom_call", output_to_operand_aliasing={{}: (1, {})} | custom-call | flops 671088640 | bytes 4000000 | tf_op jit(solution)/shard_map/pallas_call | solution.py:28
  64.7 1.5 %shard_map.120.refs_2_ = f32[4,272,256]{2,1,0:T(8,128)S(1)} custom-call(bf16[4,256,256]{2,1,0:T(8,128)(2,1)S(1)} %get-tuple-element.69.refs_0_, f32[4,272,256]{2,1,0:T(8,128)S(1)} %shard_map.119.refs_1_, bf16[2,256,256]{2,1,0:T(8,128)(2,1)S(1)} %collective-permute-done.14.refs_2_.plus, ...), custom_call_target="tpu_custom_call", output_to_operand_aliasing={{}: (1, {})} | custom-call | flops 671088640 | bytes 4000000 | tf_op jit(solution)/shard_map/pallas_call | solution.py:28
  67.3 3.0 %collective-permute-start.19 = (f32[2,272,256]{2,1,0:T(8,128)S(1)}, f32[2,272,256]{2,1,0:T(8,128)S(1)}, u32[]{:S(2)}, u32[]{:S(2)}) collective-permute-start(f32[2,272,256]{2,1,0:T(8,128)S(1)} %get-tuple-element.85), channel_id=1, source_target_pairs={{0,1},{1,0},{2,3},{3,2},{4,5},{5,4},{6,7},{7,6},{8,9},{9,8},{10,11... | collective-permute-start | bytes 1671176 | tf_op jit(solution)/shard_map/ppermute | solution.py:441
  72.0 3.2 %collective-permute-start.20 = (bf16[2,272,256]{2,1,0:T(8,128)(2,1)S(1)}, bf16[2,272,256]{2,1,0:T(8,128)(2,1)S(1)}, u32[]{:S(2)}, u32[]{:S(2)}) collective-permute-start(bf16[2,272,256]{2,1,0:T(8,128)(2,1)S(1)} %shard_map.127), channel_id=1, source_target_pairs={{0,2},{1,3},{2,0},{3,1},{4,6},{5,7},{6,4},{7,5},{8,10},{9,11},{10,... | collective-permute-start | bytes 835592 | tf_op jit(solution)/shard_map/ppermute | solution.py:441
  75.3 6.5 %collective-permute-done.20.received = bf16[2,272,256]{2,1,0:T(8,128)(2,1)S(1)} collective-permute-done((bf16[2,272,256]{2,1,0:T(8,128)(2,1)S(1)}, bf16[2,272,256]{2,1,0:T(8,128)(2,1)S(1)}, u32[]{:S(2)}, u32[]{:S(2)}) %collective-permute-start.20) | collective-permute-done | bytes 278560 | tf_op jit(solution)/shard_map/ppermute | solution.py:441
  (39 shorter events, 14.2 us)
Async XLA Ops:
  0.0 16.2 %collective-permute-start = (bf16[2,8,128,128]{3,2,1,0:T(8,128)(2,1)}, bf16[2,8,128,128]{3,2,1,0:T(8,128)(2,1)S(1)}, u32[]{:S(2)}, u32[]{:S(2)}) collective-permute-start(bf16[2,8,128,128]{3,2,1,0:T(8,128)(2,1)} %video.1), channel_id=1, source_target_pairs={{0,32},{32,64},{64,96},{96,128},{128,160},{160,192},{192,224},{224... | collective-permute-start | bytes 1572872 | tf_op jit(solution)/shard_map/ppermute | solution.py:427
  3.0 19.2 %collective-permute-start.2 = (bf16[2,2,128,128]{3,2,1,0:T(8,128)(2,1)S(1)}, bf16[2,2,128,128]{3,2,1,0:T(8,128)(2,1)S(1)}, u32[]{:S(2)}, u32[]{:S(2)}) collective-permute-start(bf16[2,2,128,128]{3,2,1,0:T(8,128)(2,1)S(1)} %get-tuple-element.52), channel_id=1, source_target_pairs={{0,31},{1,0},{2,1},{3,2},{4,3},{5,4},{6,5},{7,6},{8,7},{9,8},{10,9... | collective-permute-start | bytes 393224 | tf_op jit(solution)/shard_map/ppermute | solution.py:430
  4.3 18.0 %collective-permute-start.4 = (bf16[2,2,128,128]{3,2,1,0:T(8,128)(2,1)S(1)}, bf16[2,2,128,128]{3,2,1,0:T(8,128)(2,1)S(1)}, u32[]{:S(2)}, u32[]{:S(2)}) collective-permute-start(bf16[2,2,128,128]{3,2,1,0:T(8,128)(2,1)S(1)} %get-tuple-element.52), channel_id=1, source_target_pairs={{0,63},{1,32},{2,33},{3,34},{4,35},{5,36},{6,37},{7,38},{8,39},{9,... | collective-permute-start | bytes 393224 | tf_op jit(solution)/shard_map/ppermute | solution.py:438
  12.1 8.8 %collective-permute-start.1 = (bf16[2,1,128,128]{3,2,1,0:T(8,128)(2,1)S(1)}, bf16[2,1,128,128]{3,2,1,0:T(8,128)(2,1)S(1)}, u32[]{:S(2)}, u32[]{:S(2)}) collective-permute-start(bf16[2,1,128,128]{3,2,1,0:T(8,128)(2,1)S(1)} %get-tuple-element.51), channel_id=1, source_target_pairs={{0,1},{1,2},{2,3},{3,4},{4,5},{5,6},{6,7},{7,8},{8,9},{9,10},{10,1... | collective-permute-start | bytes 196616 | tf_op jit(solution)/shard_map/ppermute | solution.py:430
  12.1 10.2 %collective-permute-start.3 = (bf16[2,1,128,128]{3,2,1,0:T(8,128)(2,1)S(1)}, bf16[2,1,128,128]{3,2,1,0:T(8,128)(2,1)S(1)}, u32[]{:S(2)}, u32[]{:S(2)}) collective-permute-start(bf16[2,1,128,128]{3,2,1,0:T(8,128)(2,1)S(1)} %get-tuple-element.51), channel_id=1, source_target_pairs={{0,33},{1,34},{2,35},{3,36},{4,37},{5,38},{6,39},{7,40},{8,41},{9,... | collective-permute-start | bytes 196616 | tf_op jit(solution)/shard_map/ppermute | solution.py:438
  19.6 6.4 %collective-permute-start.5 = (bf16[2,128,256]{2,1,0:T(8,128)(2,1)S(1)}, bf16[2,128,256]{2,1,0:T(8,128)(2,1)S(1)}, u32[]{:S(2)}, u32[]{:S(2)}) collective-permute-start(bf16[2,128,256]{2,1,0:T(8,128)(2,1)S(1)} %get-tuple-element.56), channel_id=1, source_target_pairs={{0,32},{32,64},{64,96},{96,128},{128,160},{160,192},{192,224},{224... | collective-permute-start | bytes 393224 | tf_op jit(solution)/shard_map/ppermute | solution.py:427
  24.5 6.7 %collective-permute-start.6 = (bf16[2,128,256]{2,1,0:T(8,128)(2,1)S(1)}, bf16[2,128,256]{2,1,0:T(8,128)(2,1)S(1)}, u32[]{:S(2)}, u32[]{:S(2)}) collective-permute-start(bf16[2,128,256]{2,1,0:T(8,128)(2,1)S(1)} %get-tuple-element.60), channel_id=1, source_target_pairs={{0,32},{32,64},{64,96},{96,128},{128,160},{160,192},{192,224},{224... | collective-permute-start | bytes 393224 | tf_op jit(solution)/shard_map/ppermute | solution.py:427
  32.1 10.2 %collective-permute-start.10 = (bf16[2,256,256]{2,1,0:T(8,128)(2,1)S(1)}, bf16[2,256,256]{2,1,0:T(8,128)(2,1)S(1)}, u32[]{:S(2)}, u32[]{:S(2)}) collective-permute-start(bf16[2,256,256]{2,1,0:T(8,128)(2,1)S(1)} %get-tuple-element.65.refs_2_.refs_5_), channel_id=1, source_target_pairs={{0,4},{1,5},{2,6},{3,7},{4,8},{5,9},{6,10},{7,11},{8,12},{9,13},{1... | collective-permute-start | bytes 786440 | tf_op jit(solution)/shard_map/ppermute | solution.py:430
  34.3 8.0 %collective-permute-start.12 = (bf16[2,256,256]{2,1,0:T(8,128)(2,1)S(1)}, bf16[2,256,256]{2,1,0:T(8,128)(2,1)S(1)}, u32[]{:S(2)}, u32[]{:S(2)}) collective-permute-start(bf16[2,256,256]{2,1,0:T(8,128)(2,1)S(1)} %get-tuple-element.65.refs_2_.refs_5_), channel_id=1, source_target_pairs={{0,28},{1,29},{2,30},{3,31},{4,0},{5,1},{6,2},{7,3},{8,4},{9,5},{1... | collective-permute-start | bytes 786440 | tf_op jit(solution)/shard_map/ppermute | solution.py:430
  38.1 10.4 %collective-permute-start.8 = (bf16[2,256,256]{2,1,0:T(8,128)(2,1)S(1)}, bf16[2,256,256]{2,1,0:T(8,128)(2,1)S(1)}, u32[]{:S(2)}, u32[]{:S(2)}) collective-permute-start(bf16[2,256,256]{2,1,0:T(8,128)(2,1)S(1)} %get-tuple-element.64.refs_0_), channel_id=1, source_target_pairs={{0,2},{1,3},{2,0},{3,1},{4,6},{5,7},{6,4},{7,5},{8,10},{9,11},{10,... | collective-permute-start | bytes 786440 | tf_op jit(solution)/shard_map/ppermute | solution.py:441
  42.3 9.0 %collective-permute-start.11 = (bf16[2,256,256]{2,1,0:T(8,128)(2,1)S(1)}, bf16[2,256,256]{2,1,0:T(8,128)(2,1)S(1)}, u32[]{:S(2)}, u32[]{:S(2)}) collective-permute-start(bf16[2,256,256]{2,1,0:T(8,128)(2,1)S(1)} %collective-permute-done.10.refs_3_.refs_6_), channel_id=1, source_target_pairs={{0,4},{1,5},{2,6},{3,7},{4,8},{5,9},{6,10},{7,11},{8,12},{9,13},{1... | collective-permute-start | bytes 786440 | tf_op jit(solution)/shard_map/ppermute | solution.py:430
  42.3 9.1 %collective-permute-start.13 = (bf16[2,256,256]{2,1,0:T(8,128)(2,1)S(1)}, bf16[2,256,256]{2,1,0:T(8,128)(2,1)S(1)}, u32[]{:S(2)}, u32[]{:S(2)}) collective-permute-start(bf16[2,256,256]{2,1,0:T(8,128)(2,1)S(1)} %collective-permute-done.12.refs_4_.refs_7_), channel_id=1, source_target_pairs={{0,28},{1,29},{2,30},{3,31},{4,0},{5,1},{6,2},{7,3},{8,4},{9,5},{1... | collective-permute-start | bytes 786440 | tf_op jit(solution)/shard_map/ppermute | solution.py:430
  45.0 9.1 %collective-permute-start.7 = (bf16[2,256,256]{2,1,0:T(8,128)(2,1)S(1)}, bf16[2,256,256]{2,1,0:T(8,128)(2,1)S(1)}, u32[]{:S(2)}, u32[]{:S(2)}) collective-permute-start(bf16[2,256,256]{2,1,0:T(8,128)(2,1)S(1)} %get-tuple-element.64.refs_0_), channel_id=1, source_target_pairs={{0,1},{1,0},{2,3},{3,2},{4,5},{5,4},{6,7},{7,6},{8,9},{9,8},{10,11... | collective-permute-start | bytes 786440 | tf_op jit(solution)/shard_map/ppermute | solution.py:441
  48.5 5.6 %collective-permute-start.9 = (bf16[2,256,256]{2,1,0:T(8,128)(2,1)S(1)}, bf16[2,256,256]{2,1,0:T(8,128)(2,1)S(1)}, u32[]{:S(2)}, u32[]{:S(2)}) collective-permute-start(bf16[2,256,256]{2,1,0:T(8,128)(2,1)S(1)} %collective-permute-done.8.refs_1_.refs_2_), channel_id=1, source_target_pairs={{0,1},{1,0},{2,3},{3,2},{4,5},{5,4},{6,7},{7,6},{8,9},{9,8},{10,11... | collective-permute-start | bytes 786440 | tf_op jit(solution)/shard_map/ppermute | solution.py:441
  51.3 7.6 %collective-permute-start.14 = (bf16[2,256,256]{2,1,0:T(8,128)(2,1)S(1)}, bf16[2,256,256]{2,1,0:T(8,128)(2,1)S(1)}, u32[]{:S(2)}, u32[]{:S(2)}) collective-permute-start(bf16[2,256,256]{2,1,0:T(8,128)(2,1)S(1)} %collective-permute-done.11.refs_2_), channel_id=1, source_target_pairs={{0,4},{1,5},{2,6},{3,7},{4,8},{5,9},{6,10},{7,11},{8,12},{9,13},{1... | collective-permute-start | bytes 786440 | tf_op jit(solution)/shard_map/ppermute | solution.py:430
  51.4 7.5 %collective-permute-start.15 = (bf16[2,256,256]{2,1,0:T(8,128)(2,1)S(1)}, bf16[2,256,256]{2,1,0:T(8,128)(2,1)S(1)}, u32[]{:S(2)}, u32[]{:S(2)}) collective-permute-start(bf16[2,256,256]{2,1,0:T(8,128)(2,1)S(1)} %collective-permute-done.13.refs_3_), channel_id=1, source_target_pairs={{0,28},{1,29},{2,30},{3,31},{4,0},{5,1},{6,2},{7,3},{8,4},{9,5},{1... | collective-permute-start | bytes 786440 | tf_op jit(solution)/shard_map/ppermute | solution.py:430
  59.0 7.1 %collective-permute-start.16 = (bf16[256,256]{1,0:T(8,128)(2,1)S(1)}, bf16[256,256]{1,0:T(8,128)(2,1)S(1)}, u32[]{:S(2)}, u32[]{:S(2)}) collective-permute-start(bf16[256,256]{1,0:T(8,128)(2,1)S(1)} %get-tuple-element.80), channel_id=1, source_target_pairs={{0,4},{1,5},{2,6},{3,7},{4,8},{5,9},{6,10},{7,11},{8,12},{9,13},{1... | collective-permute-start | bytes 393224 | tf_op jit(solution)/shard_map/ppermute | solution.py:430
  59.1 7.0 %collective-permute-start.17 = (bf16[256,256]{1,0:T(8,128)(2,1)S(1)}, bf16[256,256]{1,0:T(8,128)(2,1)S(1)}, u32[]{:S(2)}, u32[]{:S(2)}) collective-permute-start(bf16[256,256]{1,0:T(8,128)(2,1)S(1)} %get-tuple-element.81), channel_id=1, source_target_pairs={{0,28},{1,29},{2,30},{3,31},{4,0},{5,1},{6,2},{7,3},{8,4},{9,5},{1... | collective-permute-start | bytes 393224 | tf_op jit(solution)/shard_map/ppermute | solution.py:430
  67.3 4.6 %collective-permute-start.19 = (f32[2,272,256]{2,1,0:T(8,128)S(1)}, f32[2,272,256]{2,1,0:T(8,128)S(1)}, u32[]{:S(2)}, u32[]{:S(2)}) collective-permute-start(f32[2,272,256]{2,1,0:T(8,128)S(1)} %get-tuple-element.85), channel_id=1, source_target_pairs={{0,1},{1,0},{2,3},{3,2},{4,5},{5,4},{6,7},{7,6},{8,9},{9,8},{10,11... | collective-permute-start | bytes 1671176 | tf_op jit(solution)/shard_map/ppermute | solution.py:441
  71.4 3.8 %collective-permute-start.18 = (f32[2,272,256]{2,1,0:T(8,128)S(1)}, f32[2,272,256]{2,1,0:T(8,128)S(1)}, u32[]{:S(2)}, u32[]{:S(2)}) collective-permute-start(f32[2,272,256]{2,1,0:T(8,128)S(1)} %get-tuple-element.83), channel_id=1, source_target_pairs={{0,1},{1,0},{2,3},{3,2},{4,5},{5,4},{6,7},{7,6},{8,9},{9,8},{10,11... | collective-permute-start | bytes 1671176 | tf_op jit(solution)/shard_map/ppermute | solution.py:441
  72.0 9.9 %collective-permute-start.20 = (bf16[2,272,256]{2,1,0:T(8,128)(2,1)S(1)}, bf16[2,272,256]{2,1,0:T(8,128)(2,1)S(1)}, u32[]{:S(2)}, u32[]{:S(2)}) collective-permute-start(bf16[2,272,256]{2,1,0:T(8,128)(2,1)S(1)} %shard_map.127), channel_id=1, source_target_pairs={{0,2},{1,3},{2,0},{3,1},{4,6},{5,7},{6,4},{7,5},{8,10},{9,11},{10,... | collective-permute-start | bytes 835592 | tf_op jit(solution)/shard_map/ppermute | solution.py:441

commit v7 on v6

--- a/solution.py
+++ b/solution.py
@@ -240,41 +240,40 @@
     send_down(send, half_taps, down, ((0, 3), (5, 8), (1, 4)))
 
 
-def normalise(value, gain, query_weight):
+def normalise(value, gain):
     centred = value - jnp.mean(value, axis=2, keepdims=True)
     spread = jnp.mean(centred * centred, axis=2, keepdims=True)
-    result = (centred * lax.rsqrt(spread + epsilon) * gain[...]).astype(bf16)
-    query = [(dot(result[i], query_weight[...]).astype(bf16) * (C2**-0.5)).astype(bf16) for i in range(2)]
-    return result, query
+    return (centred * lax.rsqrt(spread + epsilon) * gain[...]).astype(bf16)
 
 
 INNER = slice(HALF, 3 * HALF)
 
 
-def down_kernel(flags, half_taps, down, bias, inner, gain, query_weight, out, normed, queries):
+def down_kernel(flags, half_taps, down, bias, inner, gain, out, normed):
     out[0] = dot(down_taps(half_taps, slice(0, C1)), down_weights(down, (2,))) + bias[...]
     out[1] = dot(down_taps(half_taps, slice(None)), down_weights(down, (1, 2))) + bias[...]
     value = out[:, INNER, :] + inner[...].astype(f32) * flags[0]
     out[:, INNER, :] = value
-    normed[...], query = normalise(value, gain, query_weight)
-    queries[0], queries[1] = query
-
-
-def norm_kernel(
-    flags, part, outer, inner_normed, inner_queries, gain, query_weight, reduced, normed, queries
-):
+    normed[...] = normalise(value, gain)
+
+
+def norm_kernel(flags, part, outer, inner_normed, gain, reduced, normed):
     value = jnp.concatenate([part[:, :HALF], part[:, 3 * HALF :]], axis=1)
     value = value + outer[...].astype(f32) * flags[0]
-    result, query = normalise(value, gain, query_weight)
+    result = normalise(value, gain)
     for frame in range(2):
         for ref, edge, middle in (
             (reduced, value[frame], part[frame, INNER, :]),
             (normed, result[frame], inner_normed[frame]),
-            (queries, query[frame], inner_queries[frame]),
         ):
             ref[frame, :HALF, :] = edge[:HALF]
             ref[frame, INNER, :] = middle
             ref[frame, 3 * HALF :, :] = edge[HALF:]
+
+
+def query_kernel(normed, weight, queries):
+    for frame in range(2):
+        queries[frame] = (dot(normed[frame], weight[...]).astype(bf16) * (C2**-0.5)).astype(bf16)
 
 
 GROUPS = 4
@@ -503,23 +502,24 @@
         nbytes=5_000_000,
     )
     received = next_frames(send)
-    part, *inner = call(
+    part, inner = call(
         down_kernel,
-        [((2, QUERIES, C2), f32), some, some],
-        [flags, half_taps, down_weight, down_bias, received_inner, attention_gain, query_weight],
+        [((2, QUERIES, C2), f32), some],
+        [flags, half_taps, down_weight, down_bias, received_inner, attention_gain],
         spaces=scalar,
         flops=2 * 18 * 256 * 256 * 256,
         nbytes=3_000_000,
     )
     pixels = ((2, QUERIES, C2), bf16)
-    reduced, normed, own = call(
+    reduced, normed = call(
         norm_kernel,
-        [((2, QUERIES, C2), f32), pixels, pixels],
-        [flags, part, received, *inner, attention_gain, query_weight],
+        [((2, QUERIES, C2), f32), pixels],
+        [flags, part, received, inner, attention_gain],
         spaces=scalar,
         nbytes=2_000_000,
     )
     plus, minus = [along(normed, 4)], [along(normed, -4)]
+    (own,) = call(query_kernel, [pixels], [normed, query_weight], nbytes=600_000)
     plus.append(along(plus[0], 4))
     minus.append(along(minus[0], -4))
     sibling, across = swap(own, 1), swap(own, 2)

time: 83.2 us -> 83 us (level)
    pallas_call x20 -> x21, Pallas kernels: 26.5 us -> 26.4 us  [call(): pl.pallas_call(kernel, out_shape=[jax.ShapeDtypeStruct(s, d) for s, d in...]
where the time goes in v7:
time: 83 us; the launch traced here: 82.9 us
  starting transfers between devices  42.3 us (51%)
  Pallas kernels  26.4 us (32%)
  waiting for transfers between devices  13.8 us (17%)
    pallas_call x21, Pallas kernels, call(): pl.pallas_call(kernel, out_shape=[jax.ShapeDtypeStruct(s, d) for s, d in...  26.4 us
    ppermute x10, starting transfers between devices, along(): lax.ppermute(x, 'space', [(i, (i + distance) % space) for i in range(spac...  15.5 us
    ppermute x6, starting transfers between devices, swap(): return lax.ppermute(x, 'space', [(i, i ^ bit) for i in range(space)])  14.2 us
    ppermute x2, starting transfers between devices, diagonal(): return lax.ppermute(x, ('tm', 'space'), route)  7.78 us
    ppermute x6, waiting for transfers between devices, swap(): return lax.ppermute(x, 'space', [(i, i ^ bit) for i in range(space)])  6.74 us
    ppermute x3, starting transfers between devices, next_frames(): return lax.ppermute(x, 'tm', [(i, (i + 1) % times) for i in range(times)])  4.81 us
    ppermute x3, waiting for transfers between devices, next_frames(): return lax.ppermute(x, 'tm', [(i, (i + 1) % times) for i in range(times)])  4.18 us
  transfers between devices with their start and end apart: 21, of which 7 were waited for; matrix products, arithmetic and copies ran while one was open for 0% of the time, Pallas kernels for 28%

profile of v7, /device:TPU:1, one launch (start us, length us, event | category | flops | bytes accessed | tf_op | source)
XLA Modules:
  0.0 82.9 jit_solution(15763433765656677783)
XLA Ops:
  0.0 2.0 %collective-permute-start = (bf16[2,8,128,128]{3,2,1,0:T(8,128)(2,1)}, bf16[2,8,128,128]{3,2,1,0:T(8,128)(2,1)S(1)}, u32[]{:S(2)}, u32[]{:S(2)}) collective-permute-start(bf16[2,8,128,128]{3,2,1,0:T(8,128)(2,1)} %video.1), channel_id=1, source_target_pairs={{0,32},{32,64},{64,96},{96,128},{128,160},{160,192},{192,224},{224... | collective-permute-start | bytes 1572872 | tf_op jit(solution)/shard_map/ppermute | solution.py:426
  4.3 7.8 %collective-permute-start.4 = (bf16[2,2,128,128]{3,2,1,0:T(8,128)(2,1)S(1)}, bf16[2,2,128,128]{3,2,1,0:T(8,128)(2,1)S(1)}, u32[]{:S(2)}, u32[]{:S(2)}) collective-permute-start(bf16[2,2,128,128]{3,2,1,0:T(8,128)(2,1)S(1)} %get-tuple-element.50), channel_id=1, source_target_pairs={{0,63},{1,32},{2,33},{3,34},{4,35},{5,36},{6,37},{7,38},{8,39},{9,... | collective-permute-start | bytes 393224 | tf_op jit(solution)/shard_map/ppermute | solution.py:437
  12.1 3.8 %shard_map.109 = (f32[1152,256]{1,0:T(8,128)S(1)}, bf16[3,3,256,256]{3,2,1,0:T(8,128)(2,1)S(1)}, bf16[3,3,256,256]{3,2,1,0:T(8,128)(2,1)S(1)}, bf16[3,3,3,128,25...) custom-call(bf16[2,8,128,128]{3,2,1,0:T(8,128)(2,1)} %video.1, ...), custom_call_target="tpu_custom_call" | custom-call | flops 1358954496 | bytes 6000000 | tf_op jit(solution)/shard_map/pallas_call | solution.py:28
  16.2 3.4 %shard_map.110 = (f32[1152,256]{1,0:T(8,128)S(1)}, bf16[2,128,256]{2,1,0:T(8,128)(2,1)S(1)}) custom-call(f32[3]{0:T(128)S(1)} %add_convert_fusion.flags, f32[1152,256]{1,0:T(8,128)S(1)} %get-tuple-element.44.acc_in, bf16[2,8,128,128]{3,2,1,0:T(8,128)(2,1)S(1)} %collective-permute-done.halo, f32[1,128]{1,0:T(1,128)S(1)} %get-tuple-element.45.gain, ...), custom_call_target="tpu_custom_call" | custom-call | flops 1358954496 | bytes 5000000 | tf_op jit(solution)/shard_map/pallas_call | solution.py:28
  19.6 1.4 %collective-permute-start.5 = (bf16[2,128,256]{2,1,0:T(8,128)(2,1)S(1)}, bf16[2,128,256]{2,1,0:T(8,128)(2,1)S(1)}, u32[]{:S(2)}, u32[]{:S(2)}) collective-permute-start(bf16[2,128,256]{2,1,0:T(8,128)(2,1)S(1)} %get-tuple-element.54), channel_id=1, source_target_pairs={{0,32},{32,64},{64,96},{96,128},{128,160},{160,192},{192,224},{224... | collective-permute-start | bytes 393224 | tf_op jit(solution)/shard_map/ppermute | solution.py:426
  22.2 2.2 %shard_map.112 = (bf16[2,128,256]{2,1,0:T(8,128)(2,1)S(1)}, bf16[3,576,256]{2,1,0:T(8,128)(2,1)S(1)}) custom-call(f32[3]{0:T(128)S(1)} %add_convert_fusion.flags, f32[1152,256]{1,0:T(8,128)S(1)} %get-tuple-element.48.acc, bf16[2,1,128,128]{3,2,1,0:T(8,128)(2,1)S(1)} %collective-permute-done.1.above, ...), custom_call_target="tpu_custom_call" | custom-call | flops 603979776 | bytes 5000000 | tf_op jit(solution)/shard_map/pallas_call | solution.py:28
  24.5 1.4 %collective-permute-start.6 = (bf16[2,128,256]{2,1,0:T(8,128)(2,1)S(1)}, bf16[2,128,256]{2,1,0:T(8,128)(2,1)S(1)}, u32[]{:S(2)}, u32[]{:S(2)}) collective-permute-start(bf16[2,128,256]{2,1,0:T(8,128)(2,1)S(1)} %get-tuple-element.57), channel_id=1, source_target_pairs={{0,32},{32,64},{64,96},{96,128},{128,160},{160,192},{192,224},{224... | collective-permute-start | bytes 393224 | tf_op jit(solution)/shard_map/ppermute | solution.py:426
  25.9 1.3 %shard_map.113 = (f32[2,256,256]{2,1,0:T(8,128)S(1)}, bf16[2,128,256]{2,1,0:T(8,128)(2,1)S(1)}) custom-call(f32[3]{0:T(128)S(1)} %add_convert_fusion.flags, bf16[3,576,256]{2,1,0:T(8,128)(2,1)S(1)} %get-tuple-element.52.half_taps, bf16[3,3,3,128,256]{4,3,2,1,0:T(8,128)(2,1)S(1)} %get-tuple-element.47.down, f32[1,256]{1,0:T(1,128)S(1)} %get-tuple-element.53.bias, ...), custom_call_target="tpu_custom_call" | custom-call | flops 603979776 | bytes 3000000 | tf_op jit(solution)/shard_map/pallas_call | solution.py:28
  27.3 3.9 %collective-permute-done.6.outer = bf16[2,128,256]{2,1,0:T(8,128)(2,1)S(1)} collective-permute-done((bf16[2,128,256]{2,1,0:T(8,128)(2,1)S(1)}, bf16[2,128,256]{2,1,0:T(8,128)(2,1)S(1)}, u32[]{:S(2)}, u32[]{:S(2)}) %collective-permute-start.6) | collective-permute-done | bytes 131104 | tf_op jit(solution)/shard_map/ppermute | solution.py:426
  31.9 2.3 %collective-permute-start.10 = (bf16[2,256,256]{2,1,0:T(8,128)(2,1)S(1)}, bf16[2,256,256]{2,1,0:T(8,128)(2,1)S(1)}, u32[]{:S(2)}, u32[]{:S(2)}) collective-permute-start(bf16[2,256,256]{2,1,0:T(8,128)(2,1)S(1)} %get-tuple-element.60.normed.refs_2_.refs_5_), channel_id=1, source_target_pairs={{0,4},{1,5},{2,6},{3,7},{4,8},{5,9},{6,10},{7,11},{8,12},{9,13},{1... | collective-permute-start | bytes 786440 | tf_op jit(solution)/shard_map/ppermute | solution.py:429
  34.2 3.8 %collective-permute-start.12 = (bf16[2,256,256]{2,1,0:T(8,128)(2,1)S(1)}, bf16[2,256,256]{2,1,0:T(8,128)(2,1)S(1)}, u32[]{:S(2)}, u32[]{:S(2)}) collective-permute-start(bf16[2,256,256]{2,1,0:T(8,128)(2,1)S(1)} %get-tuple-element.60.normed.refs_2_.refs_5_), channel_id=1, source_target_pairs={{0,28},{1,29},{2,30},{3,31},{4,0},{5,1},{6,2},{7,3},{8,4},{9,5},{1... | collective-permute-start | bytes 786440 | tf_op jit(solution)/shard_map/ppermute | solution.py:429
  38.2 3.9 %collective-permute-start.8 = (bf16[2,256,256]{2,1,0:T(8,128)(2,1)S(1)}, bf16[2,256,256]{2,1,0:T(8,128)(2,1)S(1)}, u32[]{:S(2)}, u32[]{:S(2)}) collective-permute-start(bf16[2,256,256]{2,1,0:T(8,128)(2,1)S(1)} %shard_map.115.refs_0_), channel_id=1, source_target_pairs={{0,2},{1,3},{2,0},{3,1},{4,6},{5,7},{6,4},{7,5},{8,10},{9,11},{10,... | collective-permute-start | bytes 786440 | tf_op jit(solution)/shard_map/ppermute | solution.py:440
  42.2 2.7 %collective-permute-start.13 = (bf16[2,256,256]{2,1,0:T(8,128)(2,1)S(1)}, bf16[2,256,256]{2,1,0:T(8,128)(2,1)S(1)}, u32[]{:S(2)}, u32[]{:S(2)}) collective-permute-start(bf16[2,256,256]{2,1,0:T(8,128)(2,1)S(1)} %collective-permute-done.12.refs_4_.refs_7_), channel_id=1, source_target_pairs={{0,28},{1,29},{2,30},{3,31},{4,0},{5,1},{6,2},{7,3},{8,4},{9,5},{1... | collective-permute-start | bytes 786440 | tf_op jit(solution)/shard_map/ppermute | solution.py:429
  44.8 3.6 %collective-permute-start.7 = (bf16[2,256,256]{2,1,0:T(8,128)(2,1)S(1)}, bf16[2,256,256]{2,1,0:T(8,128)(2,1)S(1)}, u32[]{:S(2)}, u32[]{:S(2)}) collective-permute-start(bf16[2,256,256]{2,1,0:T(8,128)(2,1)S(1)} %shard_map.115.refs_0_), channel_id=1, source_target_pairs={{0,1},{1,0},{2,3},{3,2},{4,5},{5,4},{6,7},{7,6},{8,9},{9,8},{10,11... | collective-permute-start | bytes 786440 | tf_op jit(solution)/shard_map/ppermute | solution.py:440
  51.6 2.7 %collective-permute-start.15 = (bf16[2,256,256]{2,1,0:T(8,128)(2,1)S(1)}, bf16[2,256,256]{2,1,0:T(8,128)(2,1)S(1)}, u32[]{:S(2)}, u32[]{:S(2)}) collective-permute-start(bf16[2,256,256]{2,1,0:T(8,128)(2,1)S(1)} %collective-permute-done.13.refs_3_), channel_id=1, source_target_pairs={{0,28},{1,29},{2,30},{3,31},{4,0},{5,1},{6,2},{7,3},{8,4},{9,5},{1... | collective-permute-start | bytes 786440 | tf_op jit(solution)/shard_map/ppermute | solution.py:429
  56.6 1.5 %shard_map.120.refs_1_ = f32[4,272,256]{2,1,0:T(8,128)S(1)} custom-call(bf16[4,256,256]{2,1,0:T(8,128)(2,1)S(1)} %get-tuple-element.65.refs_0_, f32[4,272,256]{2,1,0:T(8,128)S(1)} %get-tuple-element.70.refs_1_, bf16[2,256,256]{2,1,0:T(8,128)(2,1)S(1)} %collective-permute-done.11.refs_2_, ...), custom_call_target="tpu_custom_call", output_to_operand_aliasing={{}: (1, {})} | custom-call | flops 671088640 | bytes 4000000 | tf_op jit(solution)/shard_map/pallas_call | solution.py:28
  58.1 1.4 %collective-permute-done.14.refs_2_.plus = bf16[2,256,256]{2,1,0:T(8,128)(2,1)S(1)} collective-permute-done((bf16[2,256,256]{2,1,0:T(8,128)(2,1)S(1)}, bf16[2,256,256]{2,1,0:T(8,128)(2,1)S(1)}, u32[]{:S(2)}, u32[]{:S(2)}) %collective-permute-start.14) | collective-permute-done | bytes 262176 | tf_op jit(solution)/shard_map/ppermute | solution.py:429
  59.6 2.7 %collective-permute-start.17 = (bf16[256,256]{1,0:T(8,128)(2,1)S(1)}, bf16[256,256]{1,0:T(8,128)(2,1)S(1)}, u32[]{:S(2)}, u32[]{:S(2)}) collective-permute-start(bf16[256,256]{1,0:T(8,128)(2,1)S(1)} %get-tuple-element.77), channel_id=1, source_target_pairs={{0,28},{1,29},{2,30},{3,31},{4,0},{5,1},{6,2},{7,3},{8,4},{9,5},{1... | collective-permute-start | bytes 393224 | tf_op jit(solution)/shard_map/ppermute | solution.py:429
  62.3 1.5 %shard_map.122.refs_1_ = f32[4,272,256]{2,1,0:T(8,128)S(1)} custom-call(bf16[4,256,256]{2,1,0:T(8,128)(2,1)S(1)} %get-tuple-element.67.refs_0_.refs_1_, f32[4,272,256]{2,1,0:T(8,128)S(1)} %get-tuple-element.75.refs_1_, bf16[2,256,256]{2,1,0:T(8,128)(2,1)S(1)} %collective-permute-done.11.refs_2_, ...), custom_call_target="tpu_custom_call", output_to_operand_aliasing={{}: (1, {})} | custom-call | flops 671088640 | bytes 4000000 | tf_op jit(solution)/shard_map/pallas_call | solution.py:28
  63.7 1.5 %shard_map.123.refs_3_ = f32[4,272,256]{2,1,0:T(8,128)S(1)} custom-call(bf16[4,256,256]{2,1,0:T(8,128)(2,1)S(1)} %get-tuple-element.67.refs_0_.refs_1_, f32[4,272,256]{2,1,0:T(8,128)S(1)} %shard_map.122.refs_1_, bf16[2,256,256]{2,1,0:T(8,128)(2,1)S(1)} %collective-permute-done.14.refs_2_.plus, ...), custom_call_target="tpu_custom_call", output_to_operand_aliasing={{}: (1, {})} | custom-call | flops 671088640 | bytes 4000000 | tf_op jit(solution)/shard_map/pallas_call | solution.py:28
  65.2 1.5 %shard_map.121.refs_2_ = f32[4,272,256]{2,1,0:T(8,128)S(1)} custom-call(bf16[4,256,256]{2,1,0:T(8,128)(2,1)S(1)} %get-tuple-element.65.refs_0_, f32[4,272,256]{2,1,0:T(8,128)S(1)} %shard_map.120.refs_1_, bf16[2,256,256]{2,1,0:T(8,128)(2,1)S(1)} %collective-permute-done.14.refs_2_.plus, ...), custom_call_target="tpu_custom_call", output_to_operand_aliasing={{}: (1, {})} | custom-call | flops 671088640 | bytes 4000000 | tf_op jit(solution)/shard_map/pallas_call | solution.py:28
  67.8 2.7 %collective-permute-start.19 = (f32[2,272,256]{2,1,0:T(8,128)S(1)}, f32[2,272,256]{2,1,0:T(8,128)S(1)}, u32[]{:S(2)}, u32[]{:S(2)}) collective-permute-start(f32[2,272,256]{2,1,0:T(8,128)S(1)} %get-tuple-element.81), channel_id=1, source_target_pairs={{0,1},{1,0},{2,3},{3,2},{4,5},{5,4},{6,7},{7,6},{8,9},{9,8},{10,11... | collective-permute-start | bytes 1671176 | tf_op jit(solution)/shard_map/ppermute | solution.py:440
  72.1 3.1 %collective-permute-start.20 = (bf16[2,272,256]{2,1,0:T(8,128)(2,1)S(1)}, bf16[2,272,256]{2,1,0:T(8,128)(2,1)S(1)}, u32[]{:S(2)}, u32[]{:S(2)}) collective-permute-start(bf16[2,272,256]{2,1,0:T(8,128)(2,1)S(1)} %shard_map.128), channel_id=1, source_target_pairs={{0,2},{1,3},{2,0},{3,1},{4,6},{5,7},{6,4},{7,5},{8,10},{9,11},{10,... | collective-permute-start | bytes 835592 | tf_op jit(solution)/shard_map/ppermute | solution.py:440
  75.3 6.3 %collective-permute-done.20.received = bf16[2,272,256]{2,1,0:T(8,128)(2,1)S(1)} collective-permute-done((bf16[2,272,256]{2,1,0:T(8,128)(2,1)S(1)}, bf16[2,272,256]{2,1,0:T(8,128)(2,1)S(1)}, u32[]{:S(2)}, u32[]{:S(2)}) %collective-permute-start.20) | collective-permute-done | bytes 278560 | tf_op jit(solution)/shard_map/ppermute | solution.py:440
  (40 shorter events, 14.5 us)
Async XLA Ops:
  0.0 16.2 %collective-permute-start = (bf16[2,8,128,128]{3,2,1,0:T(8,128)(2,1)}, bf16[2,8,128,128]{3,2,1,0:T(8,128)(2,1)S(1)}, u32[]{:S(2)}, u32[]{:S(2)}) collective-permute-start(bf16[2,8,128,128]{3,2,1,0:T(8,128)(2,1)} %video.1), channel_id=1, source_target_pairs={{0,32},{32,64},{64,96},{96,128},{128,160},{160,192},{192,224},{224... | collective-permute-start | bytes 1572872 | tf_op jit(solution)/shard_map/ppermute | solution.py:426
  3.0 19.2 %collective-permute-start.2 = (bf16[2,2,128,128]{3,2,1,0:T(8,128)(2,1)S(1)}, bf16[2,2,128,128]{3,2,1,0:T(8,128)(2,1)S(1)}, u32[]{:S(2)}, u32[]{:S(2)}) collective-permute-start(bf16[2,2,128,128]{3,2,1,0:T(8,128)(2,1)S(1)} %get-tuple-element.50), channel_id=1, source_target_pairs={{0,31},{1,0},{2,1},{3,2},{4,3},{5,4},{6,5},{7,6},{8,7},{9,8},{10,9... | collective-permute-start | bytes 393224 | tf_op jit(solution)/shard_map/ppermute | solution.py:429
  4.3 18.0 %collective-permute-start.4 = (bf16[2,2,128,128]{3,2,1,0:T(8,128)(2,1)S(1)}, bf16[2,2,128,128]{3,2,1,0:T(8,128)(2,1)S(1)}, u32[]{:S(2)}, u32[]{:S(2)}) collective-permute-start(bf16[2,2,128,128]{3,2,1,0:T(8,128)(2,1)S(1)} %get-tuple-element.50), channel_id=1, source_target_pairs={{0,63},{1,32},{2,33},{3,34},{4,35},{5,36},{6,37},{7,38},{8,39},{9,... | collective-permute-start | bytes 393224 | tf_op jit(solution)/shard_map/ppermute | solution.py:437
  12.1 8.8 %collective-permute-start.1 = (bf16[2,1,128,128]{3,2,1,0:T(8,128)(2,1)S(1)}, bf16[2,1,128,128]{3,2,1,0:T(8,128)(2,1)S(1)}, u32[]{:S(2)}, u32[]{:S(2)}) collective-permute-start(bf16[2,1,128,128]{3,2,1,0:T(8,128)(2,1)S(1)} %get-tuple-element.49), channel_id=1, source_target_pairs={{0,1},{1,2},{2,3},{3,4},{4,5},{5,6},{6,7},{7,8},{8,9},{9,10},{10,1... | collective-permute-start | bytes 196616 | tf_op jit(solution)/shard_map/ppermute | solution.py:429
  12.1 10.2 %collective-permute-start.3 = (bf16[2,1,128,128]{3,2,1,0:T(8,128)(2,1)S(1)}, bf16[2,1,128,128]{3,2,1,0:T(8,128)(2,1)S(1)}, u32[]{:S(2)}, u32[]{:S(2)}) collective-permute-start(bf16[2,1,128,128]{3,2,1,0:T(8,128)(2,1)S(1)} %get-tuple-element.49), channel_id=1, source_target_pairs={{0,33},{1,34},{2,35},{3,36},{4,37},{5,38},{6,39},{7,40},{8,41},{9,... | collective-permute-start | bytes 196616 | tf_op jit(solution)/shard_map/ppermute | solution.py:437
  19.6 6.4 %collective-permute-start.5 = (bf16[2,128,256]{2,1,0:T(8,128)(2,1)S(1)}, bf16[2,128,256]{2,1,0:T(8,128)(2,1)S(1)}, u32[]{:S(2)}, u32[]{:S(2)}) collective-permute-start(bf16[2,128,256]{2,1,0:T(8,128)(2,1)S(1)} %get-tuple-element.54), channel_id=1, source_target_pairs={{0,32},{32,64},{64,96},{96,128},{128,160},{160,192},{192,224},{224... | collective-permute-start | bytes 393224 | tf_op jit(solution)/shard_map/ppermute | solution.py:426
  24.5 6.7 %collective-permute-start.6 = (bf16[2,128,256]{2,1,0:T(8,128)(2,1)S(1)}, bf16[2,128,256]{2,1,0:T(8,128)(2,1)S(1)}, u32[]{:S(2)}, u32[]{:S(2)}) collective-permute-start(bf16[2,128,256]{2,1,0:T(8,128)(2,1)S(1)} %get-tuple-element.57), channel_id=1, source_target_pairs={{0,32},{32,64},{64,96},{96,128},{128,160},{160,192},{192,224},{224... | collective-permute-start | bytes 393224 | tf_op jit(solution)/shard_map/ppermute | solution.py:426
  31.9 10.2 %collective-permute-start.10 = (bf16[2,256,256]{2,1,0:T(8,128)(2,1)S(1)}, bf16[2,256,256]{2,1,0:T(8,128)(2,1)S(1)}, u32[]{:S(2)}, u32[]{:S(2)}) collective-permute-start(bf16[2,256,256]{2,1,0:T(8,128)(2,1)S(1)} %get-tuple-element.60.normed.refs_2_.refs_5_), channel_id=1, source_target_pairs={{0,4},{1,5},{2,6},{3,7},{4,8},{5,9},{6,10},{7,11},{8,12},{9,13},{1... | collective-permute-start | bytes 786440 | tf_op jit(solution)/shard_map/ppermute | solution.py:429
  34.2 8.0 %collective-permute-start.12 = (bf16[2,256,256]{2,1,0:T(8,128)(2,1)S(1)}, bf16[2,256,256]{2,1,0:T(8,128)(2,1)S(1)}, u32[]{:S(2)}, u32[]{:S(2)}) collective-permute-start(bf16[2,256,256]{2,1,0:T(8,128)(2,1)S(1)} %get-tuple-element.60.normed.refs_2_.refs_5_), channel_id=1, source_target_pairs={{0,28},{1,29},{2,30},{3,31},{4,0},{5,1},{6,2},{7,3},{8,4},{9,5},{1... | collective-permute-start | bytes 786440 | tf_op jit(solution)/shard_map/ppermute | solution.py:429
  38.2 10.2 %collective-permute-start.8 = (bf16[2,256,256]{2,1,0:T(8,128)(2,1)S(1)}, bf16[2,256,256]{2,1,0:T(8,128)(2,1)S(1)}, u32[]{:S(2)}, u32[]{:S(2)}) collective-permute-start(bf16[2,256,256]{2,1,0:T(8,128)(2,1)S(1)} %shard_map.115.refs_0_), channel_id=1, source_target_pairs={{0,2},{1,3},{2,0},{3,1},{4,6},{5,7},{6,4},{7,5},{8,10},{9,11},{10,... | collective-permute-start | bytes 786440 | tf_op jit(solution)/shard_map/ppermute | solution.py:440
  42.1 9.4 %collective-permute-start.11 = (bf16[2,256,256]{2,1,0:T(8,128)(2,1)S(1)}, bf16[2,256,256]{2,1,0:T(8,128)(2,1)S(1)}, u32[]{:S(2)}, u32[]{:S(2)}) collective-permute-start(bf16[2,256,256]{2,1,0:T(8,128)(2,1)S(1)} %collective-permute-done.10.refs_3_.refs_6_), channel_id=1, source_target_pairs={{0,4},{1,5},{2,6},{3,7},{4,8},{5,9},{6,10},{7,11},{8,12},{9,13},{1... | collective-permute-start | bytes 786440 | tf_op jit(solution)/shard_map/ppermute | solution.py:429
  42.2 9.4 %collective-permute-start.13 = (bf16[2,256,256]{2,1,0:T(8,128)(2,1)S(1)}, bf16[2,256,256]{2,1,0:T(8,128)(2,1)S(1)}, u32[]{:S(2)}, u32[]{:S(2)}) collective-permute-start(bf16[2,256,256]{2,1,0:T(8,128)(2,1)S(1)} %collective-permute-done.12.refs_4_.refs_7_), channel_id=1, source_target_pairs={{0,28},{1,29},{2,30},{3,31},{4,0},{5,1},{6,2},{7,3},{8,4},{9,5},{1... | collective-permute-start | bytes 786440 | tf_op jit(solution)/shard_map/ppermute | solution.py:429
  44.8 9.5 %collective-permute-start.7 = (bf16[2,256,256]{2,1,0:T(8,128)(2,1)S(1)}, bf16[2,256,256]{2,1,0:T(8,128)(2,1)S(1)}, u32[]{:S(2)}, u32[]{:S(2)}) collective-permute-start(bf16[2,256,256]{2,1,0:T(8,128)(2,1)S(1)} %shard_map.115.refs_0_), channel_id=1, source_target_pairs={{0,1},{1,0},{2,3},{3,2},{4,5},{5,4},{6,7},{7,6},{8,9},{9,8},{10,11... | collective-permute-start | bytes 786440 | tf_op jit(solution)/shard_map/ppermute | solution.py:440
  48.4 5.9 %collective-permute-start.9 = (bf16[2,256,256]{2,1,0:T(8,128)(2,1)S(1)}, bf16[2,256,256]{2,1,0:T(8,128)(2,1)S(1)}, u32[]{:S(2)}, u32[]{:S(2)}) collective-permute-start(bf16[2,256,256]{2,1,0:T(8,128)(2,1)S(1)} %collective-permute-done.8.refs_1_.refs_2_), channel_id=1, source_target_pairs={{0,1},{1,0},{2,3},{3,2},{4,5},{5,4},{6,7},{7,6},{8,9},{9,8},{10,11... | collective-permute-start | bytes 786440 | tf_op jit(solution)/shard_map/ppermute | solution.py:440
  51.5 8.0 %collective-permute-start.14 = (bf16[2,256,256]{2,1,0:T(8,128)(2,1)S(1)}, bf16[2,256,256]{2,1,0:T(8,128)(2,1)S(1)}, u32[]{:S(2)}, u32[]{:S(2)}) collective-permute-start(bf16[2,256,256]{2,1,0:T(8,128)(2,1)S(1)} %collective-permute-done.11.refs_2_), channel_id=1, source_target_pairs={{0,4},{1,5},{2,6},{3,7},{4,8},{5,9},{6,10},{7,11},{8,12},{9,13},{1... | collective-permute-start | bytes 786440 | tf_op jit(solution)/shard_map/ppermute | solution.py:429
  51.6 7.9 %collective-permute-start.15 = (bf16[2,256,256]{2,1,0:T(8,128)(2,1)S(1)}, bf16[2,256,256]{2,1,0:T(8,128)(2,1)S(1)}, u32[]{:S(2)}, u32[]{:S(2)}) collective-permute-start(bf16[2,256,256]{2,1,0:T(8,128)(2,1)S(1)} %collective-permute-done.13.refs_3_), channel_id=1, source_target_pairs={{0,28},{1,29},{2,30},{3,31},{4,0},{5,1},{6,2},{7,3},{8,4},{9,5},{1... | collective-permute-start | bytes 786440 | tf_op jit(solution)/shard_map/ppermute | solution.py:429
  59.5 7.1 %collective-permute-start.16 = (bf16[256,256]{1,0:T(8,128)(2,1)S(1)}, bf16[256,256]{1,0:T(8,128)(2,1)S(1)}, u32[]{:S(2)}, u32[]{:S(2)}) collective-permute-start(bf16[256,256]{1,0:T(8,128)(2,1)S(1)} %get-tuple-element.76), channel_id=1, source_target_pairs={{0,4},{1,5},{2,6},{3,7},{4,8},{5,9},{6,10},{7,11},{8,12},{9,13},{1... | collective-permute-start | bytes 393224 | tf_op jit(solution)/shard_map/ppermute | solution.py:429
  59.6 7.0 %collective-permute-start.17 = (bf16[256,256]{1,0:T(8,128)(2,1)S(1)}, bf16[256,256]{1,0:T(8,128)(2,1)S(1)}, u32[]{:S(2)}, u32[]{:S(2)}) collective-permute-start(bf16[256,256]{1,0:T(8,128)(2,1)S(1)} %get-tuple-element.77), channel_id=1, source_target_pairs={{0,28},{1,29},{2,30},{3,31},{4,0},{5,1},{6,2},{7,3},{8,4},{9,5},{1... | collective-permute-start | bytes 393224 | tf_op jit(solution)/shard_map/ppermute | solution.py:429
  67.8 4.3 %collective-permute-start.19 = (f32[2,272,256]{2,1,0:T(8,128)S(1)}, f32[2,272,256]{2,1,0:T(8,128)S(1)}, u32[]{:S(2)}, u32[]{:S(2)}) collective-permute-start(f32[2,272,256]{2,1,0:T(8,128)S(1)} %get-tuple-element.81), channel_id=1, source_target_pairs={{0,1},{1,0},{2,3},{3,2},{4,5},{5,4},{6,7},{7,6},{8,9},{9,8},{10,11... | collective-permute-start | bytes 1671176 | tf_op jit(solution)/shard_map/ppermute | solution.py:440
  71.5 3.7 %collective-permute-start.18 = (f32[2,272,256]{2,1,0:T(8,128)S(1)}, f32[2,272,256]{2,1,0:T(8,128)S(1)}, u32[]{:S(2)}, u32[]{:S(2)}) collective-permute-start(f32[2,272,256]{2,1,0:T(8,128)S(1)} %get-tuple-element.79), channel_id=1, source_target_pairs={{0,1},{1,0},{2,3},{3,2},{4,5},{5,4},{6,7},{7,6},{8,9},{9,8},{10,11... | collective-permute-start | bytes 1671176 | tf_op jit(solution)/shard_map/ppermute | solution.py:440
  72.1 9.5 %collective-permute-start.20 = (bf16[2,272,256]{2,1,0:T(8,128)(2,1)S(1)}, bf16[2,272,256]{2,1,0:T(8,128)(2,1)S(1)}, u32[]{:S(2)}, u32[]{:S(2)}) collective-permute-start(bf16[2,272,256]{2,1,0:T(8,128)(2,1)S(1)} %shard_map.128), channel_id=1, source_target_pairs={{0,2},{1,3},{2,0},{3,1},{4,6},{5,7},{6,4},{7,5},{8,10},{9,11},{10,... | collective-permute-start | bytes 835592 | tf_op jit(solution)/shard_map/ppermute | solution.py:440

commit v8 on v5

--- a/solution.py
+++ b/solution.py
@@ -214,7 +214,7 @@
     past = flags[0]
     edges = [(0, above, 0, flags[1]), (1, below, 0, flags[2]), (2, below, 1, flags[2])]
     far = [(3, far_above, 0, flags[1]), (4, far_below, 0, flags[2]), (5, far_below, 1, flags[2])]
-    fill_taps(taps, edges + [(row, ref, i, factor * past) for row, ref, i, factor in far], gain, 3)
+    fill_taps(taps, edges + [(row, ref, i, factor * past) for row, ref, i, factor in far], gain, 6)
 
     def extra(kr, row, count):
         tile = jnp.concatenate(

time: 83.1 us -> 82.5 us (level)
  starting transfers between devices: 42.2 us -> 41.1 us
    ppermute x6, starting transfers between devices: 14.2 us -> 13.1 us  [swap(): return lax.ppermute(x, 'space', [(i, i ^ bit) for i in range(space)])]
where the time goes in v8:
time: 82.5 us; the launch traced here: 82.4 us
  starting transfers between devices  41.1 us (50%)
  Pallas kernels  26.5 us (32%)
  waiting for transfers between devices  14.5 us (18%)
    pallas_call x20, Pallas kernels, call(): pl.pallas_call(kernel, out_shape=[jax.ShapeDtypeStruct(s, d) for s, d in...  26.5 us
    ppermute x10, starting transfers between devices, along(): lax.ppermute(x, 'space', [(i, (i + distance) % space) for i in range(spac...  15.4 us
    ppermute x6, starting transfers between devices, swap(): return lax.ppermute(x, 'space', [(i, i ^ bit) for i in range(space)])  13.1 us
    ppermute x2, starting transfers between devices, diagonal(): return lax.ppermute(x, ('tm', 'space'), route)  7.78 us
    ppermute x6, waiting for transfers between devices, swap(): return lax.ppermute(x, 'space', [(i, i ^ bit) for i in range(space)])  6.76 us
    ppermute x3, starting transfers between devices, next_frames(): return lax.ppermute(x, 'tm', [(i, (i + 1) % times) for i in range(times)])  4.82 us
    ppermute x3, waiting for transfers between devices, next_frames(): return lax.ppermute(x, 'tm', [(i, (i + 1) % times) for i in range(times)])  4.55 us
    ppermute x10, waiting for transfers between devices, along(): lax.ppermute(x, 'space', [(i, (i + distance) % space) for i in range(spac...  1.86 us
  transfers between devices with their start and end apart: 21, of which 7 were waited for; matrix products, arithmetic and copies ran while one was open for 0% of the time, Pallas kernels for 28%

profile of v8, /device:TPU:1, one launch (start us, length us, event | category | flops | bytes accessed | tf_op | source)
XLA Modules:
  0.0 82.4 jit_solution(12281498531892506688)
XLA Ops:
  0.0 2.0 %collective-permute-start = (bf16[2,8,128,128]{3,2,1,0:T(8,128)(2,1)}, bf16[2,8,128,128]{3,2,1,0:T(8,128)(2,1)S(1)}, u32[]{:S(2)}, u32[]{:S(2)}) collective-permute-start(bf16[2,8,128,128]{3,2,1,0:T(8,128)(2,1)} %video.1), channel_id=1, source_target_pairs={{0,32},{32,64},{64,96},{96,128},{128,160},{160,192},{192,224},{224... | collective-permute-start | bytes 1572872 | tf_op jit(solution)/shard_map/ppermute | solution.py:405
  4.3 7.8 %collective-permute-start.4 = (bf16[2,2,128,128]{3,2,1,0:T(8,128)(2,1)S(1)}, bf16[2,2,128,128]{3,2,1,0:T(8,128)(2,1)S(1)}, u32[]{:S(2)}, u32[]{:S(2)}) collective-permute-start(bf16[2,2,128,128]{3,2,1,0:T(8,128)(2,1)S(1)} %get-tuple-element.49), channel_id=1, source_target_pairs={{0,63},{1,32},{2,33},{3,34},{4,35},{5,36},{6,37},{7,38},{8,39},{9,... | collective-permute-start | bytes 393224 | tf_op jit(solution)/shard_map/ppermute | solution.py:416
  12.1 3.8 %shard_map.109 = (f32[1152,256]{1,0:T(8,128)S(1)}, bf16[3,3,256,256]{3,2,1,0:T(8,128)(2,1)S(1)}, bf16[3,3,256,256]{3,2,1,0:T(8,128)(2,1)S(1)}, bf16[3,3,3,128,25...) custom-call(bf16[2,8,128,128]{3,2,1,0:T(8,128)(2,1)} %video.1, ...), custom_call_target="tpu_custom_call" | custom-call | flops 1358954496 | bytes 6000000 | tf_op jit(solution)/shard_map/pallas_call | solution.py:28
  16.2 3.4 %shard_map.110 = (f32[1152,256]{1,0:T(8,128)S(1)}, bf16[2,128,256]{2,1,0:T(8,128)(2,1)S(1)}) custom-call(f32[3]{0:T(128)S(1)} %add_convert_fusion.flags, f32[1152,256]{1,0:T(8,128)S(1)} %get-tuple-element.43.acc_in, bf16[2,8,128,128]{3,2,1,0:T(8,128)(2,1)S(1)} %collective-permute-done.halo, f32[1,128]{1,0:T(1,128)S(1)} %get-tuple-element.44.gain, ...), custom_call_target="tpu_custom_call" | custom-call | flops 1358954496 | bytes 5000000 | tf_op jit(solution)/shard_map/pallas_call | solution.py:28
  19.6 1.4 %collective-permute-start.5 = (bf16[2,128,256]{2,1,0:T(8,128)(2,1)S(1)}, bf16[2,128,256]{2,1,0:T(8,128)(2,1)S(1)}, u32[]{:S(2)}, u32[]{:S(2)}) collective-permute-start(bf16[2,128,256]{2,1,0:T(8,128)(2,1)S(1)} %get-tuple-element.53), channel_id=1, source_target_pairs={{0,32},{32,64},{64,96},{96,128},{128,160},{160,192},{192,224},{224... | collective-permute-start | bytes 393224 | tf_op jit(solution)/shard_map/ppermute | solution.py:405
  20.9 1.3 %collective-permute-done.3.far_above = bf16[2,1,128,128]{3,2,1,0:T(8,128)(2,1)S(1)} collective-permute-done((bf16[2,1,128,128]{3,2,1,0:T(8,128)(2,1)S(1)}, bf16[2,1,128,128]{3,2,1,0:T(8,128)(2,1)S(1)}, u32[]{:S(2)}, u32[]{:S(2)}) %collective-permute-start.3) | collective-permute-done | bytes 65568 | tf_op jit(solution)/shard_map/ppermute | solution.py:416
  22.2 2.4 %shard_map.112 = (bf16[2,128,256]{2,1,0:T(8,128)(2,1)S(1)}, bf16[3,576,256]{2,1,0:T(8,128)(2,1)S(1)}) custom-call(f32[3]{0:T(128)S(1)} %add_convert_fusion.flags, f32[1152,256]{1,0:T(8,128)S(1)} %get-tuple-element.47.acc, bf16[2,1,128,128]{3,2,1,0:T(8,128)(2,1)S(1)} %collective-permute-done.1.above, ...), custom_call_target="tpu_custom_call" | custom-call | flops 603979776 | bytes 5000000 | tf_op jit(solution)/shard_map/pallas_call | solution.py:28
  24.7 1.4 %collective-permute-start.6 = (bf16[2,128,256]{2,1,0:T(8,128)(2,1)S(1)}, bf16[2,128,256]{2,1,0:T(8,128)(2,1)S(1)}, u32[]{:S(2)}, u32[]{:S(2)}) collective-permute-start(bf16[2,128,256]{2,1,0:T(8,128)(2,1)S(1)} %get-tuple-element.54), channel_id=1, source_target_pairs={{0,32},{32,64},{64,96},{96,128},{128,160},{160,192},{192,224},{224... | collective-permute-start | bytes 393224 | tf_op jit(solution)/shard_map/ppermute | solution.py:405
  27.3 4.3 %collective-permute-done.6.outer = bf16[2,128,256]{2,1,0:T(8,128)(2,1)S(1)} collective-permute-done((bf16[2,128,256]{2,1,0:T(8,128)(2,1)S(1)}, bf16[2,128,256]{2,1,0:T(8,128)(2,1)S(1)}, u32[]{:S(2)}, u32[]{:S(2)}) %collective-permute-start.6) | collective-permute-done | bytes 131104 | tf_op jit(solution)/shard_map/ppermute | solution.py:405
  32.6 2.1 %collective-permute-start.10 = (bf16[2,256,256]{2,1,0:T(8,128)(2,1)S(1)}, bf16[2,256,256]{2,1,0:T(8,128)(2,1)S(1)}, u32[]{:S(2)}, u32[]{:S(2)}) collective-permute-start(bf16[2,256,256]{2,1,0:T(8,128)(2,1)S(1)} %get-tuple-element.59.refs_2_.refs_5_), channel_id=1, source_target_pairs={{0,4},{1,5},{2,6},{3,7},{4,8},{5,9},{6,10},{7,11},{8,12},{9,13},{1... | collective-permute-start | bytes 786440 | tf_op jit(solution)/shard_map/ppermute | solution.py:408
  34.7 3.8 %collective-permute-start.12 = (bf16[2,256,256]{2,1,0:T(8,128)(2,1)S(1)}, bf16[2,256,256]{2,1,0:T(8,128)(2,1)S(1)}, u32[]{:S(2)}, u32[]{:S(2)}) collective-permute-start(bf16[2,256,256]{2,1,0:T(8,128)(2,1)S(1)} %get-tuple-element.59.refs_2_.refs_5_), channel_id=1, source_target_pairs={{0,28},{1,29},{2,30},{3,31},{4,0},{5,1},{6,2},{7,3},{8,4},{9,5},{1... | collective-permute-start | bytes 786440 | tf_op jit(solution)/shard_map/ppermute | solution.py:408
  38.5 2.9 %collective-permute-start.8 = (bf16[2,256,256]{2,1,0:T(8,128)(2,1)S(1)}, bf16[2,256,256]{2,1,0:T(8,128)(2,1)S(1)}, u32[]{:S(2)}, u32[]{:S(2)}) collective-permute-start(bf16[2,256,256]{2,1,0:T(8,128)(2,1)S(1)} %get-tuple-element.58.refs_0_), channel_id=1, source_target_pairs={{0,2},{1,3},{2,0},{3,1},{4,6},{5,7},{6,4},{7,5},{8,10},{9,11},{10,... | collective-permute-start | bytes 786440 | tf_op jit(solution)/shard_map/ppermute | solution.py:419
  41.5 1.3 %collective-permute-done.10.refs_3_.refs_6_ = bf16[2,256,256]{2,1,0:T(8,128)(2,1)S(1)} collective-permute-done((bf16[2,256,256]{2,1,0:T(8,128)(2,1)S(1)}, bf16[2,256,256]{2,1,0:T(8,128)(2,1)S(1)}, u32[]{:S(2)}, u32[]{:S(2)}) %collective-permute-start.10) | collective-permute-done | bytes 262176 | tf_op jit(solution)/shard_map/ppermute | solution.py:408
  42.8 2.7 %collective-permute-start.13 = (bf16[2,256,256]{2,1,0:T(8,128)(2,1)S(1)}, bf16[2,256,256]{2,1,0:T(8,128)(2,1)S(1)}, u32[]{:S(2)}, u32[]{:S(2)}) collective-permute-start(bf16[2,256,256]{2,1,0:T(8,128)(2,1)S(1)} %collective-permute-done.12.refs_4_.refs_7_), channel_id=1, source_target_pairs={{0,28},{1,29},{2,30},{3,31},{4,0},{5,1},{6,2},{7,3},{8,4},{9,5},{1... | collective-permute-start | bytes 786440 | tf_op jit(solution)/shard_map/ppermute | solution.py:408
  45.5 3.5 %collective-permute-start.7 = (bf16[2,256,256]{2,1,0:T(8,128)(2,1)S(1)}, bf16[2,256,256]{2,1,0:T(8,128)(2,1)S(1)}, u32[]{:S(2)}, u32[]{:S(2)}) collective-permute-start(bf16[2,256,256]{2,1,0:T(8,128)(2,1)S(1)} %get-tuple-element.58.refs_0_), channel_id=1, source_target_pairs={{0,1},{1,0},{2,3},{3,2},{4,5},{5,4},{6,7},{7,6},{8,9},{9,8},{10,11... | collective-permute-start | bytes 786440 | tf_op jit(solution)/shard_map/ppermute | solution.py:419
  51.2 2.7 %collective-permute-start.15 = (bf16[2,256,256]{2,1,0:T(8,128)(2,1)S(1)}, bf16[2,256,256]{2,1,0:T(8,128)(2,1)S(1)}, u32[]{:S(2)}, u32[]{:S(2)}) collective-permute-start(bf16[2,256,256]{2,1,0:T(8,128)(2,1)S(1)} %collective-permute-done.13.refs_3_), channel_id=1, source_target_pairs={{0,28},{1,29},{2,30},{3,31},{4,0},{5,1},{6,2},{7,3},{8,4},{9,5},{1... | collective-permute-start | bytes 786440 | tf_op jit(solution)/shard_map/ppermute | solution.py:408
  56.2 1.5 %shard_map.119.refs_1_ = f32[4,272,256]{2,1,0:T(8,128)S(1)} custom-call(bf16[4,256,256]{2,1,0:T(8,128)(2,1)S(1)} %get-tuple-element.63.refs_0_, f32[4,272,256]{2,1,0:T(8,128)S(1)} %get-tuple-element.68.refs_1_, bf16[2,256,256]{2,1,0:T(8,128)(2,1)S(1)} %collective-permute-done.11.refs_2_, ...), custom_call_target="tpu_custom_call", output_to_operand_aliasing={{}: (1, {})} | custom-call | flops 671088640 | bytes 4000000 | tf_op jit(solution)/shard_map/pallas_call | solution.py:28
  58.3 2.7 %collective-permute-start.17 = (bf16[256,256]{1,0:T(8,128)(2,1)S(1)}, bf16[256,256]{1,0:T(8,128)(2,1)S(1)}, u32[]{:S(2)}, u32[]{:S(2)}) collective-permute-start(bf16[256,256]{1,0:T(8,128)(2,1)S(1)} %get-tuple-element.75), channel_id=1, source_target_pairs={{0,28},{1,29},{2,30},{3,31},{4,0},{5,1},{6,2},{7,3},{8,4},{9,5},{1... | collective-permute-start | bytes 393224 | tf_op jit(solution)/shard_map/ppermute | solution.py:408
  61.0 1.5 %shard_map.121.refs_1_ = f32[4,272,256]{2,1,0:T(8,128)S(1)} custom-call(bf16[4,256,256]{2,1,0:T(8,128)(2,1)S(1)} %get-tuple-element.65.refs_0_.refs_1_, f32[4,272,256]{2,1,0:T(8,128)S(1)} %get-tuple-element.73.refs_1_, bf16[2,256,256]{2,1,0:T(8,128)(2,1)S(1)} %collective-permute-done.11.refs_2_, ...), custom_call_target="tpu_custom_call", output_to_operand_aliasing={{}: (1, {})} | custom-call | flops 671088640 | bytes 4000000 | tf_op jit(solution)/shard_map/pallas_call | solution.py:28
  62.4 1.5 %shard_map.122.refs_3_ = f32[4,272,256]{2,1,0:T(8,128)S(1)} custom-call(bf16[4,256,256]{2,1,0:T(8,128)(2,1)S(1)} %get-tuple-element.65.refs_0_.refs_1_, f32[4,272,256]{2,1,0:T(8,128)S(1)} %shard_map.121.refs_1_, bf16[2,256,256]{2,1,0:T(8,128)(2,1)S(1)} %collective-permute-done.14.refs_2_.plus, ...), custom_call_target="tpu_custom_call", output_to_operand_aliasing={{}: (1, {})} | custom-call | flops 671088640 | bytes 4000000 | tf_op jit(solution)/shard_map/pallas_call | solution.py:28
  63.9 1.5 %shard_map.120.refs_2_ = f32[4,272,256]{2,1,0:T(8,128)S(1)} custom-call(bf16[4,256,256]{2,1,0:T(8,128)(2,1)S(1)} %get-tuple-element.63.refs_0_, f32[4,272,256]{2,1,0:T(8,128)S(1)} %shard_map.119.refs_1_, bf16[2,256,256]{2,1,0:T(8,128)(2,1)S(1)} %collective-permute-done.14.refs_2_.plus, ...), custom_call_target="tpu_custom_call", output_to_operand_aliasing={{}: (1, {})} | custom-call | flops 671088640 | bytes 4000000 | tf_op jit(solution)/shard_map/pallas_call | solution.py:28
  66.5 3.6 %collective-permute-start.19 = (f32[2,272,256]{2,1,0:T(8,128)S(1)}, f32[2,272,256]{2,1,0:T(8,128)S(1)}, u32[]{:S(2)}, u32[]{:S(2)}) collective-permute-start(f32[2,272,256]{2,1,0:T(8,128)S(1)} %get-tuple-element.79), channel_id=1, source_target_pairs={{0,1},{1,0},{2,3},{3,2},{4,5},{5,4},{6,7},{7,6},{8,9},{9,8},{10,11... | collective-permute-start | bytes 1671176 | tf_op jit(solution)/shard_map/ppermute | solution.py:419
  71.8 3.0 %collective-permute-start.20 = (bf16[2,272,256]{2,1,0:T(8,128)(2,1)S(1)}, bf16[2,272,256]{2,1,0:T(8,128)(2,1)S(1)}, u32[]{:S(2)}, u32[]{:S(2)}) collective-permute-start(bf16[2,272,256]{2,1,0:T(8,128)(2,1)S(1)} %shard_map.127), channel_id=1, source_target_pairs={{0,2},{1,3},{2,0},{3,1},{4,6},{5,7},{6,4},{7,5},{8,10},{9,11},{10,... | collective-permute-start | bytes 835592 | tf_op jit(solution)/shard_map/ppermute | solution.py:419
  74.9 6.4 %collective-permute-done.20.received = bf16[2,272,256]{2,1,0:T(8,128)(2,1)S(1)} collective-permute-done((bf16[2,272,256]{2,1,0:T(8,128)(2,1)S(1)}, bf16[2,272,256]{2,1,0:T(8,128)(2,1)S(1)}, u32[]{:S(2)}, u32[]{:S(2)}) %collective-permute-start.20) | collective-permute-done | bytes 278560 | tf_op jit(solution)/shard_map/ppermute | solution.py:419
  (39 shorter events, 13.9 us)
Async XLA Ops:
  0.0 16.2 %collective-permute-start = (bf16[2,8,128,128]{3,2,1,0:T(8,128)(2,1)}, bf16[2,8,128,128]{3,2,1,0:T(8,128)(2,1)S(1)}, u32[]{:S(2)}, u32[]{:S(2)}) collective-permute-start(bf16[2,8,128,128]{3,2,1,0:T(8,128)(2,1)} %video.1), channel_id=1, source_target_pairs={{0,32},{32,64},{64,96},{96,128},{128,160},{160,192},{192,224},{224... | collective-permute-start | bytes 1572872 | tf_op jit(solution)/shard_map/ppermute | solution.py:405
  3.0 19.2 %collective-permute-start.2 = (bf16[2,2,128,128]{3,2,1,0:T(8,128)(2,1)S(1)}, bf16[2,2,128,128]{3,2,1,0:T(8,128)(2,1)S(1)}, u32[]{:S(2)}, u32[]{:S(2)}) collective-permute-start(bf16[2,2,128,128]{3,2,1,0:T(8,128)(2,1)S(1)} %get-tuple-element.49), channel_id=1, source_target_pairs={{0,31},{1,0},{2,1},{3,2},{4,3},{5,4},{6,5},{7,6},{8,7},{9,8},{10,9... | collective-permute-start | bytes 393224 | tf_op jit(solution)/shard_map/ppermute | solution.py:408
  4.3 18.0 %collective-permute-start.4 = (bf16[2,2,128,128]{3,2,1,0:T(8,128)(2,1)S(1)}, bf16[2,2,128,128]{3,2,1,0:T(8,128)(2,1)S(1)}, u32[]{:S(2)}, u32[]{:S(2)}) collective-permute-start(bf16[2,2,128,128]{3,2,1,0:T(8,128)(2,1)S(1)} %get-tuple-element.49), channel_id=1, source_target_pairs={{0,63},{1,32},{2,33},{3,34},{4,35},{5,36},{6,37},{7,38},{8,39},{9,... | collective-permute-start | bytes 393224 | tf_op jit(solution)/shard_map/ppermute | solution.py:416
  12.1 8.8 %collective-permute-start.1 = (bf16[2,1,128,128]{3,2,1,0:T(8,128)(2,1)S(1)}, bf16[2,1,128,128]{3,2,1,0:T(8,128)(2,1)S(1)}, u32[]{:S(2)}, u32[]{:S(2)}) collective-permute-start(bf16[2,1,128,128]{3,2,1,0:T(8,128)(2,1)S(1)} %get-tuple-element.48), channel_id=1, source_target_pairs={{0,1},{1,2},{2,3},{3,4},{4,5},{5,6},{6,7},{7,8},{8,9},{9,10},{10,1... | collective-permute-start | bytes 196616 | tf_op jit(solution)/shard_map/ppermute | solution.py:408
  12.1 10.2 %collective-permute-start.3 = (bf16[2,1,128,128]{3,2,1,0:T(8,128)(2,1)S(1)}, bf16[2,1,128,128]{3,2,1,0:T(8,128)(2,1)S(1)}, u32[]{:S(2)}, u32[]{:S(2)}) collective-permute-start(bf16[2,1,128,128]{3,2,1,0:T(8,128)(2,1)S(1)} %get-tuple-element.48), channel_id=1, source_target_pairs={{0,33},{1,34},{2,35},{3,36},{4,37},{5,38},{6,39},{7,40},{8,41},{9,... | collective-permute-start | bytes 196616 | tf_op jit(solution)/shard_map/ppermute | solution.py:416
  19.6 6.6 %collective-permute-start.5 = (bf16[2,128,256]{2,1,0:T(8,128)(2,1)S(1)}, bf16[2,128,256]{2,1,0:T(8,128)(2,1)S(1)}, u32[]{:S(2)}, u32[]{:S(2)}) collective-permute-start(bf16[2,128,256]{2,1,0:T(8,128)(2,1)S(1)} %get-tuple-element.53), channel_id=1, source_target_pairs={{0,32},{32,64},{64,96},{96,128},{128,160},{160,192},{192,224},{224... | collective-permute-start | bytes 393224 | tf_op jit(solution)/shard_map/ppermute | solution.py:405
  24.7 6.9 %collective-permute-start.6 = (bf16[2,128,256]{2,1,0:T(8,128)(2,1)S(1)}, bf16[2,128,256]{2,1,0:T(8,128)(2,1)S(1)}, u32[]{:S(2)}, u32[]{:S(2)}) collective-permute-start(bf16[2,128,256]{2,1,0:T(8,128)(2,1)S(1)} %get-tuple-element.54), channel_id=1, source_target_pairs={{0,32},{32,64},{64,96},{96,128},{128,160},{160,192},{192,224},{224... | collective-permute-start | bytes 393224 | tf_op jit(solution)/shard_map/ppermute | solution.py:405
  32.6 10.2 %collective-permute-start.10 = (bf16[2,256,256]{2,1,0:T(8,128)(2,1)S(1)}, bf16[2,256,256]{2,1,0:T(8,128)(2,1)S(1)}, u32[]{:S(2)}, u32[]{:S(2)}) collective-permute-start(bf16[2,256,256]{2,1,0:T(8,128)(2,1)S(1)} %get-tuple-element.59.refs_2_.refs_5_), channel_id=1, source_target_pairs={{0,4},{1,5},{2,6},{3,7},{4,8},{5,9},{6,10},{7,11},{8,12},{9,13},{1... | collective-permute-start | bytes 786440 | tf_op jit(solution)/shard_map/ppermute | solution.py:408
  34.7 8.1 %collective-permute-start.12 = (bf16[2,256,256]{2,1,0:T(8,128)(2,1)S(1)}, bf16[2,256,256]{2,1,0:T(8,128)(2,1)S(1)}, u32[]{:S(2)}, u32[]{:S(2)}) collective-permute-start(bf16[2,256,256]{2,1,0:T(8,128)(2,1)S(1)} %get-tuple-element.59.refs_2_.refs_5_), channel_id=1, source_target_pairs={{0,28},{1,29},{2,30},{3,31},{4,0},{5,1},{6,2},{7,3},{8,4},{9,5},{1... | collective-permute-start | bytes 786440 | tf_op jit(solution)/shard_map/ppermute | solution.py:408
  38.5 10.4 %collective-permute-start.8 = (bf16[2,256,256]{2,1,0:T(8,128)(2,1)S(1)}, bf16[2,256,256]{2,1,0:T(8,128)(2,1)S(1)}, u32[]{:S(2)}, u32[]{:S(2)}) collective-permute-start(bf16[2,256,256]{2,1,0:T(8,128)(2,1)S(1)} %get-tuple-element.58.refs_0_), channel_id=1, source_target_pairs={{0,2},{1,3},{2,0},{3,1},{4,6},{5,7},{6,4},{7,5},{8,10},{9,11},{10,... | collective-permute-start | bytes 786440 | tf_op jit(solution)/shard_map/ppermute | solution.py:419
  42.8 8.3 %collective-permute-start.11 = (bf16[2,256,256]{2,1,0:T(8,128)(2,1)S(1)}, bf16[2,256,256]{2,1,0:T(8,128)(2,1)S(1)}, u32[]{:S(2)}, u32[]{:S(2)}) collective-permute-start(bf16[2,256,256]{2,1,0:T(8,128)(2,1)S(1)} %collective-permute-done.10.refs_3_.refs_6_), channel_id=1, source_target_pairs={{0,4},{1,5},{2,6},{3,7},{4,8},{5,9},{6,10},{7,11},{8,12},{9,13},{1... | collective-permute-start | bytes 786440 | tf_op jit(solution)/shard_map/ppermute | solution.py:408
  42.8 8.3 %collective-permute-start.13 = (bf16[2,256,256]{2,1,0:T(8,128)(2,1)S(1)}, bf16[2,256,256]{2,1,0:T(8,128)(2,1)S(1)}, u32[]{:S(2)}, u32[]{:S(2)}) collective-permute-start(bf16[2,256,256]{2,1,0:T(8,128)(2,1)S(1)} %collective-permute-done.12.refs_4_.refs_7_), channel_id=1, source_target_pairs={{0,28},{1,29},{2,30},{3,31},{4,0},{5,1},{6,2},{7,3},{8,4},{9,5},{1... | collective-permute-start | bytes 786440 | tf_op jit(solution)/shard_map/ppermute | solution.py:408
  45.5 8.4 %collective-permute-start.7 = (bf16[2,256,256]{2,1,0:T(8,128)(2,1)S(1)}, bf16[2,256,256]{2,1,0:T(8,128)(2,1)S(1)}, u32[]{:S(2)}, u32[]{:S(2)}) collective-permute-start(bf16[2,256,256]{2,1,0:T(8,128)(2,1)S(1)} %get-tuple-element.58.refs_0_), channel_id=1, source_target_pairs={{0,1},{1,0},{2,3},{3,2},{4,5},{5,4},{6,7},{7,6},{8,9},{9,8},{10,11... | collective-permute-start | bytes 786440 | tf_op jit(solution)/shard_map/ppermute | solution.py:419
  48.9 5.0 %collective-permute-start.9 = (bf16[2,256,256]{2,1,0:T(8,128)(2,1)S(1)}, bf16[2,256,256]{2,1,0:T(8,128)(2,1)S(1)}, u32[]{:S(2)}, u32[]{:S(2)}) collective-permute-start(bf16[2,256,256]{2,1,0:T(8,128)(2,1)S(1)} %collective-permute-done.8.refs_1_.refs_2_), channel_id=1, source_target_pairs={{0,1},{1,0},{2,3},{3,2},{4,5},{5,4},{6,7},{7,6},{8,9},{9,8},{10,11... | collective-permute-start | bytes 786440 | tf_op jit(solution)/shard_map/ppermute | solution.py:419
  51.2 7.0 %collective-permute-start.14 = (bf16[2,256,256]{2,1,0:T(8,128)(2,1)S(1)}, bf16[2,256,256]{2,1,0:T(8,128)(2,1)S(1)}, u32[]{:S(2)}, u32[]{:S(2)}) collective-permute-start(bf16[2,256,256]{2,1,0:T(8,128)(2,1)S(1)} %collective-permute-done.11.refs_2_), channel_id=1, source_target_pairs={{0,4},{1,5},{2,6},{3,7},{4,8},{5,9},{6,10},{7,11},{8,12},{9,13},{1... | collective-permute-start | bytes 786440 | tf_op jit(solution)/shard_map/ppermute | solution.py:408
  51.2 6.9 %collective-permute-start.15 = (bf16[2,256,256]{2,1,0:T(8,128)(2,1)S(1)}, bf16[2,256,256]{2,1,0:T(8,128)(2,1)S(1)}, u32[]{:S(2)}, u32[]{:S(2)}) collective-permute-start(bf16[2,256,256]{2,1,0:T(8,128)(2,1)S(1)} %collective-permute-done.13.refs_3_), channel_id=1, source_target_pairs={{0,28},{1,29},{2,30},{3,31},{4,0},{5,1},{6,2},{7,3},{8,4},{9,5},{1... | collective-permute-start | bytes 786440 | tf_op jit(solution)/shard_map/ppermute | solution.py:408
  58.2 7.1 %collective-permute-start.16 = (bf16[256,256]{1,0:T(8,128)(2,1)S(1)}, bf16[256,256]{1,0:T(8,128)(2,1)S(1)}, u32[]{:S(2)}, u32[]{:S(2)}) collective-permute-start(bf16[256,256]{1,0:T(8,128)(2,1)S(1)} %get-tuple-element.74), channel_id=1, source_target_pairs={{0,4},{1,5},{2,6},{3,7},{4,8},{5,9},{6,10},{7,11},{8,12},{9,13},{1... | collective-permute-start | bytes 393224 | tf_op jit(solution)/shard_map/ppermute | solution.py:408
  58.3 7.0 %collective-permute-start.17 = (bf16[256,256]{1,0:T(8,128)(2,1)S(1)}, bf16[256,256]{1,0:T(8,128)(2,1)S(1)}, u32[]{:S(2)}, u32[]{:S(2)}) collective-permute-start(bf16[256,256]{1,0:T(8,128)(2,1)S(1)} %get-tuple-element.75), channel_id=1, source_target_pairs={{0,28},{1,29},{2,30},{3,31},{4,0},{5,1},{6,2},{7,3},{8,4},{9,5},{1... | collective-permute-start | bytes 393224 | tf_op jit(solution)/shard_map/ppermute | solution.py:408
  66.5 5.2 %collective-permute-start.19 = (f32[2,272,256]{2,1,0:T(8,128)S(1)}, f32[2,272,256]{2,1,0:T(8,128)S(1)}, u32[]{:S(2)}, u32[]{:S(2)}) collective-permute-start(f32[2,272,256]{2,1,0:T(8,128)S(1)} %get-tuple-element.79), channel_id=1, source_target_pairs={{0,1},{1,0},{2,3},{3,2},{4,5},{5,4},{6,7},{7,6},{8,9},{9,8},{10,11... | collective-permute-start | bytes 1671176 | tf_op jit(solution)/shard_map/ppermute | solution.py:419
  71.2 3.6 %collective-permute-start.18 = (f32[2,272,256]{2,1,0:T(8,128)S(1)}, f32[2,272,256]{2,1,0:T(8,128)S(1)}, u32[]{:S(2)}, u32[]{:S(2)}) collective-permute-start(f32[2,272,256]{2,1,0:T(8,128)S(1)} %get-tuple-element.77), channel_id=1, source_target_pairs={{0,1},{1,0},{2,3},{3,2},{4,5},{5,4},{6,7},{7,6},{8,9},{9,8},{10,11... | collective-permute-start | bytes 1671176 | tf_op jit(solution)/shard_map/ppermute | solution.py:419
  71.8 9.5 %collective-permute-start.20 = (bf16[2,272,256]{2,1,0:T(8,128)(2,1)S(1)}, bf16[2,272,256]{2,1,0:T(8,128)(2,1)S(1)}, u32[]{:S(2)}, u32[]{:S(2)}) collective-permute-start(bf16[2,272,256]{2,1,0:T(8,128)(2,1)S(1)} %shard_map.127), channel_id=1, source_target_pairs={{0,2},{1,3},{2,0},{3,1},{4,6},{5,7},{6,4},{7,5},{8,10},{9,11},{10,... | collective-permute-start | bytes 835592 | tf_op jit(solution)/shard_map/ppermute | solution.py:419
